TPU v7x, 256 devices: a whole 4x4x8 slice. The times are simulated.
256 devices in a mesh: grp: 8 (over z_hi, core), shard: 32 (over y, x, z_lo).
Axes of the slice: x: 4, y: 4, z: 8 (z_hi: 4, z_lo: 2; z = z_hi * 2 + z_lo), core: 2. Of those that a mesh axis runs over, the one named last changes fastest.
Arguments:
- embeddings: bfloat16 [262144, 768], P(('grp', 'shard')), may hold values from -0.26 to 0.26
- centers: bfloat16 [2048, 768], P('shard'), may hold values from -0.26 to 0.26
- assignment: int32 [262144, 1], P(('grp', 'shard')), may hold values from 0 to 2047, as said below
Outputs:
- old_min: float32 [262144], P(('grp', 'shard'))
- refined_centers: float32 [2048, 768], P('shard')
- new_min: float32 [262144], P(('grp', 'shard'))
Inputs may be any that keep to these rules, and one draw needn't show every extreme that they name: `assignment`: every cluster is named by at least one row; cluster k belongs to the index of shard that holds centers[k]; the rows of one device name clusters belonging to any one index of shard at least 16 and at most 64 times, and in every group one index of shard is named 64 times by the rows of each device of that group.
All inputs are finite; a program needn't handle non-finite values.
Results may differ from a plain program's by a relative error of at most 0.0003.
Values may be sent and summed in bfloat16 or wider, within the bound.
No kernel may reach another device: no remote copies, remote signals or barrier semaphores. Data moves between devices by JAX's collectives and lax.ppermute only.
A program may use at most 64 MiB of HBM per device.

v0:
```python
import jax
import jax.numpy as jnp
from jax import lax
from jax.sharding import PartitionSpec as P


def on_device(embeddings, centers, assignment):
    wide_rows = embeddings.astype(jnp.float32)
    row_norms = jnp.sum(jnp.square(wide_rows), 1)
    starting = jnp.full((embeddings.shape[0],), jnp.inf, jnp.float32)
    portion = lax.all_gather(centers, "shard", axis=0, tiled=True)
    portion_norms = jnp.sum(jnp.square(portion.astype(jnp.float32)), 1)
    products = lax.dot_general(
        embeddings, portion, (((1,), (1,)), ((), ())), preferred_element_type=jnp.float32
    )
    distance = row_norms[:, None] - 2.0 * products + portion_norms[None, :]
    old_min = jnp.minimum(starting, jnp.min(distance, 1))
    n_shard = lax.axis_size("shard")
    owned = centers.shape[0]
    clusters = owned * n_shard
    labels = assignment[:, 0]
    onehot = (labels[:, None] == jnp.arange(clusters, dtype=jnp.int32)[None, :]).astype(
        jnp.bfloat16
    )
    partial_totals = lax.dot_general(
        onehot, embeddings, (((0,), (0,)), ((), ())), preferred_element_type=jnp.float32
    )
    partial_counts = jnp.sum(onehot, 0, dtype=jnp.float32)
    owner_totals, owner_counts = (
        lax.psum_scatter(partial_totals, "shard", scatter_dimension=0, tiled=True),
        lax.psum_scatter(partial_counts, "shard", scatter_dimension=0, tiled=True),
    )
    totals, counts = lax.psum((owner_totals, owner_counts), "grp")
    refined_centers = totals / counts[:, None]
    portion = lax.all_gather(refined_centers, "shard", axis=0, tiled=True)
    portion_norms = jnp.sum(jnp.square(portion), 1)
    products = lax.dot_general(
        wide_rows,
        portion,
        (((1,), (1,)), ((), ())),
        precision=lax.Precision.HIGHEST,
        preferred_element_type=jnp.float32,
    )
    distance = row_norms[:, None] - 2.0 * products + portion_norms[None, :]
    new_min = jnp.minimum(starting, jnp.min(distance, 1))
    return (old_min, refined_centers, new_min)


def solution(mesh):
    placed = (P(("grp", "shard"), None), P("shard", None), P(("grp", "shard"), None))
    return jax.shard_map(
        on_device,
        mesh=mesh,
        in_specs=placed,
        out_specs=(P(("grp", "shard")), P("shard", None), P(("grp", "shard"))),
        check_vma=False,
    )
```

profile of v0, /device:TPU:64, one launch (start us, length us, event | category | flops | bytes accessed | tf_op | source)
XLA Modules:
  0.0 637.7 jit_solution(16724863705314261311)
XLA Ops:
  7.2 0.0 reduce-scatter.2.cloned.1.call-start
  7.2 7.8 %fusion.1 = f32[2048,768]{1,0:T(8,128)} fusion(bf16[1024,768]{1,0:T(8,128)(2,1)} %param.3, s32[1024]{0:T(1024)} %bitcast.7), kind=kOutput, calls=%fused_computation.4 | convolution fusion | flops 3223322624 | bytes 7868416 | tf_op jit(solution)/shard_map/dot_general | solution.py:25
  15.0 0.0 copy-start.3
  15.0 0.0 copy-start.2
  15.0 0.0 copy-start.1
  15.1 0.0 reduce-scatter.2.cloned.1.call-update
  15.1 0.0 all-reduce.3.cloned.1.call-start
  15.1 186.0 %reduce-scatter.2.cloned.1.call-done = f32[64,768]{1,0:T(8,128)} async-done(((f32[2048,768]{1,0:T(8,128)}), f32[64,768]{1,0:T(8,128)}) %reduce-scatter.2.cloned.1.call-update) | async-done | bytes 196624 | tf_op jit(solution)/shard_map/reduce_scatter | solution.py:30
  201.1 0.0 all-reduce.3.cloned.1.call-update
  201.2 0.0 all-gather.3.cloned.1.call-start
  201.2 0.7 all-gather.3.cloned.1.call-update
  201.9 0.0 all-gather.5.cloned.1.call-start
  202.0 0.0 copy-done.3
  202.0 0.6 dynamic-slice
  203.2 0.0 copy-done.2
  203.2 1.0 convert_reduce_fusion
  204.3 81.5 %all-reduce = f32[2048]{0:T(1024)S(1)} all-reduce(f32[2048]{0:T(1024)S(1)} %convert_reduce_fusion), channel_id=3, replica_groups=mesh['grp'=8,'shard'=32] {'shard'}, use_global_device_ids=true, to_apply=%region_6.0.clone | all-reduce | flops 2048 | bytes 16384
  285.7 0.1 dynamic-slice.1
  285.8 12.6 %psum.15 = f32[64]{0:T(128)S(1)} all-reduce(f32[64]{0:T(128)S(1)} %dynamic-slice.1), channel_id=1, replica_groups=mesh['grp'=8,'shard'=32] {'grp'}, use_global_device_ids=true, to_apply=%region_7.0 | all-reduce | flops 64 | bytes 512 | tf_op jit(solution)/shard_map/psum | solution.py:33
  298.4 0.0 all-reduce.3.cloned.1.call-done
  298.4 1.7 broadcast_divide_fusion
  300.1 0.0 all-gather.5.cloned.1.call-update
  300.1 0.0 copy-done.1
  300.1 0.4 multiply_reduce_fusion.2
  300.5 134.7 %all-gather.3.cloned.1.call-done = bf16[2048,768]{1,0:T(8,128)(2,1)} async-done(((bf16[64,768]{1,0:T(8,128)(2,1)}), bf16[2048,768]{1,0:T(8,128)(2,1)}) %all-gather.3.cloned.1.call-update) | async-done | bytes 3145744 | tf_op jit(solution)/shard_map/all_gather | solution.py:11
  435.2 2.6 multiply_reduce_fusion.1
  437.7 6.4 add_reduce_fusion.1
  444.1 171.4 %all-gather.5.cloned.1.call-done = f32[2048,768]{1,0:T(8,128)} async-done(((f32[64,768]{1,0:T(8,128)}), f32[2048,768]{1,0:T(8,128)}) %all-gather.5.cloned.1.call-update) | async-done | bytes 6291472 | tf_op jit(solution)/shard_map/all_gather | solution.py:35
  615.5 0.0 copy-start
  615.5 3.4 multiply_reduce_fusion
  618.9 1.2 copy-done
  620.1 11.1 %add_reduce_fusion = f32[1024]{0:T(1024)} fusion(f32[2048,768]{1,0:T(8,128)S(1)} %copy-done, bf16[1024,768]{1,0:T(8,128)(2,1)S(1)} %copy-done.1, f32[2048]{0:T(1024)S(1)} %multiply_reduce_fusion, f32[1024]{0:T(1024)S(1)} %multiply_reduce_fusion.2), kind=kOutput, calls=%fused_computation | convolution fusion | flops 19335741440 | bytes 7880704 | tf_op jit(solution)/shard_map/dot_general | solution.py:37
Async XLA Ops:
  7.2 194.0 %reduce-scatter.2.cloned.1.call-start = ((), (), s32[]{:S(2)}) async-start(), calls=%async_computation.2 | async-start | bytes 6488064 | tf_op jit(solution)/shard_map/reduce_scatter | solution.py:30
  15.0 186.9 %copy-start.3 = (u32[256]{0:T(256)S(1)}, u32[256]{0:T(256)}, u32[]{:S(2)}) copy-start(u32[256]{0:T(256)} %constant.9) | copy-start | bytes 3076
  15.0 188.2 %copy-start.2 = (s32[1024,1]{0,1:T(1,128)S(1)}, s32[1024,1]{0,1:T(1,128)}, u32[]{:S(2)}) copy-start(s32[1024,1]{0,1:T(1,128)} %param.5) | copy-start | bytes 12292
  15.0 285.1 %copy-start.1 = (bf16[1024,768]{1,0:T(8,128)(2,1)S(1)}, bf16[1024,768]{1,0:T(8,128)(2,1)}, u32[]{:S(2)}) copy-start(bf16[1024,768]{1,0:T(8,128)(2,1)} %param.3) | copy-start | bytes 4718596
  15.1 283.3 %all-reduce.3.cloned.1.call-start = ((), (), s32[]{:S(2)}) async-start(), calls=%async_computation.3 | async-start | bytes 393216 | tf_op jit(solution)/shard_map/psum | solution.py:33
  201.2 234.0 %all-gather.3.cloned.1.call-start = ((), (), s32[]{:S(2)}) async-start(), calls=%async_computation.1 | async-start | bytes 3244032 | tf_op jit(solution)/shard_map/all_gather | solution.py:11
  201.9 413.6 %all-gather.5.cloned.1.call-start = ((), (), s32[]{:S(2)}) async-start(), calls=%async_computation.4 | async-start | bytes 6488064 | tf_op jit(solution)/shard_map/all_gather | solution.py:35
  615.5 4.6 copy-start
Sparse Core Ops, SparseCore 0:
  15.2 185.9 reduce-scatter.1
  203.8 65.5 all-reduce.2
  271.3 163.8 all-gather.2
  437.5 177.9 all-gather.4
where the time goes:
time: 638 us
  waiting for transfers between devices  493 us (77%)
  blocking collectives  94 us (15%)
  matrix products  25.3 us (4%)
  between operations  14.5 us (2%)
  other arithmetic  9.09 us (1%)
    reduce_scatter x1, waiting for transfers between devices, on_device(): lax.psum_scatter(partial_totals, 'shard', scatter_dimension=0, tiled=True)  186 us
    all_gather x1, waiting for transfers between devices, on_device(): portion = lax.all_gather(refined_centers, 'shard', axis=0, tiled=True)  171 us
    all_gather x1, waiting for transfers between devices, on_device(): portion = lax.all_gather(centers, 'shard', axis=0, tiled=True)  135 us
    unnamed x1, blocking collectives  81.5 us
  transfers between devices with their start and end apart: 4, of which 3 were waited for; matrix products, arithmetic and copies ran while one was open for 2% of the time, Pallas kernels for 0%

commit v1 on v0

v1 whole, which is shorter than its diff:
```python
import jax
import jax.numpy as jnp
from jax import lax
from jax.experimental import pallas as pl
from jax.experimental.pallas import tpu as pltpu
from jax.sharding import Mesh, PartitionSpec as P

AXES = ("zh", "core", "y", "x", "zl")
SIZES = (4, 2, 4, 4, 2)
SHARD = ("y", "x", "zl")

D = 768
HALF = 32
CHUNKS = 32
COLS = D // 128
BODY = COLS * HALF
CODED = BODY + 16
LIMIT = 32700.0
VMEM = 48 * 1024 * 1024


def diagonal(rows):
    r = lax.broadcasted_iota(jnp.int32, (rows, 128), 0) % HALF
    c = lax.broadcasted_iota(jnp.int32, (rows, 128), 1)
    return r == c


def to_lanes(column):
    return jnp.sum(jnp.where(diagonal(HALF), column, 0.0), 0, keepdims=True)


def to_column(row):
    return jnp.sum(jnp.where(diagonal(HALF), row, 0.0), 1, keepdims=True)


def code_of(values):
    most = jnp.max(jnp.abs(values), 1, keepdims=True)
    return jnp.ceil(jnp.log2(jnp.maximum(most, 1e-30)) * 256.0)


def quantize(values, code):
    scaled = values * (LIMIT * jnp.exp2(code * (-1.0 / 256.0)))
    return jnp.floor(scaled + 0.5).astype(jnp.int32).astype(jnp.int16)


def scale_of(code):
    return jnp.exp2(code * (1.0 / 256.0)) * (1.0 / LIMIT)


def footer(counts, codes):
    r = lax.broadcasted_iota(jnp.int32, (16, 128), 0)
    both = jnp.where(r == 0, counts, jnp.where(r == 1, codes, 0.0))
    return both.astype(jnp.int32).astype(jnp.int16)


def partial_kernel(base_ref, lab_a, lab_b, rows_a, rows_b, out_ref):
    tile = 128

    def step(t, carry):
        j = t * tile + lax.broadcasted_iota(jnp.int32, (tile, 1), 0)
        k = j + (j // HALF) * HALF + base_ref[0]
        hot_a = jnp.where(k == lab_a[...], 1.0, 0.0)
        hot_b = jnp.where(k == lab_b[...], 1.0, 0.0)
        sums = jnp.dot(
            hot_a.astype(jnp.bfloat16), rows_a[...], preferred_element_type=jnp.float32
        ) + jnp.dot(
            hot_b.astype(jnp.bfloat16), rows_b[...], preferred_element_type=jnp.float32
        )
        counts = jnp.sum(hot_a + hot_b, 1, keepdims=True)
        code = code_of(sums)
        coded = quantize(sums, code)
        for c in range(tile // HALF):
            at = t * (tile // HALF) + c
            part = slice(c * HALF, (c + 1) * HALF)
            for b in range(COLS):
                out_ref[at, b * HALF : (b + 1) * HALF, :] = coded[
                    part, b * 128 : (b + 1) * 128
                ]
            out_ref[at, BODY:CODED, :] = footer(
                to_lanes(counts[part]), to_lanes(code[part])
            )
        return carry

    lax.fori_loop(0, CHUNKS * HALF // tile, step, 0)


def gather_sums_kernel(in_ref, out_ref):
    def step(s, carry):
        blocks, counts = carry
        foot = in_ref[s, BODY:CODED, :].astype(jnp.float32)
        scale = scale_of(to_column(foot[1:2, :]))
        blocks = tuple(
            blocks[b]
            + in_ref[s, b * HALF : (b + 1) * HALF, :].astype(jnp.float32) * scale
            for b in range(COLS)
        )
        return blocks, counts + foot[0:1, :]

    zeros = tuple(jnp.zeros((HALF, 128), jnp.float32) for _ in range(COLS))
    blocks, counts = lax.fori_loop(
        0, CHUNKS, step, (zeros, jnp.zeros((1, 128), jnp.float32))
    )
    for b in range(COLS):
        out_ref[b * HALF : (b + 1) * HALF, :] = blocks[b]
    out_ref[BODY : BODY + 8, :] = jnp.broadcast_to(counts, (8, 128))


def refine_kernel(own, one, two, three, refined_ref, coded_ref):
    total = own[...] + one[...] + two[...] + three[...]
    counts = to_column(total[BODY : BODY + 1, :])
    refined = [total[b * HALF : (b + 1) * HALF, :] / counts for b in range(COLS)]
    for b in range(COLS):
        refined_ref[:, b * 128 : (b + 1) * 128] = refined[b]
    most = refined[0]
    for b in range(COLS):
        most = jnp.maximum(jnp.abs(most), jnp.abs(refined[b]))
    code = code_of(most)
    coded = [quantize(refined[b], code) for b in range(COLS)]
    foot = footer(to_lanes(jnp.zeros_like(code)), to_lanes(code))

    def step(s, carry):
        for b in range(COLS):
            coded_ref[s, b * HALF : (b + 1) * HALF, :] = coded[b]
        coded_ref[s, BODY:CODED, :] = foot
        return carry

    lax.fori_loop(0, CHUNKS, step, 0)


def rows_dot(centers, rows):
    return lax.dot_general(
        centers, rows, (((1,), (1,)), ((), ())), preferred_element_type=jnp.float32
    )


def nearest(value, least):
    n = value.shape[0]
    return jnp.minimum(least, jnp.min(value.reshape(n // 8, 8, value.shape[1]), 0))


def old_kernel(norms_ref, rows_ref, own_ref, other_ref, out_ref):
    tile = 256
    rows = rows_ref[...] * jnp.bfloat16(-2.0)
    least = jnp.full((8, rows.shape[0]), jnp.inf, jnp.float32)
    for ref in (own_ref, other_ref):

        def step(t, least, ref=ref):
            part = ref[pl.ds(pl.multiple_of(t * tile, tile), tile), :]
            wide = part.astype(jnp.float32)
            norm = jnp.sum(wide * wide, 1, keepdims=True)
            return nearest(rows_dot(part, rows) + norm, least)

        least = lax.fori_loop(0, ref.shape[0] // tile, step, least)
    out_ref[...] = norms_ref[...] + jnp.min(least, 0, keepdims=True)


def new_kernel(rows_ref, coded_ref, least_ref, out_ref):
    per = 8
    rows = rows_ref[...] * jnp.bfloat16(-2.0)

    def step(t, least):
        high, low, scale, norm = [], [], [], []
        for c in range(per):
            at = t * per + c
            wide = jnp.concatenate(
                [
                    coded_ref[at, b * HALF : (b + 1) * HALF, :].astype(jnp.float32)
                    for b in range(COLS)
                ],
                1,
            )
            top = wide.astype(jnp.bfloat16)
            high.append(top)
            low.append((wide - top.astype(jnp.float32)).astype(jnp.bfloat16))
            foot = coded_ref[at, BODY:CODED, :].astype(jnp.float32)
            s = scale_of(to_column(foot[1:2, :]))
            scale.append(s)
            norm.append(jnp.sum(wide * wide, 1, keepdims=True) * (s * s))
        product = rows_dot(jnp.concatenate(high, 0), rows) + rows_dot(
            jnp.concatenate(low, 0), rows
        )
        value = product * jnp.concatenate(scale, 0) + jnp.concatenate(norm, 0)
        return nearest(value, least)

    out_ref[...] = lax.fori_loop(0, CHUNKS // per, step, least_ref[...])


def call(kernel, out_shape, *args, flops=0, moved=0, smem=0):
    specs = [
        pl.BlockSpec(memory_space=pltpu.SMEM if i < smem else pltpu.VMEM)
        for i in range(len(args))
    ]
    many = isinstance(out_shape, tuple)
    out_specs = pl.BlockSpec(memory_space=pltpu.VMEM)
    return pl.pallas_call(
        kernel,
        out_shape=out_shape,
        in_specs=specs,
        out_specs=tuple([out_specs] * len(out_shape)) if many else out_specs,
        compiler_params=pltpu.CompilerParams(vmem_limit_bytes=VMEM),
        cost_estimate=pl.CostEstimate(
            flops=flops, bytes_accessed=moved, transcendentals=0
        ),
    )(*args)


def ring(axis, size, k):
    return [(i, (i + k) % size) for i in range(size)]


def swap(value, axis):
    return lax.ppermute(value, axis, [(0, 1), (1, 0)])


def gather_centers(part):
    part = jnp.concatenate([part, swap(part, "zl")])
    for axis in ("x", "y"):
        part = jnp.concatenate(
            [part] + [lax.ppermute(part, axis, ring(axis, 4, k)) for k in (1, 2, 3)]
        )
    return part


def on_device(embeddings, centers, assignment):
    n = embeddings.shape[0]
    core = lax.axis_index("core")
    f32, i16 = jnp.float32, jnp.int16
    labels = assignment.reshape(1, n)
    other_labels = swap(labels, "core")
    other_rows = swap(embeddings, "core")

    mine = lax.dynamic_slice(centers, (core * HALF, 0), (HALF, D))
    old_own = gather_centers(mine)
    old_other = swap(old_own, "core")

    wide = embeddings.astype(f32)
    norms = jnp.sum(wide * wide, 1).reshape(1, n)

    base = (core * HALF).astype(jnp.int32).reshape(1)
    sums = call(
        partial_kernel,
        jax.ShapeDtypeStruct((CHUNKS, CODED, 128), i16),
        base, labels, other_labels, embeddings, other_rows,
        flops=2 * 1024 * 2 * n * D, moved=6 << 20, smem=1,
    )
    sums = lax.all_to_all(sums, SHARD, 0, 0)
    group = call(
        gather_sums_kernel,
        jax.ShapeDtypeStruct((BODY + 8, 128), f32),
        sums,
        flops=1 << 22, moved=2 << 20,
    )
    others = [lax.ppermute(group, "zh", ring("zh", 4, k)) for k in (1, 2, 3)]
    refined, coded = call(
        refine_kernel,
        (
            jax.ShapeDtypeStruct((HALF, D), f32),
            jax.ShapeDtypeStruct((CHUNKS, CODED, 128), i16),
        ),
        group, *others,
        flops=1 << 20, moved=2 << 20,
    )
    refined_other = swap(refined, "core")
    first = core == 0
    refined_centers = jnp.concatenate(
        [
            jnp.where(first, refined, refined_other),
            jnp.where(first, refined_other, refined),
        ]
    )
    new_own = lax.all_to_all(coded, SHARD, 0, 0)
    new_other = swap(new_own, "core")

    old_min = call(
        old_kernel,
        jax.ShapeDtypeStruct((1, n), f32),
        norms, embeddings, old_own, old_other,
        flops=2 * 2048 * n * D, moved=5 << 20,
    )

    least = jnp.full((8, n), jnp.inf, f32)
    for coded in (new_own, new_other):
        least = call(
            new_kernel,
            jax.ShapeDtypeStruct((8, n), f32),
            embeddings, coded, least,
            flops=2 * 2048 * n * D, moved=3 << 20,
        )
    new_min = norms[0] + jnp.min(least, 0)
    return old_min.reshape(n), refined_centers, new_min


def solution(mesh):
    fine = Mesh(mesh.devices.reshape(SIZES), AXES)
    rows = ("zh", "core") + SHARD
    return jax.shard_map(
        on_device,
        mesh=fine,
        in_specs=(P(rows, None), P(SHARD, None), P(rows, None)),
        out_specs=(P(rows), P(SHARD, None), P(rows)),
        check_vma=False,
    )
```

time: 638 us -> 151 us (0.24)
  the two profiles are of different devices: /device:TPU:64 before, /device:TPU:1 now
where the time goes in v1:
time: 151 us; the launch traced here: 150 us
  waiting for transfers between devices  47.4 us (31%)
  starting transfers between devices  32.3 us (21%)
  blocking collectives  30.4 us (20%)
  Pallas kernels  29.4 us (19%)
  local copies, waits for them, and re-layouts  7.67 us (5%)
  other arithmetic  1.7 us (1%)
    all_to_all x1, blocking collectives, on_device(): sums = lax.all_to_all(sums, SHARD, 0, 0)  30.4 us
    pallas_call x6, Pallas kernels, call(): pl.pallas_call(kernel, out_shape=out_shape, in_specs=specs, out_specs=tup...  29.4 us
    ppermute x6, waiting for transfers between devices, swap(): return lax.ppermute(value, axis, [(0, 1), (1, 0)])  26.5 us
    ppermute x6, waiting for transfers between devices, gather_centers(): lax.ppermute(part, axis, ring(axis, 4, k))  13.6 us
    ppermute x3, starting transfers between devices, on_device(): others = [lax.ppermute(group, 'zh', ring('zh', 4, k)) for k in (1, 2, 3)]  9.68 us
    ppermute x6, starting transfers between devices, gather_centers(): lax.ppermute(part, axis, ring(axis, 4, k))  9.37 us
    ppermute x6, starting transfers between devices, swap(): return lax.ppermute(value, axis, [(0, 1), (1, 0)])  9.1 us
    ppermute x3, waiting for transfers between devices, on_device(): others = [lax.ppermute(group, 'zh', ring('zh', 4, k)) for k in (1, 2, 3)]  7.22 us
  transfers between devices with their start and end apart: 16, of which 9 were waited for; matrix products, arithmetic and copies ran while one was open for 4% of the time, Pallas kernels for 8%

profile of v1, /device:TPU:1, one launch (start us, length us, event | category | flops | bytes accessed | tf_op | source)
XLA Modules:
  0.0 149.6 jit_solution(10988996205365741886)
XLA Ops:
  0.6 3.3 %collective-permute-start.9 = (bf16[1024,768]{1,0:T(8,128)(2,1)}, bf16[1024,768]{1,0:T(8,128)(2,1)S(1)}, u32[]{:S(2)}, u32[]{:S(2)}) collective-permute-start(bf16[1024,768]{1,0:T(8,128)(2,1)} %rows_ref.5), channel_id=1, source_target_pairs={{0,32},{32,0},{1,33},{33,1},{2,34},{34,2},{3,35},{35,3},{4,36},{36... | collective-permute-start | bytes 4718600 | tf_op jit(solution)/shard_map/ppermute | solution.py:212
  4.1 3.2 %collective-permute-done.8.lab_b = s32[1,1024]{1,0:T(1,128)S(1)} collective-permute-done((s32[1,1024]{1,0:T(1,128)}, s32[1,1024]{1,0:T(1,128)S(1)}, u32[]{:S(2)}, u32[]{:S(2)}) %collective-permute-start.8) | collective-permute-done | bytes 4128 | tf_op jit(solution)/shard_map/ppermute | solution.py:212
  7.2 1.4 copy-done
  9.3 6.3 %shard_map.59 = s16[32,208,128]{2,1,0:T(8,128)(2,1)S(1)} custom-call(s32[1]{0:T(128)} %bitcast.2.base_ref, s32[1,1024]{1,0:T(1,128)S(1)} %bitcast.6, s32[1,1024]{1,0:T(1,128)S(1)} %collective-permute-done.8.lab_b, bf16[1024,768]{1,0:T(8,128)(2,1)S(1)} %copy-done, bf16[1024,768]{1,0:T(8,128)(2,1)S(1)} %collective-permute-done.9.rows_b), custom_call_target="tpu_custom_call" | custom-call | flops 3221225472 | bytes 6291456 | tf_op jit(solution)/shard_map/pallas_call | solution.py:195
  15.6 30.4 %all_to_all.10.in_ref = s16[32,208,128]{2,1,0:T(8,128)(2,1)S(1)} all-to-all(s16[32,208,128]{2,1,0:T(8,128)(2,1)S(1)} %shard_map.59), channel_id=1, replica_groups=mesh['zh'=4,'core'=2,'y'=4,'x'=4,'zl'=2] {'y','x','zl'}, dimensions={0} | all-to-all | bytes 3407872 | tf_op jit(solution)/shard_map/all_to_all | solution.py:246
  46.1 3.2 %shard_map.60.own = f32[200,128]{1,0:T(8,128)S(1)} custom-call(s16[32,208,128]{2,1,0:T(8,128)(2,1)S(1)} %all_to_all.10.in_ref), custom_call_target="tpu_custom_call" | custom-call | flops 4194304 | bytes 2097152 | tf_op jit(solution)/shard_map/pallas_call | solution.py:195
  49.3 3.1 %collective-permute-start.10 = (f32[200,128]{1,0:T(8,128)S(1)}, f32[200,128]{1,0:T(8,128)S(1)}, u32[]{:S(2)}, u32[]{:S(2)}) collective-permute-start(f32[200,128]{1,0:T(8,128)S(1)} %shard_map.60.own), channel_id=1, source_target_pairs={{0,64},{64,128},{128,192},{192,0},{1,65},{65,129},{129,193},{193,1... | collective-permute-start | bytes 307208 | tf_op jit(solution)/shard_map/ppermute | solution.py:253
  52.4 4.2 %collective-permute-start.11 = (f32[200,128]{1,0:T(8,128)S(1)}, f32[200,128]{1,0:T(8,128)S(1)}, u32[]{:S(2)}, u32[]{:S(2)}) collective-permute-start(f32[200,128]{1,0:T(8,128)S(1)} %shard_map.60.own), channel_id=1, source_target_pairs={{0,128},{64,192},{128,0},{192,64},{1,129},{65,193},{129,1},{193,65... | collective-permute-start | bytes 307208 | tf_op jit(solution)/shard_map/ppermute | solution.py:253
  56.6 2.4 %collective-permute-start.12 = (f32[200,128]{1,0:T(8,128)S(1)}, f32[200,128]{1,0:T(8,128)S(1)}, u32[]{:S(2)}, u32[]{:S(2)}) collective-permute-start(f32[200,128]{1,0:T(8,128)S(1)} %shard_map.60.own), channel_id=1, source_target_pairs={{0,192},{64,0},{128,64},{192,128},{1,193},{65,1},{129,65},{193,129... | collective-permute-start | bytes 307208 | tf_op jit(solution)/shard_map/ppermute | solution.py:253
  59.0 3.9 %collective-permute-done.11.two = f32[200,128]{1,0:T(8,128)S(1)} collective-permute-done((f32[200,128]{1,0:T(8,128)S(1)}, f32[200,128]{1,0:T(8,128)S(1)}, u32[]{:S(2)}, u32[]{:S(2)}) %collective-permute-start.11) | collective-permute-done | bytes 102432 | tf_op jit(solution)/shard_map/ppermute | solution.py:253
  62.9 3.3 %collective-permute-done.12.three = f32[200,128]{1,0:T(8,128)S(1)} collective-permute-done((f32[200,128]{1,0:T(8,128)S(1)}, f32[200,128]{1,0:T(8,128)S(1)}, u32[]{:S(2)}, u32[]{:S(2)}) %collective-permute-start.12) | collective-permute-done | bytes 102432 | tf_op jit(solution)/shard_map/ppermute | solution.py:253
  66.2 1.7 %shard_map.61 = (f32[32,768]{1,0:T(8,128)S(1)}, s16[32,208,128]{2,1,0:T(8,128)(2,1)}) custom-call(f32[200,128]{1,0:T(8,128)S(1)} %shard_map.60.own, f32[200,128]{1,0:T(8,128)S(1)} %collective-permute-done.10.one, f32[200,128]{1,0:T(8,128)S(1)} %collective-permute-done.11.two, f32[200,128]{1,0:T(8,128)S(1)} %collective-permute-done.12.three), custom_call_target="tpu_custom_call" | custom-call | flops 1048576 | bytes 2097152 | tf_op jit(solution)/shard_map/pallas_call | solution.py:195
  67.9 4.1 %all-to-all-start.1 = ((s16[32,208,128]{2,1,0:T(8,128)(2,1)}), s16[32,208,128]{2,1,0:T(8,128)(2,1)S(1)}, u32[]{:S(2)}, u32[]{:S(2)}) async-start(s16[32,208,128]{2,1,0:T(8,128)(2,1)} %get-tuple-element.6), calls=%async_computation.1 | async-start | bytes 3407872 | tf_op jit(solution)/shard_map/all_to_all | solution.py:271
  72.1 1.2 collective-permute-start
  74.0 19.0 %collective-permute-done = bf16[32,768]{1,0:T(8,128)(2,1)S(1)} collective-permute-done((bf16[32,768]{1,0:T(8,128)(2,1)S(1)}, bf16[32,768]{1,0:T(8,128)(2,1)S(1)}, u32[]{:S(2)}, u32[]{:S(2)}) %collective-permute-start) | collective-permute-done | bytes 49184 | tf_op jit(solution)/shard_map/ppermute | solution.py:212
  92.9 1.2 collective-permute-start.1
  94.2 2.1 %collective-permute-start.2 = (bf16[64,768]{1,0:T(8,128)(2,1)S(1)}, bf16[64,768]{1,0:T(8,128)(2,1)S(1)}, u32[]{:S(2)}, u32[]{:S(2)}) collective-permute-start(bf16[64,768]{1,0:T(8,128)(2,1)S(1)} %pad_maximum_fusion.1), channel_id=1, source_target_pairs={{0,4},{2,6},{4,0},{6,2},{1,5},{3,7},{5,1},{7,3},{8,12},{10,14},{12... | collective-permute-start | bytes 294920 | tf_op jit(solution)/shard_map/ppermute | solution.py:219
  96.3 1.1 collective-permute-start.3
  100.7 1.2 collective-permute-start.4
  102.0 2.5 %collective-permute-start.5 = (bf16[256,768]{1,0:T(8,128)(2,1)S(1)}, bf16[256,768]{1,0:T(8,128)(2,1)S(1)}, u32[]{:S(2)}, u32[]{:S(2)}) collective-permute-start(bf16[256,768]{1,0:T(8,128)(2,1)S(1)} %get-tuple-element.11), channel_id=1, source_target_pairs={{0,16},{8,24},{16,0},{24,8},{1,17},{9,25},{17,1},{25,9},{2,18},{10... | collective-permute-start | bytes 1179656 | tf_op jit(solution)/shard_map/ppermute | solution.py:219
  104.5 1.1 collective-permute-start.6
  105.6 3.7 %collective-permute-done.4 = bf16[256,768]{1,0:T(8,128)(2,1)S(1)} collective-permute-done((bf16[256,768]{1,0:T(8,128)(2,1)S(1)}, bf16[256,768]{1,0:T(8,128)(2,1)S(1)}, u32[]{:S(2)}, u32[]{:S(2)}) %collective-permute-start.4) | collective-permute-done | bytes 393248 | tf_op jit(solution)/shard_map/ppermute | solution.py:219
  109.3 0.8 constant_dynamic-update-slice_fusion.7
  110.0 8.7 %collective-permute-done.5 = bf16[256,768]{1,0:T(8,128)(2,1)S(1)} collective-permute-done((bf16[256,768]{1,0:T(8,128)(2,1)S(1)}, bf16[256,768]{1,0:T(8,128)(2,1)S(1)}, u32[]{:S(2)}, u32[]{:S(2)}) %collective-permute-start.5) | collective-permute-done | bytes 393248 | tf_op jit(solution)/shard_map/ppermute | solution.py:219
  118.8 0.8 constant_dynamic-update-slice_fusion.6
  120.1 0.8 constant_dynamic-update-slice_fusion.5.own_ref
  120.9 3.7 %collective-permute-start.7 = (bf16[1024,768]{1,0:T(8,128)(2,1)}, bf16[1024,768]{1,0:T(8,128)(2,1)}, u32[]{:S(2)}, u32[]{:S(2)}) collective-permute-start(bf16[1024,768]{1,0:T(8,128)(2,1)} %constant_dynamic-update-slice_fusion.5.own_ref), channel_id=1, source_target_pairs={{0,32},{32,0},{1,33},{33,1},{2,34},{34,2},{3,35},{35,3},{4,36},{36... | collective-permute-start | bytes 4718600 | tf_op jit(solution)/shard_map/ppermute | solution.py:212
  124.9 0.8 collective-permute-start.13
  125.7 4.4 %collective-permute-done.7.other_ref = bf16[1024,768]{1,0:T(8,128)(2,1)} collective-permute-done((bf16[1024,768]{1,0:T(8,128)(2,1)}, bf16[1024,768]{1,0:T(8,128)(2,1)}, u32[]{:S(2)}, u32[]{:S(2)}) %collective-permute-start.7) | collective-permute-done | bytes 1572896 | tf_op jit(solution)/shard_map/ppermute | solution.py:212
  130.1 7.8 %shard_map.58 = f32[1,1024]{1,0:T(1,128)} custom-call(f32[1,1024]{1,0:T(1,128)S(1)} %bitcast.4, bf16[1024,768]{1,0:T(8,128)(2,1)S(1)} %copy-done.1, bf16[1024,768]{1,0:T(8,128)(2,1)} %constant_dynamic-update-slice_fusion.5.own_ref, bf16[1024,768]{1,0:T(8,128)(2,1)} %collective-permute-done.7.other_ref), custom_call_target="tpu_custom_call" | custom-call | flops 3221225472 | bytes 5242880 | tf_op jit(solution)/shard_map/pallas_call | solution.py:195
  138.6 4.5 %shard_map.62.least_ref = f32[8,1024]{1,0:T(8,128)S(1)} custom-call(bf16[1024,768]{1,0:T(8,128)(2,1)S(1)} %copy-done.1, s16[32,208,128]{2,1,0:T(8,128)(2,1)S(1)} %all-to-all-done.1.coded_ref, f32[8,1024]{1,0:T(8,128)S(1)} %broadcast_in_dim.3.least_ref), custom_call_target="tpu_custom_call" | custom-call | flops 3221225472 | bytes 3145728 | tf_op jit(solution)/shard_map/pallas_call | solution.py:195
  143.1 5.9 %shard_map.63 = f32[8,1024]{1,0:T(8,128)S(1)} custom-call(bf16[1024,768]{1,0:T(8,128)(2,1)S(1)} %copy-done.1, s16[32,208,128]{2,1,0:T(8,128)(2,1)} %collective-permute-done.14.coded_ref, f32[8,1024]{1,0:T(8,128)S(1)} %shard_map.62.least_ref), custom_call_target="tpu_custom_call" | custom-call | flops 3221225472 | bytes 3145728 | tf_op jit(solution)/shard_map/pallas_call | solution.py:195
  (31 shorter events, 7.0 us)
Async XLA Ops:
  0.6 6.6 %collective-permute-start.9 = (bf16[1024,768]{1,0:T(8,128)(2,1)}, bf16[1024,768]{1,0:T(8,128)(2,1)S(1)}, u32[]{:S(2)}, u32[]{:S(2)}) collective-permute-start(bf16[1024,768]{1,0:T(8,128)(2,1)} %rows_ref.5), channel_id=1, source_target_pairs={{0,32},{32,0},{1,33},{33,1},{2,34},{34,2},{3,35},{35,3},{4,36},{36... | collective-permute-start | bytes 4718600 | tf_op jit(solution)/shard_map/ppermute | solution.py:212
  4.0 3.3 %collective-permute-start.8 = (s32[1,1024]{1,0:T(1,128)}, s32[1,1024]{1,0:T(1,128)S(1)}, u32[]{:S(2)}, u32[]{:S(2)}) collective-permute-start(s32[1,1024]{1,0:T(1,128)} %bitcast.5), channel_id=1, source_target_pairs={{0,32},{32,0},{1,33},{33,1},{2,34},{34,2},{3,35},{35,3},{4,36},{36... | collective-permute-start | bytes 12296 | tf_op jit(solution)/shard_map/ppermute | solution.py:212
  7.2 1.4 copy-start
  8.6 0.7 copy-start.2
  49.3 9.7 %collective-permute-start.10 = (f32[200,128]{1,0:T(8,128)S(1)}, f32[200,128]{1,0:T(8,128)S(1)}, u32[]{:S(2)}, u32[]{:S(2)}) collective-permute-start(f32[200,128]{1,0:T(8,128)S(1)} %shard_map.60.own), channel_id=1, source_target_pairs={{0,64},{64,128},{128,192},{192,0},{1,65},{65,129},{129,193},{193,1... | collective-permute-start | bytes 307208 | tf_op jit(solution)/shard_map/ppermute | solution.py:253
  52.4 10.5 %collective-permute-start.11 = (f32[200,128]{1,0:T(8,128)S(1)}, f32[200,128]{1,0:T(8,128)S(1)}, u32[]{:S(2)}, u32[]{:S(2)}) collective-permute-start(f32[200,128]{1,0:T(8,128)S(1)} %shard_map.60.own), channel_id=1, source_target_pairs={{0,128},{64,192},{128,0},{192,64},{1,129},{65,193},{129,1},{193,65... | collective-permute-start | bytes 307208 | tf_op jit(solution)/shard_map/ppermute | solution.py:253
  56.6 9.6 %collective-permute-start.12 = (f32[200,128]{1,0:T(8,128)S(1)}, f32[200,128]{1,0:T(8,128)S(1)}, u32[]{:S(2)}, u32[]{:S(2)}) collective-permute-start(f32[200,128]{1,0:T(8,128)S(1)} %shard_map.60.own), channel_id=1, source_target_pairs={{0,192},{64,0},{128,64},{192,128},{1,193},{65,1},{129,65},{193,129... | collective-permute-start | bytes 307208 | tf_op jit(solution)/shard_map/ppermute | solution.py:253
  67.9 4.1 %copy-start.3 = (bf16[64,768]{1,0:T(8,128)(2,1)S(1)}, bf16[64,768]{1,0:T(8,128)(2,1)}, u32[]{:S(2)}) copy-start(bf16[64,768]{1,0:T(8,128)(2,1)} %param.4) | copy-start | bytes 294916
  67.9 56.6 %all-to-all-start.1 = ((s16[32,208,128]{2,1,0:T(8,128)(2,1)}), s16[32,208,128]{2,1,0:T(8,128)(2,1)S(1)}, u32[]{:S(2)}, u32[]{:S(2)}) async-start(s16[32,208,128]{2,1,0:T(8,128)(2,1)} %get-tuple-element.6), calls=%async_computation.1 | async-start | bytes 3407872 | tf_op jit(solution)/shard_map/all_to_all | solution.py:271
  72.1 20.8 %collective-permute-start = (bf16[32,768]{1,0:T(8,128)(2,1)S(1)}, bf16[32,768]{1,0:T(8,128)(2,1)S(1)}, u32[]{:S(2)}, u32[]{:S(2)}) collective-permute-start(bf16[32,768]{1,0:T(8,128)(2,1)S(1)} %get-tuple-element.8), channel_id=1, source_target_pairs={{0,1},{1,0},{2,3},{3,2},{4,5},{5,4},{6,7},{7,6},{8,9},{9,8},{10,11... | collective-permute-start | bytes 147464 | tf_op jit(solution)/shard_map/ppermute | solution.py:212
  92.9 5.2 %collective-permute-start.1 = (bf16[64,768]{1,0:T(8,128)(2,1)S(1)}, bf16[64,768]{1,0:T(8,128)(2,1)S(1)}, u32[]{:S(2)}, u32[]{:S(2)}) collective-permute-start(bf16[64,768]{1,0:T(8,128)(2,1)S(1)} %pad_maximum_fusion.1), channel_id=1, source_target_pairs={{0,2},{2,4},{4,6},{6,0},{1,3},{3,5},{5,7},{7,1},{8,10},{10,12},{12... | collective-permute-start | bytes 294920 | tf_op jit(solution)/shard_map/ppermute | solution.py:219
  94.2 5.2 %collective-permute-start.2 = (bf16[64,768]{1,0:T(8,128)(2,1)S(1)}, bf16[64,768]{1,0:T(8,128)(2,1)S(1)}, u32[]{:S(2)}, u32[]{:S(2)}) collective-permute-start(bf16[64,768]{1,0:T(8,128)(2,1)S(1)} %pad_maximum_fusion.1), channel_id=1, source_target_pairs={{0,4},{2,6},{4,0},{6,2},{1,5},{3,7},{5,1},{7,3},{8,12},{10,14},{12... | collective-permute-start | bytes 294920 | tf_op jit(solution)/shard_map/ppermute | solution.py:219
  96.3 3.8 %collective-permute-start.3 = (bf16[64,768]{1,0:T(8,128)(2,1)S(1)}, bf16[64,768]{1,0:T(8,128)(2,1)S(1)}, u32[]{:S(2)}, u32[]{:S(2)}) collective-permute-start(bf16[64,768]{1,0:T(8,128)(2,1)S(1)} %pad_maximum_fusion.1), channel_id=1, source_target_pairs={{0,6},{2,0},{4,2},{6,4},{1,7},{3,1},{5,3},{7,5},{8,14},{10,8},{12,... | collective-permute-start | bytes 294920 | tf_op jit(solution)/shard_map/ppermute | solution.py:219
  98.1 26.5 %copy-start.1 = (bf16[1024,768]{1,0:T(8,128)(2,1)S(1)}, bf16[1024,768]{1,0:T(8,128)(2,1)}, u32[]{:S(2)}) copy-start(bf16[1024,768]{1,0:T(8,128)(2,1)} %rows_ref.5) | copy-start | bytes 4718596
  100.7 8.5 %collective-permute-start.4 = (bf16[256,768]{1,0:T(8,128)(2,1)S(1)}, bf16[256,768]{1,0:T(8,128)(2,1)S(1)}, u32[]{:S(2)}, u32[]{:S(2)}) collective-permute-start(bf16[256,768]{1,0:T(8,128)(2,1)S(1)} %get-tuple-element.11), channel_id=1, source_target_pairs={{0,8},{8,16},{16,24},{24,0},{1,9},{9,17},{17,25},{25,1},{2,10},{10... | collective-permute-start | bytes 1179656 | tf_op jit(solution)/shard_map/ppermute | solution.py:219
  102.0 16.8 %collective-permute-start.5 = (bf16[256,768]{1,0:T(8,128)(2,1)S(1)}, bf16[256,768]{1,0:T(8,128)(2,1)S(1)}, u32[]{:S(2)}, u32[]{:S(2)}) collective-permute-start(bf16[256,768]{1,0:T(8,128)(2,1)S(1)} %get-tuple-element.11), channel_id=1, source_target_pairs={{0,16},{8,24},{16,0},{24,8},{1,17},{9,25},{17,1},{25,9},{2,18},{10... | collective-permute-start | bytes 1179656 | tf_op jit(solution)/shard_map/ppermute | solution.py:219
  104.5 15.6 %collective-permute-start.6 = (bf16[256,768]{1,0:T(8,128)(2,1)S(1)}, bf16[256,768]{1,0:T(8,128)(2,1)S(1)}, u32[]{:S(2)}, u32[]{:S(2)}) collective-permute-start(bf16[256,768]{1,0:T(8,128)(2,1)S(1)} %get-tuple-element.11), channel_id=1, source_target_pairs={{0,24},{8,0},{16,8},{24,16},{1,25},{9,1},{17,9},{25,17},{2,26},{10... | collective-permute-start | bytes 1179656 | tf_op jit(solution)/shard_map/ppermute | solution.py:219
  120.9 9.2 %collective-permute-start.7 = (bf16[1024,768]{1,0:T(8,128)(2,1)}, bf16[1024,768]{1,0:T(8,128)(2,1)}, u32[]{:S(2)}, u32[]{:S(2)}) collective-permute-start(bf16[1024,768]{1,0:T(8,128)(2,1)} %constant_dynamic-update-slice_fusion.5.own_ref), channel_id=1, source_target_pairs={{0,32},{32,0},{1,33},{33,1},{2,34},{34,2},{3,35},{35,3},{4,36},{36... | collective-permute-start | bytes 4718600 | tf_op jit(solution)/shard_map/ppermute | solution.py:212
  124.6 18.5 %collective-permute-start.14 = (s16[32,208,128]{2,1,0:T(8,128)(2,1)S(1)}, s16[32,208,128]{2,1,0:T(8,128)(2,1)}, u32[]{:S(2)}, u32[]{:S(2)}) collective-permute-start(s16[32,208,128]{2,1,0:T(8,128)(2,1)S(1)} %all-to-all-done.1.coded_ref), channel_id=1, source_target_pairs={{0,32},{32,0},{1,33},{33,1},{2,34},{34,2},{3,35},{35,3},{4,36},{36... | collective-permute-start | bytes 5111816 | tf_op jit(solution)/shard_map/ppermute | solution.py:212
  124.9 12.9 %collective-permute-start.13 = (f32[32,768]{1,0:T(8,128)S(1)}, f32[32,768]{1,0:T(8,128)S(1)}, u32[]{:S(2)}, u32[]{:S(2)}) collective-permute-start(f32[32,768]{1,0:T(8,128)S(1)} %get-tuple-element.5), channel_id=1, source_target_pairs={{0,32},{32,0},{1,33},{33,1},{2,34},{34,2},{3,35},{35,3},{4,36},{36... | collective-permute-start | bytes 294920 | tf_op jit(solution)/shard_map/ppermute | solution.py:212

commit v2 on v1

v2 whole, which is shorter than its diff:
```python
import jax
import jax.numpy as jnp
from jax import lax
from jax.experimental import pallas as pl
from jax.experimental.pallas import tpu as pltpu
from jax.sharding import Mesh, PartitionSpec as P

AXES = ("zh", "core", "y", "x", "zl")
SIZES = (4, 2, 4, 4, 2)
SHARD = ("y", "x", "zl")

D = 768
HALF = 32
CHUNKS = 32
COLS = D // 128
BODY = COLS * HALF
CODED = BODY + 16
LIMIT = 32700.0
VMEM = 16 * 1024 * 1024


def diagonal(rows):
    r = lax.broadcasted_iota(jnp.int32, (rows, 128), 0) % HALF
    c = lax.broadcasted_iota(jnp.int32, (rows, 128), 1)
    return r == c


def to_lanes(column):
    return jnp.sum(jnp.where(diagonal(HALF), column, 0.0), 0, keepdims=True)


def to_column(row):
    return jnp.sum(jnp.where(diagonal(HALF), row, 0.0), 1, keepdims=True)


def code_of(values):
    most = jnp.max(jnp.abs(values), 1, keepdims=True)
    return jnp.ceil(jnp.log2(jnp.maximum(most, 1e-30)) * 256.0)


def quantize(values, code):
    scaled = values * (LIMIT * jnp.exp2(code * (-1.0 / 256.0)))
    return jnp.floor(scaled + 0.5).astype(jnp.int32).astype(jnp.int16)


def scale_of(code):
    return jnp.exp2(code * (1.0 / 256.0)) * (1.0 / LIMIT)


def footer(counts, codes):
    r = lax.broadcasted_iota(jnp.int32, (16, 128), 0)
    both = jnp.where(r == 0, counts, jnp.where(r == 1, codes, 0.0))
    return both.astype(jnp.int32).astype(jnp.int16)


TILE = 256


def is_named(t, base, labels):
    j = t * TILE + lax.broadcasted_iota(jnp.int32, (TILE, 1), 0)
    k = j + (j // HALF) * HALF + base
    return jnp.where(k == labels, 1.0, 0.0)


def own_sums_kernel(base_ref, labels, rows, out_ref):
    for t in range(CHUNKS * HALF // TILE):
        hot = is_named(t, base_ref[0], labels[...]).astype(jnp.bfloat16)
        out_ref[t * TILE : (t + 1) * TILE, :] = jnp.dot(
            hot, rows[...], preferred_element_type=jnp.float32
        )


def chip_sums_kernel(base_ref, own_labels, labels, own_sums, rows, out_ref):
    for t in range(CHUNKS * HALF // TILE):
        hot = is_named(t, base_ref[0], labels[...])
        sums = own_sums[t * TILE : (t + 1) * TILE, :] + jnp.dot(
            hot.astype(jnp.bfloat16), rows[...], preferred_element_type=jnp.float32
        )
        hot = hot + is_named(t, base_ref[0], own_labels[...])
        counts = jnp.sum(hot, 1, keepdims=True)
        code = code_of(sums)
        coded = quantize(sums, code)
        for c in range(TILE // HALF):
            at = t * (TILE // HALF) + c
            part = slice(c * HALF, (c + 1) * HALF)
            for b in range(COLS):
                out_ref[at, b * HALF : (b + 1) * HALF, :] = coded[
                    part, b * 128 : (b + 1) * 128
                ]
            out_ref[at, BODY:CODED, :] = footer(
                to_lanes(counts[part]), to_lanes(code[part])
            )


def block(b):
    return slice(b * HALF, (b + 1) * HALF)


def add_coded(ref, at, blocks, counts):
    foot = ref[at, BODY:CODED, :].astype(jnp.float32)
    scale = scale_of(to_column(foot[1:2, :]))
    blocks = [
        blocks[b] + ref[at, block(b), :].astype(jnp.float32) * scale
        for b in range(COLS)
    ]
    return blocks, counts + foot[0:1, :]


def nothing():
    zeros = [jnp.zeros((HALF, 128), jnp.float32) for _ in range(COLS)]
    return zeros, jnp.zeros((1, 128), jnp.float32)


def code_blocks(blocks):
    most = jnp.abs(blocks[0])
    for b in range(1, COLS):
        most = jnp.maximum(most, jnp.abs(blocks[b]))
    code = code_of(most)
    return [quantize(blocks[b], code) for b in range(COLS)], to_lanes(code)


def group_kernel(in_ref, c0, c1, c2, c3, out_ref, centers_ref):
    together = 8

    def step(t, carry):
        blocks, counts = list(carry[0]), carry[1]
        for i in range(together):
            blocks, counts = add_coded(in_ref, t * together + i, blocks, counts)
        return tuple(blocks), counts

    blocks, counts = nothing()
    blocks, counts = lax.fori_loop(0, CHUNKS // together, step, (tuple(blocks), counts))
    coded, codes = code_blocks(blocks)
    for b in range(COLS):
        out_ref[0, block(b), :] = coded[b]
    out_ref[0, BODY:CODED, :] = footer(counts, codes)
    for i, ref in enumerate((c0, c1, c2, c3)):
        n = ref.shape[0]
        centers_ref[i * n : (i + 1) * n, :] = ref[...]


def refine_kernel(own, one, two, three, refined_ref, coded_ref):
    even = add_coded(two, 0, *add_coded(own, 0, *nothing()))
    odd = add_coded(three, 0, *add_coded(one, 0, *nothing()))
    counts = to_column(even[1] + odd[1])
    refined = [(even[0][b] + odd[0][b]) / counts for b in range(COLS)]
    for b in range(COLS):
        refined_ref[:, b * 128 : (b + 1) * 128] = refined[b]
    coded, codes = code_blocks(refined)
    foot = footer(jnp.zeros_like(codes), codes)

    def step(s, carry):
        for b in range(COLS):
            coded_ref[s, block(b), :] = coded[b]
        coded_ref[s, BODY:CODED, :] = foot
        return carry

    lax.fori_loop(0, CHUNKS, step, 0)


def nearest(value, least):
    n = value.shape[0]
    return jnp.minimum(least, jnp.min(value.reshape(n // 8, 8, value.shape[1]), 0))


def old_kernel(norms_ref, rows_ref, *refs):
    *centers, out_ref, turned_ref = refs
    turned_ref[...] = (rows_ref[...] * jnp.bfloat16(-2.0)).T
    turned = turned_ref[...]
    least = jnp.full((8, turned.shape[1]), jnp.inf, jnp.float32)
    for ref in centers:
        wide = ref[...].astype(jnp.float32)
        norm = jnp.sum(wide * wide, 1, keepdims=True)
        product = jnp.dot(ref[...], turned, preferred_element_type=jnp.float32)
        least = nearest(product + norm, least)
    out_ref[...] = norms_ref[...] + jnp.min(least, 0, keepdims=True)


def new_kernel(turned_ref, coded_ref, norms_ref, least_ref, out_ref):
    per = TILE // HALF
    turned = turned_ref[...]
    least = least_ref[...]
    for t in range(CHUNKS // per):
        high, low, scale, norm = [], [], [], []
        for c in range(per):
            at = t * per + c
            wide = jnp.concatenate(
                [coded_ref[at, block(b), :].astype(jnp.float32) for b in range(COLS)], 1
            )
            top = wide.astype(jnp.bfloat16)
            high.append(top)
            low.append((wide - top.astype(jnp.float32)).astype(jnp.bfloat16))
            foot = coded_ref[at, BODY:CODED, :].astype(jnp.float32)
            s = scale_of(to_column(foot[1:2, :]))
            scale.append(s)
            norm.append(jnp.sum(wide * wide, 1, keepdims=True) * (s * s))
        product = jnp.dot(
            jnp.concatenate(high, 0), turned, preferred_element_type=jnp.float32
        ) + jnp.dot(jnp.concatenate(low, 0), turned, preferred_element_type=jnp.float32)
        value = product * jnp.concatenate(scale, 0) + jnp.concatenate(norm, 0)
        least = nearest(value, least)
    if out_ref.shape == least.shape:
        out_ref[...] = least
    else:
        out_ref[...] = norms_ref[...] + jnp.min(least, 0, keepdims=True)


def call(kernel, out_shape, *args, flops=0, moved=0, smem=0):
    specs = [
        pl.BlockSpec(memory_space=pltpu.SMEM if i < smem else pltpu.VMEM)
        for i in range(len(args))
    ]
    many = isinstance(out_shape, tuple)
    out_specs = pl.BlockSpec(memory_space=pltpu.VMEM)
    return pl.pallas_call(
        kernel,
        out_shape=out_shape,
        in_specs=specs,
        out_specs=tuple([out_specs] * len(out_shape)) if many else out_specs,
        compiler_params=pltpu.CompilerParams(vmem_limit_bytes=VMEM),
        cost_estimate=pl.CostEstimate(
            flops=flops, bytes_accessed=moved, transcendentals=0
        ),
    )(*args)


def ring(axis, size, k):
    return [(i, (i + k) % size) for i in range(size)]


def swap(value, axis):
    return lax.ppermute(value, axis, [(0, 1), (1, 0)])


def around(part, axis):
    return [part] + [lax.ppermute(part, axis, ring(axis, 4, k)) for k in (1, 2, 3)]


def after(first, values):
    return lax.optimization_barrier((first, *values))[1:]


def on_device(embeddings, centers, assignment):
    n = embeddings.shape[0]
    core = lax.axis_index("core")
    f32, bf16, i16 = jnp.float32, jnp.bfloat16, jnp.int16
    shape = jax.ShapeDtypeStruct
    labels = assignment.reshape(1, n)
    other_labels = swap(labels, "core")
    other_rows = swap(embeddings, "core")

    mine = lax.dynamic_slice(centers, (core * HALF, 0), (HALF, D))
    current = around(jnp.concatenate([mine, swap(mine, "zl")]), "x")

    wide = embeddings.astype(f32)
    norms = jnp.sum(wide * wide, 1).reshape(1, n)

    base = (core * HALF).astype(jnp.int32).reshape(1)
    sums = call(
        own_sums_kernel,
        shape((CHUNKS * HALF, D), f32),
        base, labels, embeddings,
        flops=2 * 1024 * n * D, moved=5 << 20, smem=1,
    )
    sums = call(
        chip_sums_kernel,
        shape((CHUNKS, CODED, 128), i16),
        base, labels, other_labels, sums, other_rows,
        flops=2 * 1024 * n * D, moved=6 << 20, smem=1,
    )
    sums = lax.all_to_all(sums, SHARD, 0, 0)
    group, current = call(
        group_kernel,
        (shape((1, CODED, 128), i16), shape((8 * HALF, D), bf16)),
        sums, *current,
        flops=1 << 22, moved=2 << 20,
    )
    current = around(current, "y")
    groups, current[1], current[3] = lax.optimization_barrier(
        (around(group, "zh"), current[1], current[3])
    )
    refined, coded = call(
        refine_kernel,
        (shape((HALF, D), f32), shape((CHUNKS, CODED, 128), i16)),
        *groups,
        flops=1 << 20, moved=2 << 20,
    )
    new_own = lax.all_to_all(coded, SHARD, 0, 0)

    current = after(coded, current)
    current = current + tuple(swap(part, "core") for part in current)
    old_min, turned = call(
        old_kernel,
        (shape((1, n), f32), shape((D, n), bf16)),
        norms, embeddings, *current,
        flops=2 * 2048 * n * D, moved=5 << 20,
    )

    refined_other = swap(refined, "core")
    first = core == 0
    refined_centers = jnp.concatenate(
        [
            jnp.where(first, refined, refined_other),
            jnp.where(first, refined_other, refined),
        ]
    )

    (new_own,) = after(turned, (new_own,))
    new_other = swap(new_own, "core")
    least = jnp.full((8, n), jnp.inf, f32)
    for coded, result in ((new_own, 8), (new_other, 1)):
        least = call(
            new_kernel,
            shape((result, n), f32),
            turned, coded, norms, least,
            flops=2 * 2048 * n * D, moved=3 << 20,
        )
    return old_min.reshape(n), refined_centers, least.reshape(n)


def solution(mesh):
    fine = Mesh(mesh.devices.reshape(SIZES), AXES)
    rows = ("zh", "core") + SHARD
    return jax.shard_map(
        on_device,
        mesh=fine,
        in_specs=(P(rows, None), P(SHARD, None), P(rows, None)),
        out_specs=(P(rows), P(SHARD, None), P(rows)),
        check_vma=False,
    )
```

time: 151 us -> 130 us (0.86)
  blocking collectives: 30.4 us -> 0 us
  waiting for transfers between devices: 47.4 us -> 56.9 us
  starting transfers between devices: 32.3 us -> 40.5 us
  Pallas kernels: 29.4 us -> 22.8 us
    all_to_all x1 -> x0, blocking collectives: 30.4 us -> none  [on_device(): sums = lax.all_to_all(sums, SHARD, 0, 0)]
    ppermute x9, waiting for transfers between devices: 20.9 us -> 31.5 us  [around(): lax.ppermute(part, axis, ring(axis, 4, k))]
    all_to_all x0 -> x1, starting transfers between devices: none -> 6.67 us  [on_device(): sums = lax.all_to_all(sums, SHARD, 0, 0)]
    pallas_call x6 -> x7, Pallas kernels: 29.4 us -> 22.8 us  [call(): pl.pallas_call(kernel, out_shape=out_shape, in_specs=specs, out_specs=tup...]
    all_to_all x1, starting transfers between devices: 4.11 us -> 5.96 us  [on_device(): new_own = lax.all_to_all(coded, SHARD, 0, 0)]
    unnamed x15 -> x22, local copies, waits for them, and re-layouts: 6.22 us -> 7.44 us
    ppermute x6 -> x9, starting transfers between devices: 9.1 us -> 8.04 us  [swap(): return lax.ppermute(value, axis, [(0, 1), (1, 0)])]
    ppermute x6 -> x9, waiting for transfers between devices: 26.5 us -> 25.5 us  [swap(): return lax.ppermute(value, axis, [(0, 1), (1, 0)])]
  transfers between devices with their start and end apart: 16 -> 20, of which waited for: 9 -> 11; matrix products, arithmetic and copies ran while one was open for 4% -> 1% of each run, Pallas kernels for 8% -> 8%
where the time goes in v2:
time: 130 us
  waiting for transfers between devices  56.9 us (44%)
  starting transfers between devices  40.5 us (31%)
  Pallas kernels  22.8 us (18%)
  local copies, waits for them, and re-layouts  7.46 us (6%)
    ppermute x9, waiting for transfers between devices, around(): lax.ppermute(part, axis, ring(axis, 4, k))  31.5 us
    ppermute x9, waiting for transfers between devices, swap(): return lax.ppermute(value, axis, [(0, 1), (1, 0)])  25.5 us
    pallas_call x7, Pallas kernels, call(): pl.pallas_call(kernel, out_shape=out_shape, in_specs=specs, out_specs=tup...  22.8 us
    ppermute x9, starting transfers between devices, around(): lax.ppermute(part, axis, ring(axis, 4, k))  19.8 us
    ppermute x9, starting transfers between devices, swap(): return lax.ppermute(value, axis, [(0, 1), (1, 0)])  8.04 us
    unnamed x22, local copies, waits for them, and re-layouts  7.44 us
    all_to_all x1, starting transfers between devices, on_device(): sums = lax.all_to_all(sums, SHARD, 0, 0)  6.67 us
    all_to_all x1, starting transfers between devices, on_device(): new_own = lax.all_to_all(coded, SHARD, 0, 0)  5.96 us
  transfers between devices with their start and end apart: 20, of which 11 were waited for; matrix products, arithmetic and copies ran while one was open for 1% of the time, Pallas kernels for 8%

profile of v2, /device:TPU:1, one launch (start us, length us, event | category | flops | bytes accessed | tf_op | source)
XLA Modules:
  0.0 129.5 jit_solution(238456563302320729)
XLA Ops:
  0.6 3.3 %collective-permute-start.1 = (bf16[1024,768]{1,0:T(8,128)(2,1)}, bf16[1024,768]{1,0:T(8,128)(2,1)S(1)}, u32[]{:S(2)}, u32[]{:S(2)}) collective-permute-start(bf16[1024,768]{1,0:T(8,128)(2,1)} %rows_ref.1), channel_id=1, source_target_pairs={{0,32},{32,0},{1,33},{33,1},{2,34},{34,2},{3,35},{35,3},{4,36},{36... | collective-permute-start | bytes 4718600 | tf_op jit(solution)/shard_map/ppermute | solution.py:232
  4.1 1.4 %copy-done.1 = bf16[1024,768]{1,0:T(8,128)(2,1)S(1)} copy-done((bf16[1024,768]{1,0:T(8,128)(2,1)S(1)}, bf16[1024,768]{1,0:T(8,128)(2,1)}, u32[]{:S(2)}) %copy-start.1) | copy-done | bytes 1572888
  6.2 1.8 %shard_map.58.own_sums = f32[1024,768]{1,0:T(8,128)S(1)} custom-call(s32[1]{0:T(128)} %bitcast.1.base_ref, s32[1,1024]{1,0:T(1,128)S(1)} %bitcast.6, bf16[1024,768]{1,0:T(8,128)(2,1)S(1)} %copy-done.1), custom_call_target="tpu_custom_call" | custom-call | flops 1610612736 | bytes 5242880 | tf_op jit(solution)/shard_map/pallas_call | solution.py:215
  8.0 4.2 %shard_map.59 = s16[32,208,128]{2,1,0:T(8,128)(2,1)} custom-call(s32[1]{0:T(128)} %bitcast.1.base_ref, s32[1,1024]{1,0:T(1,128)S(1)} %bitcast.7, s32[1,1024]{1,0:T(1,128)S(1)} %collective-permute-done.labels, f32[1024,768]{1,0:T(8,128)S(1)} %shard_map.58.own_sums, bf16[1024,768]{1,0:T(8,128)(2,1)S(1)} %collective-permute-done.1.rows), custom_call_target="tpu_custom_call" | custom-call | flops 1610612736 | bytes 6291456 | tf_op jit(solution)/shard_map/pallas_call | solution.py:215
  12.2 6.7 %all-to-all-start = ((s16[32,208,128]{2,1,0:T(8,128)(2,1)}), s16[32,208,128]{2,1,0:T(8,128)(2,1)S(1)}, u32[]{:S(2)}, u32[]{:S(2)}) async-start(s16[32,208,128]{2,1,0:T(8,128)(2,1)} %shard_map.59), calls=%async_computation | async-start | bytes 3407872 | tf_op jit(solution)/shard_map/all_to_all | solution.py:271
  18.9 1.3 %collective-permute-start.2 = (bf16[32,768]{1,0:T(8,128)(2,1)S(1)}, bf16[32,768]{1,0:T(8,128)(2,1)S(1)}, u32[]{:S(2)}, u32[]{:S(2)}) collective-permute-start(bf16[32,768]{1,0:T(8,128)(2,1)S(1)} %constant_dynamic-slice_fusion), channel_id=1, source_target_pairs={{0,1},{1,0},{2,3},{3,2},{4,5},{5,4},{6,7},{7,6},{8,9},{9,8},{10,11... | collective-permute-start | bytes 147464 | tf_op jit(solution)/shard_map/ppermute | solution.py:232
  20.2 19.9 %collective-permute-done.2 = bf16[32,768]{1,0:T(8,128)(2,1)S(1)} collective-permute-done((bf16[32,768]{1,0:T(8,128)(2,1)S(1)}, bf16[32,768]{1,0:T(8,128)(2,1)S(1)}, u32[]{:S(2)}, u32[]{:S(2)}) %collective-permute-start.2) | collective-permute-done | bytes 49184 | tf_op jit(solution)/shard_map/ppermute | solution.py:232
  40.1 1.3 collective-permute-start.3
  41.4 2.2 %collective-permute-start.4 = (bf16[64,768]{1,0:T(8,128)(2,1)S(1)}, bf16[64,768]{1,0:T(8,128)(2,1)S(1)}, u32[]{:S(2)}, u32[]{:S(2)}) collective-permute-start(bf16[64,768]{1,0:T(8,128)(2,1)S(1)} %pad_maximum_fusion.1.c0), channel_id=1, source_target_pairs={{0,4},{2,6},{4,0},{6,2},{1,5},{3,7},{5,1},{7,3},{8,12},{10,14},{12... | collective-permute-start | bytes 294920 | tf_op jit(solution)/shard_map/ppermute | solution.py:236
  43.6 1.0 collective-permute-start.5
  44.9 1.8 %collective-permute-done.4.c2 = bf16[64,768]{1,0:T(8,128)(2,1)S(1)} collective-permute-done((bf16[64,768]{1,0:T(8,128)(2,1)S(1)}, bf16[64,768]{1,0:T(8,128)(2,1)S(1)}, u32[]{:S(2)}, u32[]{:S(2)}) %collective-permute-start.4) | collective-permute-done | bytes 98336 | tf_op jit(solution)/shard_map/ppermute | solution.py:236
  46.7 1.0 collective-permute-done.5.c3
  48.5 1.6 %collective-permute-start.9 = (bf16[256,768]{1,0:T(8,128)(2,1)S(1)}, bf16[256,768]{1,0:T(8,128)(2,1)S(1)}, u32[]{:S(2)}, u32[]{:S(2)}) collective-permute-start(bf16[256,768]{1,0:T(8,128)(2,1)S(1)} %get-tuple-element.29.refs_0_), channel_id=1, source_target_pairs={{0,8},{8,16},{16,24},{24,0},{1,9},{9,17},{17,25},{25,1},{2,10},{10... | collective-permute-start | bytes 1179656 | tf_op jit(solution)/shard_map/ppermute | solution.py:236
  50.1 1.4 %collective-permute-start.10 = (bf16[256,768]{1,0:T(8,128)(2,1)S(1)}, bf16[256,768]{1,0:T(8,128)(2,1)}, u32[]{:S(2)}, u32[]{:S(2)}) collective-permute-start(bf16[256,768]{1,0:T(8,128)(2,1)S(1)} %get-tuple-element.29.refs_0_), channel_id=1, source_target_pairs={{0,24},{8,0},{16,8},{24,16},{1,25},{9,1},{17,9},{25,17},{2,26},{10... | collective-permute-start | bytes 1179656 | tf_op jit(solution)/shard_map/ppermute | solution.py:236
  51.5 2.9 %collective-permute-start.6 = (s16[1,208,128]{2,1,0:T(8,128)(2,1)S(1)}, s16[1,208,128]{2,1,0:T(8,128)(2,1)S(1)}, u32[]{:S(2)}, u32[]{:S(2)}) collective-permute-start(s16[1,208,128]{2,1,0:T(8,128)(2,1)S(1)} %get-tuple-element.22.own), channel_id=1, source_target_pairs={{0,64},{64,128},{128,192},{192,0},{1,65},{65,129},{129,193},{193,1... | collective-permute-start | bytes 159752 | tf_op jit(solution)/shard_map/ppermute | solution.py:236
  54.5 4.2 %collective-permute-start.7 = (s16[1,208,128]{2,1,0:T(8,128)(2,1)S(1)}, s16[1,208,128]{2,1,0:T(8,128)(2,1)S(1)}, u32[]{:S(2)}, u32[]{:S(2)}) collective-permute-start(s16[1,208,128]{2,1,0:T(8,128)(2,1)S(1)} %get-tuple-element.22.own), channel_id=1, source_target_pairs={{0,128},{64,192},{128,0},{192,64},{1,129},{65,193},{129,1},{193,65... | collective-permute-start | bytes 159752 | tf_op jit(solution)/shard_map/ppermute | solution.py:236
  58.7 2.4 %collective-permute-start.8 = (s16[1,208,128]{2,1,0:T(8,128)(2,1)S(1)}, s16[1,208,128]{2,1,0:T(8,128)(2,1)S(1)}, u32[]{:S(2)}, u32[]{:S(2)}) collective-permute-start(s16[1,208,128]{2,1,0:T(8,128)(2,1)S(1)} %get-tuple-element.22.own), channel_id=1, source_target_pairs={{0,192},{64,0},{128,64},{192,128},{1,193},{65,1},{129,65},{193,129... | collective-permute-start | bytes 159752 | tf_op jit(solution)/shard_map/ppermute | solution.py:236
  61.8 1.3 collective-permute-done.8.three
  63.9 1.7 %shard_map.61 = (f32[32,768]{1,0:T(8,128)S(1)}, s16[32,208,128]{2,1,0:T(8,128)(2,1)}) custom-call(s16[1,208,128]{2,1,0:T(8,128)(2,1)S(1)} %get-tuple-element.22.own, s16[1,208,128]{2,1,0:T(8,128)(2,1)S(1)} %collective-permute-done.6.one, s16[1,208,128]{2,1,0:T(8,128)(2,1)S(1)} %collective-permute-done.7.two, s16[1,208,128]{2,1,0:T(8,128)(2,1)S(1)} %collective-permute-done.8.three), custom_call_target="tpu_custom_call" | custom-call | flops 1048576 | bytes 2097152 | tf_op jit(solution)/shard_map/pallas_call | solution.py:215
  65.6 6.0 %all-to-all-start.1 = ((s16[32,208,128]{2,1,0:T(8,128)(2,1)}), s16[32,208,128]{2,1,0:T(8,128)(2,1)S(1)}, u32[]{:S(2)}, u32[]{:S(2)}) async-start(s16[32,208,128]{2,1,0:T(8,128)(2,1)} %get-tuple-element.26), calls=%async_computation.1 | async-start | bytes 3407872 | tf_op jit(solution)/shard_map/all_to_all | solution.py:288
  71.6 2.8 %collective-permute-start.11 = (bf16[256,768]{1,0:T(8,128)(2,1)}, bf16[256,768]{1,0:T(8,128)(2,1)S(1)}, u32[]{:S(2)}, u32[]{:S(2)}) collective-permute-start(bf16[256,768]{1,0:T(8,128)(2,1)} %copy-done.4), channel_id=1, source_target_pairs={{0,16},{8,24},{16,0},{24,8},{1,17},{9,25},{17,1},{25,9},{2,18},{10... | collective-permute-start | bytes 1179656 | tf_op jit(solution)/shard_map/ppermute | solution.py:236
  74.4 26.2 %collective-permute-done.11.refs_2_ = bf16[256,768]{1,0:T(8,128)(2,1)S(1)} collective-permute-done((bf16[256,768]{1,0:T(8,128)(2,1)}, bf16[256,768]{1,0:T(8,128)(2,1)S(1)}, u32[]{:S(2)}, u32[]{:S(2)}) %collective-permute-start.11) | collective-permute-done | bytes 393248 | tf_op jit(solution)/shard_map/ppermute | solution.py:236
  100.6 2.3 %collective-permute-start.12 = (bf16[256,768]{1,0:T(8,128)(2,1)}, bf16[256,768]{1,0:T(8,128)(2,1)S(1)}, u32[]{:S(2)}, u32[]{:S(2)}) collective-permute-start(bf16[256,768]{1,0:T(8,128)(2,1)} %copy-done.4), channel_id=1, source_target_pairs={{0,32},{32,0},{1,33},{33,1},{2,34},{34,2},{3,35},{35,3},{4,36},{36... | collective-permute-start | bytes 1179656 | tf_op jit(solution)/shard_map/ppermute | solution.py:232
  104.5 1.1 collective-permute-done.13.refs_5_
  106.2 1.0 copy-done.5
  107.2 1.0 copy-done.7
  108.2 5.2 %shard_map.62 = (f32[1,1024]{1,0:T(1,128)}, bf16[768,1024]{1,0:T(8,128)(2,1)S(1)}) custom-call(f32[1,1024]{1,0:T(1,128)S(1)} %bitcast.8, bf16[1024,768]{1,0:T(8,128)(2,1)S(1)} %copy-done.2, bf16[256,768]{1,0:T(8,128)(2,1)S(1)} %copy-done.5, bf16[256,768]{1,0:T(8,128)(2,1)S(1)} %copy-done.7, bf16[256,768]{1,0:T(8,128)(2,1)S(1)} %collective-permute-done.11.refs_2_, ...), custom_call_target="tpu_custom_call" | custom-call | flops 3221225472 | bytes 5242880 | tf_op jit(solution)/shard_map/pallas_call | solution.py:215
  113.3 1.2 copy-done.8
  115.0 3.2 %collective-permute-done.16 = f32[32,768]{1,0:T(8,128)S(1)} collective-permute-done((f32[32,768]{1,0:T(8,128)S(1)}, f32[32,768]{1,0:T(8,128)S(1)}, u32[]{:S(2)}, u32[]{:S(2)}) %collective-permute-start.16) | collective-permute-done | bytes 98336 | tf_op jit(solution)/shard_map/ppermute | solution.py:232
  119.0 1.4 %copy-done.9 = bf16[768,1024]{1,0:T(8,128)(2,1)S(1)} copy-done((bf16[768,1024]{1,0:T(8,128)(2,1)S(1)}, bf16[768,1024]{1,0:T(8,128)(2,1)}, u32[]{:S(2)}) %copy-start.9) | copy-done | bytes 1572888
  120.4 3.5 %shard_map.63.least_ref = f32[8,1024]{1,0:T(8,128)S(1)} custom-call(bf16[768,1024]{1,0:T(8,128)(2,1)S(1)} %copy-done.9, s16[32,208,128]{2,1,0:T(8,128)(2,1)S(1)} %all-to-all-done.1.coded_ref, f32[1,1024]{1,0:T(1,128)S(1)} %bitcast.9, f32[8,1024]{1,0:T(8,128)S(1)} %broadcast_in_dim.3.least_ref), custom_call_target="tpu_custom_call" | custom-call | flops 3221225472 | bytes 3145728 | tf_op jit(solution)/shard_map/pallas_call | solution.py:215
  123.9 5.6 %shard_map.64 = f32[1,1024]{1,0:T(1,128)} custom-call(bf16[768,1024]{1,0:T(8,128)(2,1)S(1)} %copy-done.10, s16[32,208,128]{2,1,0:T(8,128)(2,1)} %collective-permute-done.17.coded_ref, f32[1,1024]{1,0:T(1,128)S(1)} %bitcast.10, f32[8,1024]{1,0:T(8,128)S(1)} %shard_map.63.least_ref), custom_call_target="tpu_custom_call" | custom-call | flops 3221225472 | bytes 3145728 | tf_op jit(solution)/shard_map/pallas_call | solution.py:215
  (43 shorter events, 6.9 us)
Async XLA Ops:
  0.6 18.2 %copy-start = (bf16[64,768]{1,0:T(8,128)(2,1)S(1)}, bf16[64,768]{1,0:T(8,128)(2,1)}, u32[]{:S(2)}) copy-start(bf16[64,768]{1,0:T(8,128)(2,1)} %param.4) | copy-start | bytes 294916
  0.6 7.4 %collective-permute-start.1 = (bf16[1024,768]{1,0:T(8,128)(2,1)}, bf16[1024,768]{1,0:T(8,128)(2,1)S(1)}, u32[]{:S(2)}, u32[]{:S(2)}) collective-permute-start(bf16[1024,768]{1,0:T(8,128)(2,1)} %rows_ref.1), channel_id=1, source_target_pairs={{0,32},{32,0},{1,33},{33,1},{2,34},{34,2},{3,35},{35,3},{4,36},{36... | collective-permute-start | bytes 4718600 | tf_op jit(solution)/shard_map/ppermute | solution.py:232
  4.0 4.0 %collective-permute-start = (s32[1,1024]{1,0:T(1,128)}, s32[1,1024]{1,0:T(1,128)S(1)}, u32[]{:S(2)}, u32[]{:S(2)}) collective-permute-start(s32[1,1024]{1,0:T(1,128)} %bitcast.5), channel_id=1, source_target_pairs={{0,32},{32,0},{1,33},{33,1},{2,34},{34,2},{3,35},{35,3},{4,36},{36... | collective-permute-start | bytes 12296 | tf_op jit(solution)/shard_map/ppermute | solution.py:232
  4.1 1.4 %copy-start.1 = (bf16[1024,768]{1,0:T(8,128)(2,1)S(1)}, bf16[1024,768]{1,0:T(8,128)(2,1)}, u32[]{:S(2)}) copy-start(bf16[1024,768]{1,0:T(8,128)(2,1)} %rows_ref.1) | copy-start | bytes 4718596
  5.5 0.7 copy-start.3
  12.2 35.6 %all-to-all-start = ((s16[32,208,128]{2,1,0:T(8,128)(2,1)}), s16[32,208,128]{2,1,0:T(8,128)(2,1)S(1)}, u32[]{:S(2)}, u32[]{:S(2)}) async-start(s16[32,208,128]{2,1,0:T(8,128)(2,1)} %shard_map.59), calls=%async_computation | async-start | bytes 3407872 | tf_op jit(solution)/shard_map/all_to_all | solution.py:271
  18.9 21.2 %collective-permute-start.2 = (bf16[32,768]{1,0:T(8,128)(2,1)S(1)}, bf16[32,768]{1,0:T(8,128)(2,1)S(1)}, u32[]{:S(2)}, u32[]{:S(2)}) collective-permute-start(bf16[32,768]{1,0:T(8,128)(2,1)S(1)} %constant_dynamic-slice_fusion), channel_id=1, source_target_pairs={{0,1},{1,0},{2,3},{3,2},{4,5},{5,4},{6,7},{7,6},{8,9},{9,8},{10,11... | collective-permute-start | bytes 147464 | tf_op jit(solution)/shard_map/ppermute | solution.py:232
  40.1 4.8 %collective-permute-start.3 = (bf16[64,768]{1,0:T(8,128)(2,1)S(1)}, bf16[64,768]{1,0:T(8,128)(2,1)S(1)}, u32[]{:S(2)}, u32[]{:S(2)}) collective-permute-start(bf16[64,768]{1,0:T(8,128)(2,1)S(1)} %pad_maximum_fusion.1.c0), channel_id=1, source_target_pairs={{0,2},{2,4},{4,6},{6,0},{1,3},{3,5},{5,7},{7,1},{8,10},{10,12},{12... | collective-permute-start | bytes 294920 | tf_op jit(solution)/shard_map/ppermute | solution.py:236
  41.4 5.4 %collective-permute-start.4 = (bf16[64,768]{1,0:T(8,128)(2,1)S(1)}, bf16[64,768]{1,0:T(8,128)(2,1)S(1)}, u32[]{:S(2)}, u32[]{:S(2)}) collective-permute-start(bf16[64,768]{1,0:T(8,128)(2,1)S(1)} %pad_maximum_fusion.1.c0), channel_id=1, source_target_pairs={{0,4},{2,6},{4,0},{6,2},{1,5},{3,7},{5,1},{7,3},{8,12},{10,14},{12... | collective-permute-start | bytes 294920 | tf_op jit(solution)/shard_map/ppermute | solution.py:236
  43.6 4.2 %collective-permute-start.5 = (bf16[64,768]{1,0:T(8,128)(2,1)S(1)}, bf16[64,768]{1,0:T(8,128)(2,1)S(1)}, u32[]{:S(2)}, u32[]{:S(2)}) collective-permute-start(bf16[64,768]{1,0:T(8,128)(2,1)S(1)} %pad_maximum_fusion.1.c0), channel_id=1, source_target_pairs={{0,6},{2,0},{4,2},{6,4},{1,7},{3,1},{5,3},{7,5},{8,14},{10,8},{12,... | collective-permute-start | bytes 294920 | tf_op jit(solution)/shard_map/ppermute | solution.py:236
  48.5 14.6 %copy-start.4 = (bf16[256,768]{1,0:T(8,128)(2,1)}, bf16[256,768]{1,0:T(8,128)(2,1)S(1)}, u32[]{:S(2)}) copy-start(bf16[256,768]{1,0:T(8,128)(2,1)S(1)} %get-tuple-element.29.refs_0_) | copy-start | bytes 1179652
  48.5 14.6 %collective-permute-start.9 = (bf16[256,768]{1,0:T(8,128)(2,1)S(1)}, bf16[256,768]{1,0:T(8,128)(2,1)S(1)}, u32[]{:S(2)}, u32[]{:S(2)}) collective-permute-start(bf16[256,768]{1,0:T(8,128)(2,1)S(1)} %get-tuple-element.29.refs_0_), channel_id=1, source_target_pairs={{0,8},{8,16},{16,24},{24,0},{1,9},{9,17},{17,25},{25,1},{2,10},{10... | collective-permute-start | bytes 1179656 | tf_op jit(solution)/shard_map/ppermute | solution.py:236
  50.1 13.8 %collective-permute-start.10 = (bf16[256,768]{1,0:T(8,128)(2,1)S(1)}, bf16[256,768]{1,0:T(8,128)(2,1)}, u32[]{:S(2)}, u32[]{:S(2)}) collective-permute-start(bf16[256,768]{1,0:T(8,128)(2,1)S(1)} %get-tuple-element.29.refs_0_), channel_id=1, source_target_pairs={{0,24},{8,0},{16,8},{24,16},{1,25},{9,1},{17,9},{25,17},{2,26},{10... | collective-permute-start | bytes 1179656 | tf_op jit(solution)/shard_map/ppermute | solution.py:236
  51.5 9.5 %collective-permute-start.6 = (s16[1,208,128]{2,1,0:T(8,128)(2,1)S(1)}, s16[1,208,128]{2,1,0:T(8,128)(2,1)S(1)}, u32[]{:S(2)}, u32[]{:S(2)}) collective-permute-start(s16[1,208,128]{2,1,0:T(8,128)(2,1)S(1)} %get-tuple-element.22.own), channel_id=1, source_target_pairs={{0,64},{64,128},{128,192},{192,0},{1,65},{65,129},{129,193},{193,1... | collective-permute-start | bytes 159752 | tf_op jit(solution)/shard_map/ppermute | solution.py:236
  54.5 7.4 %collective-permute-start.7 = (s16[1,208,128]{2,1,0:T(8,128)(2,1)S(1)}, s16[1,208,128]{2,1,0:T(8,128)(2,1)S(1)}, u32[]{:S(2)}, u32[]{:S(2)}) collective-permute-start(s16[1,208,128]{2,1,0:T(8,128)(2,1)S(1)} %get-tuple-element.22.own), channel_id=1, source_target_pairs={{0,128},{64,192},{128,0},{192,64},{1,129},{65,193},{129,1},{193,65... | collective-permute-start | bytes 159752 | tf_op jit(solution)/shard_map/ppermute | solution.py:236
  58.7 4.4 %collective-permute-start.8 = (s16[1,208,128]{2,1,0:T(8,128)(2,1)S(1)}, s16[1,208,128]{2,1,0:T(8,128)(2,1)S(1)}, u32[]{:S(2)}, u32[]{:S(2)}) collective-permute-start(s16[1,208,128]{2,1,0:T(8,128)(2,1)S(1)} %get-tuple-element.22.own), channel_id=1, source_target_pairs={{0,192},{64,0},{128,64},{192,128},{1,193},{65,1},{129,65},{193,129... | collective-permute-start | bytes 159752 | tf_op jit(solution)/shard_map/ppermute | solution.py:236
  63.1 0.8 copy-start.6
  65.6 37.8 %copy-start.2 = (bf16[1024,768]{1,0:T(8,128)(2,1)S(1)}, bf16[1024,768]{1,0:T(8,128)(2,1)}, u32[]{:S(2)}) copy-start(bf16[1024,768]{1,0:T(8,128)(2,1)} %rows_ref.1) | copy-start | bytes 4718596
  65.6 48.9 %all-to-all-start.1 = ((s16[32,208,128]{2,1,0:T(8,128)(2,1)}), s16[32,208,128]{2,1,0:T(8,128)(2,1)S(1)}, u32[]{:S(2)}, u32[]{:S(2)}) async-start(s16[32,208,128]{2,1,0:T(8,128)(2,1)} %get-tuple-element.26), calls=%async_computation.1 | async-start | bytes 3407872 | tf_op jit(solution)/shard_map/all_to_all | solution.py:288
  71.6 29.0 %collective-permute-start.11 = (bf16[256,768]{1,0:T(8,128)(2,1)}, bf16[256,768]{1,0:T(8,128)(2,1)S(1)}, u32[]{:S(2)}, u32[]{:S(2)}) collective-permute-start(bf16[256,768]{1,0:T(8,128)(2,1)} %copy-done.4), channel_id=1, source_target_pairs={{0,16},{8,24},{16,0},{24,8},{1,17},{9,25},{17,1},{25,9},{2,18},{10... | collective-permute-start | bytes 1179656 | tf_op jit(solution)/shard_map/ppermute | solution.py:236
  100.6 3.8 %collective-permute-start.12 = (bf16[256,768]{1,0:T(8,128)(2,1)}, bf16[256,768]{1,0:T(8,128)(2,1)S(1)}, u32[]{:S(2)}, u32[]{:S(2)}) collective-permute-start(bf16[256,768]{1,0:T(8,128)(2,1)} %copy-done.4), channel_id=1, source_target_pairs={{0,32},{32,0},{1,33},{33,1},{2,34},{34,2},{3,35},{35,3},{4,36},{36... | collective-permute-start | bytes 1179656 | tf_op jit(solution)/shard_map/ppermute | solution.py:232
  102.9 2.7 %collective-permute-start.13 = (bf16[256,768]{1,0:T(8,128)(2,1)}, bf16[256,768]{1,0:T(8,128)(2,1)S(1)}, u32[]{:S(2)}, u32[]{:S(2)}) collective-permute-start(bf16[256,768]{1,0:T(8,128)(2,1)} %copy-done.6), channel_id=1, source_target_pairs={{0,32},{32,0},{1,33},{33,1},{2,34},{34,2},{3,35},{35,3},{4,36},{36... | collective-permute-start | bytes 1179656 | tf_op jit(solution)/shard_map/ppermute | solution.py:232
  102.9 2.7 %collective-permute-start.14 = (bf16[256,768]{1,0:T(8,128)(2,1)S(1)}, bf16[256,768]{1,0:T(8,128)(2,1)S(1)}, u32[]{:S(2)}, u32[]{:S(2)}) collective-permute-start(bf16[256,768]{1,0:T(8,128)(2,1)S(1)} %collective-permute-done.11.refs_2_), channel_id=1, source_target_pairs={{0,32},{32,0},{1,33},{33,1},{2,34},{34,2},{3,35},{35,3},{4,36},{36... | collective-permute-start | bytes 1179656 | tf_op jit(solution)/shard_map/ppermute | solution.py:232
  103.4 2.7 %collective-permute-start.15 = (bf16[256,768]{1,0:T(8,128)(2,1)}, bf16[256,768]{1,0:T(8,128)(2,1)S(1)}, u32[]{:S(2)}, u32[]{:S(2)}) collective-permute-start(bf16[256,768]{1,0:T(8,128)(2,1)} %collective-permute-done.10.refs_3_), channel_id=1, source_target_pairs={{0,32},{32,0},{1,33},{33,1},{2,34},{34,2},{3,35},{35,3},{4,36},{36... | collective-permute-start | bytes 1179656 | tf_op jit(solution)/shard_map/ppermute | solution.py:232
  106.2 1.0 copy-start.5
  107.2 1.0 copy-start.7
  113.3 1.2 copy-start.8
  114.5 9.4 %collective-permute-start.17 = (s16[32,208,128]{2,1,0:T(8,128)(2,1)S(1)}, s16[32,208,128]{2,1,0:T(8,128)(2,1)}, u32[]{:S(2)}, u32[]{:S(2)}) collective-permute-start(s16[32,208,128]{2,1,0:T(8,128)(2,1)S(1)} %all-to-all-done.1.coded_ref), channel_id=1, source_target_pairs={{0,32},{32,0},{1,33},{33,1},{2,34},{34,2},{3,35},{35,3},{4,36},{36... | collective-permute-start | bytes 5111816 | tf_op jit(solution)/shard_map/ppermute | solution.py:232
  114.9 3.4 %collective-permute-start.16 = (f32[32,768]{1,0:T(8,128)S(1)}, f32[32,768]{1,0:T(8,128)S(1)}, u32[]{:S(2)}, u32[]{:S(2)}) collective-permute-start(f32[32,768]{1,0:T(8,128)S(1)} %get-tuple-element.34), channel_id=1, source_target_pairs={{0,32},{32,0},{1,33},{33,1},{2,34},{34,2},{3,35},{35,3},{4,36},{36... | collective-permute-start | bytes 294920 | tf_op jit(solution)/shard_map/ppermute | solution.py:232
  119.0 1.4 %copy-start.9 = (bf16[768,1024]{1,0:T(8,128)(2,1)S(1)}, bf16[768,1024]{1,0:T(8,128)(2,1)}, u32[]{:S(2)}) copy-start(bf16[768,1024]{1,0:T(8,128)(2,1)} %copy-done.8) | copy-start | bytes 4718596
  120.4 3.6 %copy-start.10 = (bf16[768,1024]{1,0:T(8,128)(2,1)S(1)}, bf16[768,1024]{1,0:T(8,128)(2,1)}, u32[]{:S(2)}) copy-start(bf16[768,1024]{1,0:T(8,128)(2,1)} %copy-done.8) | copy-start | bytes 4718596

commit v3 on v2

--- a/solution.py
+++ b/solution.py
@@ -268,6 +268,7 @@
         base, labels, other_labels, sums, other_rows,
         flops=2 * 1024 * n * D, moved=6 << 20, smem=1,
     )
+    sums, *current = lax.optimization_barrier((sums, *current))
     sums = lax.all_to_all(sums, SHARD, 0, 0)
     group, current = call(
         group_kernel,
@@ -275,9 +276,8 @@
         sums, *current,
         flops=1 << 22, moved=2 << 20,
     )
-    current = around(current, "y")
-    groups, current[1], current[3] = lax.optimization_barrier(
-        (around(group, "zh"), current[1], current[3])
+    groups, current = lax.optimization_barrier(
+        (around(group, "zh"), around(current, "y"))
     )
     refined, coded = call(
         refine_kernel,
@@ -287,8 +287,8 @@
     )
     new_own = lax.all_to_all(coded, SHARD, 0, 0)
 
-    current = after(coded, current)
-    current = current + tuple(swap(part, "core") for part in current)
+    current = list(after(coded, current))
+    current = current + list(swap(part, "core") for part in current)
     old_min, turned = call(
         old_kernel,
         (shape((1, n), f32), shape((D, n), bf16)),
@@ -305,7 +305,9 @@
         ]
     )
 
-    (new_own,) = after(turned, (new_own,))
+    new_own, turned, refined_centers = lax.optimization_barrier(
+        (new_own, turned, refined_centers)
+    )
     new_other = swap(new_own, "core")
     least = jnp.full((8, n), jnp.inf, f32)
     for coded, result in ((new_own, 8), (new_other, 1)):

time: 130 us -> 111 us (0.85)
  waiting for transfers between devices: 56.9 us -> 17 us
  blocking collectives: 0 us -> 29.4 us
  starting transfers between devices: 40.5 us -> 32.1 us
  Pallas kernels: 22.8 us -> 20.7 us
    all_to_all x0 -> x1, blocking collectives: none -> 29.4 us  [on_device(): sums = lax.all_to_all(sums, SHARD, 0, 0)]
    ppermute x9, waiting for transfers between devices: 31.5 us -> 6.52 us  [around(): lax.ppermute(part, axis, ring(axis, 4, k))]
    ppermute x9, waiting for transfers between devices: 25.5 us -> 0.94 us  [swap(): return lax.ppermute(value, axis, [(0, 1), (1, 0)])]
    all_to_all x1, waiting for transfers between devices: 0.01 us -> 9.49 us  [on_device(): new_own = lax.all_to_all(coded, SHARD, 0, 0)]
    all_to_all x1 -> x0, starting transfers between devices: 6.67 us -> none  [on_device(): sums = lax.all_to_all(sums, SHARD, 0, 0)]
    ppermute x9, starting transfers between devices: 19.8 us -> 17.5 us  [around(): lax.ppermute(part, axis, ring(axis, 4, k))]
    pallas_call x7, Pallas kernels: 22.8 us -> 20.7 us  [call(): pl.pallas_call(kernel, out_shape=out_shape, in_specs=specs, out_specs=tup...]
    unnamed x22 -> x24, local copies, waits for them, and re-layouts: 7.44 us -> 8.41 us
  transfers between devices with their start and end apart: 20 -> 19, of which waited for: 11 -> 6; matrix products, arithmetic and copies ran while one was open for 1% -> 2% of each run, Pallas kernels for 8% -> 13%
where the time goes in v3:
time: 111 us; the launch traced here: 110 us
  starting transfers between devices  32.1 us (29%)
  blocking collectives  29.4 us (26%)
  Pallas kernels  20.7 us (19%)
  waiting for transfers between devices  17 us (15%)
  local copies, waits for them, and re-layouts  8.42 us (8%)
  other arithmetic  1.98 us (2%)
    all_to_all x1, blocking collectives, on_device(): sums = lax.all_to_all(sums, SHARD, 0, 0)  29.4 us
    pallas_call x7, Pallas kernels, call(): pl.pallas_call(kernel, out_shape=out_shape, in_specs=specs, out_specs=tup...  20.7 us
    ppermute x9, starting transfers between devices, around(): lax.ppermute(part, axis, ring(axis, 4, k))  17.5 us
    all_to_all x1, waiting for transfers between devices, on_device(): new_own = lax.all_to_all(coded, SHARD, 0, 0)  9.49 us
    unnamed x24, local copies, waits for them, and re-layouts  8.41 us
    ppermute x9, starting transfers between devices, swap(): return lax.ppermute(value, axis, [(0, 1), (1, 0)])  7.33 us
    all_to_all x1, starting transfers between devices, on_device(): new_own = lax.all_to_all(coded, SHARD, 0, 0)  7.19 us
    ppermute x9, waiting for transfers between devices, around(): lax.ppermute(part, axis, ring(axis, 4, k))  6.52 us
  transfers between devices with their start and end apart: 19, of which 6 were waited for; matrix products, arithmetic and copies ran while one was open for 2% of the time, Pallas kernels for 13%

profile of v3, /device:TPU:1, one launch (start us, length us, event | category | flops | bytes accessed | tf_op | source)
XLA Modules:
  0.0 110.3 jit_solution(4703065586830758856)
XLA Ops:
  0.6 3.3 %collective-permute-start.1 = (bf16[1024,768]{1,0:T(8,128)(2,1)}, bf16[1024,768]{1,0:T(8,128)(2,1)S(1)}, u32[]{:S(2)}, u32[]{:S(2)}) collective-permute-start(bf16[1024,768]{1,0:T(8,128)(2,1)} %rows_ref.1), channel_id=1, source_target_pairs={{0,32},{32,0},{1,33},{33,1},{2,34},{34,2},{3,35},{35,3},{4,36},{36... | collective-permute-start | bytes 4718600 | tf_op jit(solution)/shard_map/ppermute | solution.py:232
  4.2 1.4 %copy-done.1 = bf16[1024,768]{1,0:T(8,128)(2,1)S(1)} copy-done((bf16[1024,768]{1,0:T(8,128)(2,1)S(1)}, bf16[1024,768]{1,0:T(8,128)(2,1)}, u32[]{:S(2)}) %copy-start.1) | copy-done | bytes 1572888
  6.3 1.8 %shard_map.58.own_sums = f32[1024,768]{1,0:T(8,128)S(1)} custom-call(s32[1]{0:T(128)} %bitcast.1.base_ref, s32[1,1024]{1,0:T(1,128)S(1)} %bitcast.6, bf16[1024,768]{1,0:T(8,128)(2,1)S(1)} %copy-done.1), custom_call_target="tpu_custom_call" | custom-call | flops 1610612736 | bytes 5242880 | tf_op jit(solution)/shard_map/pallas_call | solution.py:215
  8.1 1.2 %collective-permute-start.3 = (bf16[64,768]{1,0:T(8,128)(2,1)S(1)}, bf16[64,768]{1,0:T(8,128)(2,1)S(1)}, u32[]{:S(2)}, u32[]{:S(2)}) collective-permute-start(bf16[64,768]{1,0:T(8,128)(2,1)S(1)} %pad_maximum_fusion.1.c0), channel_id=1, source_target_pairs={{0,2},{2,4},{4,6},{6,0},{1,3},{3,5},{5,7},{7,1},{8,10},{10,12},{12... | collective-permute-start | bytes 294920 | tf_op jit(solution)/shard_map/ppermute | solution.py:236
  9.3 2.5 %collective-permute-start.4 = (bf16[64,768]{1,0:T(8,128)(2,1)S(1)}, bf16[64,768]{1,0:T(8,128)(2,1)S(1)}, u32[]{:S(2)}, u32[]{:S(2)}) collective-permute-start(bf16[64,768]{1,0:T(8,128)(2,1)S(1)} %pad_maximum_fusion.1.c0), channel_id=1, source_target_pairs={{0,4},{2,6},{4,0},{6,2},{1,5},{3,7},{5,1},{7,3},{8,12},{10,14},{12... | collective-permute-start | bytes 294920 | tf_op jit(solution)/shard_map/ppermute | solution.py:236
  11.7 1.2 %collective-permute-start.5 = (bf16[64,768]{1,0:T(8,128)(2,1)S(1)}, bf16[64,768]{1,0:T(8,128)(2,1)S(1)}, u32[]{:S(2)}, u32[]{:S(2)}) collective-permute-start(bf16[64,768]{1,0:T(8,128)(2,1)S(1)} %pad_maximum_fusion.1.c0), channel_id=1, source_target_pairs={{0,6},{2,0},{4,2},{6,4},{1,7},{3,1},{5,3},{7,5},{8,14},{10,8},{12,... | collective-permute-start | bytes 294920 | tf_op jit(solution)/shard_map/ppermute | solution.py:236
  12.9 3.0 %shard_map.59 = s16[32,208,128]{2,1,0:T(8,128)(2,1)S(1)} custom-call(s32[1]{0:T(128)} %bitcast.1.base_ref, s32[1,1024]{1,0:T(1,128)S(1)} %bitcast.7, s32[1,1024]{1,0:T(1,128)S(1)} %collective-permute-done.labels, f32[1024,768]{1,0:T(8,128)S(1)} %shard_map.58.own_sums, bf16[1024,768]{1,0:T(8,128)(2,1)S(1)} %collective-permute-done.1.rows), custom_call_target="tpu_custom_call" | custom-call | flops 1610612736 | bytes 6291456 | tf_op jit(solution)/shard_map/pallas_call | solution.py:215
  16.3 29.4 %all_to_all.10.in_ref = s16[32,208,128]{2,1,0:T(8,128)(2,1)S(1)} all-to-all(s16[32,208,128]{2,1,0:T(8,128)(2,1)S(1)} %shard_map.59), channel_id=1, replica_groups=mesh['zh'=4,'core'=2,'y'=4,'x'=4,'zl'=2] {'y','x','zl'}, dimensions={0} | all-to-all | bytes 3407872 | tf_op jit(solution)/shard_map/all_to_all | solution.py:272
  46.6 1.7 %collective-permute-start.10 = (bf16[256,768]{1,0:T(8,128)(2,1)S(1)}, bf16[256,768]{1,0:T(8,128)(2,1)S(1)}, u32[]{:S(2)}, u32[]{:S(2)}) collective-permute-start(bf16[256,768]{1,0:T(8,128)(2,1)S(1)} %get-tuple-element.45.refs_0_), channel_id=1, source_target_pairs={{0,16},{8,24},{16,0},{24,8},{1,17},{9,25},{17,1},{25,9},{2,18},{10... | collective-permute-start | bytes 1179656 | tf_op jit(solution)/shard_map/ppermute | solution.py:236
  48.2 1.0 collective-permute-start.11
  49.2 3.0 %collective-permute-start.6 = (s16[1,208,128]{2,1,0:T(8,128)(2,1)S(1)}, s16[1,208,128]{2,1,0:T(8,128)(2,1)S(1)}, u32[]{:S(2)}, u32[]{:S(2)}) collective-permute-start(s16[1,208,128]{2,1,0:T(8,128)(2,1)S(1)} %get-tuple-element.36.own), channel_id=1, source_target_pairs={{0,64},{64,128},{128,192},{192,0},{1,65},{65,129},{129,193},{193,1... | collective-permute-start | bytes 159752 | tf_op jit(solution)/shard_map/ppermute | solution.py:236
  52.2 4.7 %collective-permute-start.7 = (s16[1,208,128]{2,1,0:T(8,128)(2,1)S(1)}, s16[1,208,128]{2,1,0:T(8,128)(2,1)S(1)}, u32[]{:S(2)}, u32[]{:S(2)}) collective-permute-start(s16[1,208,128]{2,1,0:T(8,128)(2,1)S(1)} %get-tuple-element.36.own), channel_id=1, source_target_pairs={{0,128},{64,192},{128,0},{192,64},{1,129},{65,193},{129,1},{193,65... | collective-permute-start | bytes 159752 | tf_op jit(solution)/shard_map/ppermute | solution.py:236
  56.9 2.4 %collective-permute-start.8 = (s16[1,208,128]{2,1,0:T(8,128)(2,1)S(1)}, s16[1,208,128]{2,1,0:T(8,128)(2,1)S(1)}, u32[]{:S(2)}, u32[]{:S(2)}) collective-permute-start(s16[1,208,128]{2,1,0:T(8,128)(2,1)S(1)} %get-tuple-element.36.own), channel_id=1, source_target_pairs={{0,192},{64,0},{128,64},{192,128},{1,193},{65,1},{129,65},{193,129... | collective-permute-start | bytes 159752 | tf_op jit(solution)/shard_map/ppermute | solution.py:236
  59.2 2.4 %collective-permute-done.8.three = s16[1,208,128]{2,1,0:T(8,128)(2,1)S(1)} collective-permute-done((s16[1,208,128]{2,1,0:T(8,128)(2,1)S(1)}, s16[1,208,128]{2,1,0:T(8,128)(2,1)S(1)}, u32[]{:S(2)}, u32[]{:S(2)}) %collective-permute-start.8) | collective-permute-done | bytes 53280 | tf_op jit(solution)/shard_map/ppermute | solution.py:236
  61.6 1.5 %collective-permute-done.10.refs_2_ = bf16[256,768]{1,0:T(8,128)(2,1)S(1)} collective-permute-done((bf16[256,768]{1,0:T(8,128)(2,1)S(1)}, bf16[256,768]{1,0:T(8,128)(2,1)S(1)}, u32[]{:S(2)}, u32[]{:S(2)}) %collective-permute-start.10) | collective-permute-done | bytes 393248 | tf_op jit(solution)/shard_map/ppermute | solution.py:236
  63.1 0.8 copy-done.8
  63.8 2.3 %collective-permute-done.11.refs_3_ = bf16[256,768]{1,0:T(8,128)(2,1)} collective-permute-done((bf16[256,768]{1,0:T(8,128)(2,1)S(1)}, bf16[256,768]{1,0:T(8,128)(2,1)}, u32[]{:S(2)}, u32[]{:S(2)}) %collective-permute-start.11) | collective-permute-done | bytes 393248 | tf_op jit(solution)/shard_map/ppermute | solution.py:236
  66.1 1.7 %shard_map.61 = (f32[32,768]{1,0:T(8,128)S(1)}, s16[32,208,128]{2,1,0:T(8,128)(2,1)}) custom-call(s16[1,208,128]{2,1,0:T(8,128)(2,1)S(1)} %get-tuple-element.36.own, s16[1,208,128]{2,1,0:T(8,128)(2,1)S(1)} %collective-permute-done.6.one, s16[1,208,128]{2,1,0:T(8,128)(2,1)S(1)} %collective-permute-done.7.two, s16[1,208,128]{2,1,0:T(8,128)(2,1)S(1)} %collective-permute-done.8.three), custom_call_target="tpu_custom_call" | custom-call | flops 1048576 | bytes 2097152 | tf_op jit(solution)/shard_map/pallas_call | solution.py:215
  67.9 7.2 %all-to-all-start.1 = ((s16[32,208,128]{2,1,0:T(8,128)(2,1)}), s16[32,208,128]{2,1,0:T(8,128)(2,1)S(1)}, u32[]{:S(2)}, u32[]{:S(2)}) async-start(s16[32,208,128]{2,1,0:T(8,128)(2,1)} %get-tuple-element.40), calls=%async_computation.1 | async-start | bytes 3407872 | tf_op jit(solution)/shard_map/all_to_all | solution.py:288
  75.1 0.9 collective-permute-start.12
  77.3 0.9 collective-permute-done.16
  78.3 0.9 broadcast_select_fusion.1
  79.9 1.0 copy-done.5
  80.9 1.0 copy-done.7
  81.9 1.0 copy-done.9
  82.9 5.6 %shard_map.62 = (f32[1,1024]{1,0:T(1,128)}, bf16[768,1024]{1,0:T(8,128)(2,1)S(1)}) custom-call(f32[1,1024]{1,0:T(1,128)S(1)} %bitcast.8, bf16[1024,768]{1,0:T(8,128)(2,1)S(1)} %copy-done.2, bf16[256,768]{1,0:T(8,128)(2,1)S(1)} %copy-done.5, bf16[256,768]{1,0:T(8,128)(2,1)S(1)} %copy-done.7, bf16[256,768]{1,0:T(8,128)(2,1)S(1)} %copy-done.9, ...), custom_call_target="tpu_custom_call" | custom-call | flops 3221225472 | bytes 5242880 | tf_op jit(solution)/shard_map/pallas_call | solution.py:215
  88.5 1.2 %copy-done.10 = bf16[768,1024]{1,0:T(8,128)(2,1)} copy-done((bf16[768,1024]{1,0:T(8,128)(2,1)}, bf16[768,1024]{1,0:T(8,128)(2,1)S(1)}, u32[]{:S(2)}) %copy-start.10) | copy-done | bytes 1572888
  89.7 9.5 %all-to-all-done.1.coded_ref = s16[32,208,128]{2,1,0:T(8,128)(2,1)S(1)} async-done(((s16[32,208,128]{2,1,0:T(8,128)(2,1)}), s16[32,208,128]{2,1,0:T(8,128)(2,1)S(1)}, u32[]{:S(2)}, u32[]{:S(2)}) %all-to-all-start.1) | async-done | bytes 1703968 | tf_op jit(solution)/shard_map/all_to_all | solution.py:288
  99.2 2.0 %collective-permute-start.17 = (s16[32,208,128]{2,1,0:T(8,128)(2,1)S(1)}, s16[32,208,128]{2,1,0:T(8,128)(2,1)S(1)}, u32[]{:S(2)}, u32[]{:S(2)}) collective-permute-start(s16[32,208,128]{2,1,0:T(8,128)(2,1)S(1)} %all-to-all-done.1.coded_ref), channel_id=1, source_target_pairs={{0,32},{32,0},{1,33},{33,1},{2,34},{34,2},{3,35},{35,3},{4,36},{36... | collective-permute-start | bytes 5111816 | tf_op jit(solution)/shard_map/ppermute | solution.py:232
  101.1 1.4 %copy-done.11 = bf16[768,1024]{1,0:T(8,128)(2,1)S(1)} copy-done((bf16[768,1024]{1,0:T(8,128)(2,1)S(1)}, bf16[768,1024]{1,0:T(8,128)(2,1)}, u32[]{:S(2)}) %copy-start.11) | copy-done | bytes 1572888
  102.5 3.6 %shard_map.63.least_ref = f32[8,1024]{1,0:T(8,128)S(1)} custom-call(bf16[768,1024]{1,0:T(8,128)(2,1)S(1)} %copy-done.11, s16[32,208,128]{2,1,0:T(8,128)(2,1)S(1)} %all-to-all-done.1.coded_ref, f32[1,1024]{1,0:T(1,128)S(1)} %bitcast.9, f32[8,1024]{1,0:T(8,128)S(1)} %broadcast_in_dim.3.least_ref), custom_call_target="tpu_custom_call" | custom-call | flops 3221225472 | bytes 3145728 | tf_op jit(solution)/shard_map/pallas_call | solution.py:215
  106.1 4.1 %shard_map.64 = f32[1,1024]{1,0:T(1,128)} custom-call(bf16[768,1024]{1,0:T(8,128)(2,1)S(1)} %copy-done.11, s16[32,208,128]{2,1,0:T(8,128)(2,1)S(1)} %collective-permute-done.17.coded_ref, f32[1,1024]{1,0:T(1,128)S(1)} %bitcast.10, f32[8,1024]{1,0:T(8,128)S(1)} %shard_map.63.least_ref), custom_call_target="tpu_custom_call" | custom-call | flops 3221225472 | bytes 3145728 | tf_op jit(solution)/shard_map/pallas_call | solution.py:215
  (44 shorter events, 4.2 us)
Async XLA Ops:
  0.6 3.4 %copy-start = (bf16[64,768]{1,0:T(8,128)(2,1)S(1)}, bf16[64,768]{1,0:T(8,128)(2,1)}, u32[]{:S(2)}) copy-start(bf16[64,768]{1,0:T(8,128)(2,1)} %param.4) | copy-start | bytes 294916
  0.6 12.2 %collective-permute-start.1 = (bf16[1024,768]{1,0:T(8,128)(2,1)}, bf16[1024,768]{1,0:T(8,128)(2,1)S(1)}, u32[]{:S(2)}, u32[]{:S(2)}) collective-permute-start(bf16[1024,768]{1,0:T(8,128)(2,1)} %rows_ref.1), channel_id=1, source_target_pairs={{0,32},{32,0},{1,33},{33,1},{2,34},{34,2},{3,35},{35,3},{4,36},{36... | collective-permute-start | bytes 4718600 | tf_op jit(solution)/shard_map/ppermute | solution.py:232
  4.0 8.9 %collective-permute-start = (s32[1,1024]{1,0:T(1,128)}, s32[1,1024]{1,0:T(1,128)S(1)}, u32[]{:S(2)}, u32[]{:S(2)}) collective-permute-start(s32[1,1024]{1,0:T(1,128)} %bitcast.5), channel_id=1, source_target_pairs={{0,32},{32,0},{1,33},{33,1},{2,34},{34,2},{3,35},{35,3},{4,36},{36... | collective-permute-start | bytes 12296 | tf_op jit(solution)/shard_map/ppermute | solution.py:232
  4.1 4.0 %collective-permute-start.2 = (bf16[32,768]{1,0:T(8,128)(2,1)S(1)}, bf16[32,768]{1,0:T(8,128)(2,1)S(1)}, u32[]{:S(2)}, u32[]{:S(2)}) collective-permute-start(bf16[32,768]{1,0:T(8,128)(2,1)S(1)} %constant_dynamic-slice_fusion), channel_id=1, source_target_pairs={{0,1},{1,0},{2,3},{3,2},{4,5},{5,4},{6,7},{7,6},{8,9},{9,8},{10,11... | collective-permute-start | bytes 147464 | tf_op jit(solution)/shard_map/ppermute | solution.py:232
  4.2 1.4 %copy-start.1 = (bf16[1024,768]{1,0:T(8,128)(2,1)S(1)}, bf16[1024,768]{1,0:T(8,128)(2,1)}, u32[]{:S(2)}) copy-start(bf16[1024,768]{1,0:T(8,128)(2,1)} %rows_ref.1) | copy-start | bytes 4718596
  5.6 0.7 copy-start.3
  8.1 7.8 %collective-permute-start.3 = (bf16[64,768]{1,0:T(8,128)(2,1)S(1)}, bf16[64,768]{1,0:T(8,128)(2,1)S(1)}, u32[]{:S(2)}, u32[]{:S(2)}) collective-permute-start(bf16[64,768]{1,0:T(8,128)(2,1)S(1)} %pad_maximum_fusion.1.c0), channel_id=1, source_target_pairs={{0,2},{2,4},{4,6},{6,0},{1,3},{3,5},{5,7},{7,1},{8,10},{10,12},{12... | collective-permute-start | bytes 294920 | tf_op jit(solution)/shard_map/ppermute | solution.py:236
  9.3 6.6 %collective-permute-start.4 = (bf16[64,768]{1,0:T(8,128)(2,1)S(1)}, bf16[64,768]{1,0:T(8,128)(2,1)S(1)}, u32[]{:S(2)}, u32[]{:S(2)}) collective-permute-start(bf16[64,768]{1,0:T(8,128)(2,1)S(1)} %pad_maximum_fusion.1.c0), channel_id=1, source_target_pairs={{0,4},{2,6},{4,0},{6,2},{1,5},{3,7},{5,1},{7,3},{8,12},{10,14},{12... | collective-permute-start | bytes 294920 | tf_op jit(solution)/shard_map/ppermute | solution.py:236
  11.7 4.6 %collective-permute-start.5 = (bf16[64,768]{1,0:T(8,128)(2,1)S(1)}, bf16[64,768]{1,0:T(8,128)(2,1)S(1)}, u32[]{:S(2)}, u32[]{:S(2)}) collective-permute-start(bf16[64,768]{1,0:T(8,128)(2,1)S(1)} %pad_maximum_fusion.1.c0), channel_id=1, source_target_pairs={{0,6},{2,0},{4,2},{6,4},{1,7},{3,1},{5,3},{7,5},{8,14},{10,8},{12,... | collective-permute-start | bytes 294920 | tf_op jit(solution)/shard_map/ppermute | solution.py:236
  46.5 21.4 %copy-start.4 = (bf16[256,768]{1,0:T(8,128)(2,1)}, bf16[256,768]{1,0:T(8,128)(2,1)S(1)}, u32[]{:S(2)}) copy-start(bf16[256,768]{1,0:T(8,128)(2,1)S(1)} %get-tuple-element.45.refs_0_) | copy-start | bytes 1179652
  46.5 15.2 %collective-permute-start.9 = (bf16[256,768]{1,0:T(8,128)(2,1)S(1)}, bf16[256,768]{1,0:T(8,128)(2,1)S(1)}, u32[]{:S(2)}, u32[]{:S(2)}) collective-permute-start(bf16[256,768]{1,0:T(8,128)(2,1)S(1)} %get-tuple-element.45.refs_0_), channel_id=1, source_target_pairs={{0,8},{8,16},{16,24},{24,0},{1,9},{9,17},{17,25},{25,1},{2,10},{10... | collective-permute-start | bytes 1179656 | tf_op jit(solution)/shard_map/ppermute | solution.py:236
  46.6 16.5 %collective-permute-start.10 = (bf16[256,768]{1,0:T(8,128)(2,1)S(1)}, bf16[256,768]{1,0:T(8,128)(2,1)S(1)}, u32[]{:S(2)}, u32[]{:S(2)}) collective-permute-start(bf16[256,768]{1,0:T(8,128)(2,1)S(1)} %get-tuple-element.45.refs_0_), channel_id=1, source_target_pairs={{0,16},{8,24},{16,0},{24,8},{1,17},{9,25},{17,1},{25,9},{2,18},{10... | collective-permute-start | bytes 1179656 | tf_op jit(solution)/shard_map/ppermute | solution.py:236
  48.2 17.9 %collective-permute-start.11 = (bf16[256,768]{1,0:T(8,128)(2,1)S(1)}, bf16[256,768]{1,0:T(8,128)(2,1)}, u32[]{:S(2)}, u32[]{:S(2)}) collective-permute-start(bf16[256,768]{1,0:T(8,128)(2,1)S(1)} %get-tuple-element.45.refs_0_), channel_id=1, source_target_pairs={{0,24},{8,0},{16,8},{24,16},{1,25},{9,1},{17,9},{25,17},{2,26},{10... | collective-permute-start | bytes 1179656 | tf_op jit(solution)/shard_map/ppermute | solution.py:236
  49.2 7.6 %collective-permute-start.6 = (s16[1,208,128]{2,1,0:T(8,128)(2,1)S(1)}, s16[1,208,128]{2,1,0:T(8,128)(2,1)S(1)}, u32[]{:S(2)}, u32[]{:S(2)}) collective-permute-start(s16[1,208,128]{2,1,0:T(8,128)(2,1)S(1)} %get-tuple-element.36.own), channel_id=1, source_target_pairs={{0,64},{64,128},{128,192},{192,0},{1,65},{65,129},{129,193},{193,1... | collective-permute-start | bytes 159752 | tf_op jit(solution)/shard_map/ppermute | solution.py:236
  52.2 7.0 %collective-permute-start.7 = (s16[1,208,128]{2,1,0:T(8,128)(2,1)S(1)}, s16[1,208,128]{2,1,0:T(8,128)(2,1)S(1)}, u32[]{:S(2)}, u32[]{:S(2)}) collective-permute-start(s16[1,208,128]{2,1,0:T(8,128)(2,1)S(1)} %get-tuple-element.36.own), channel_id=1, source_target_pairs={{0,128},{64,192},{128,0},{192,64},{1,129},{65,193},{129,1},{193,65... | collective-permute-start | bytes 159752 | tf_op jit(solution)/shard_map/ppermute | solution.py:236
  56.9 4.7 %collective-permute-start.8 = (s16[1,208,128]{2,1,0:T(8,128)(2,1)S(1)}, s16[1,208,128]{2,1,0:T(8,128)(2,1)S(1)}, u32[]{:S(2)}, u32[]{:S(2)}) collective-permute-start(s16[1,208,128]{2,1,0:T(8,128)(2,1)S(1)} %get-tuple-element.36.own), channel_id=1, source_target_pairs={{0,192},{64,0},{128,64},{192,128},{1,193},{65,1},{129,65},{193,129... | collective-permute-start | bytes 159752 | tf_op jit(solution)/shard_map/ppermute | solution.py:236
  61.6 1.5 %copy-start.6 = (bf16[256,768]{1,0:T(8,128)(2,1)}, bf16[256,768]{1,0:T(8,128)(2,1)S(1)}, u32[]{:S(2)}) copy-start(bf16[256,768]{1,0:T(8,128)(2,1)S(1)} %collective-permute-done.9.refs_1_) | copy-start | bytes 1179652
  63.1 0.8 copy-start.8
  67.9 9.1 %copy-start.2 = (bf16[1024,768]{1,0:T(8,128)(2,1)S(1)}, bf16[1024,768]{1,0:T(8,128)(2,1)}, u32[]{:S(2)}) copy-start(bf16[1024,768]{1,0:T(8,128)(2,1)} %rows_ref.1) | copy-start | bytes 4718596
  67.9 31.3 %all-to-all-start.1 = ((s16[32,208,128]{2,1,0:T(8,128)(2,1)}), s16[32,208,128]{2,1,0:T(8,128)(2,1)S(1)}, u32[]{:S(2)}, u32[]{:S(2)}) async-start(s16[32,208,128]{2,1,0:T(8,128)(2,1)} %get-tuple-element.40), calls=%async_computation.1 | async-start | bytes 3407872 | tf_op jit(solution)/shard_map/all_to_all | solution.py:288
  75.1 4.8 %collective-permute-start.12 = (bf16[256,768]{1,0:T(8,128)(2,1)}, bf16[256,768]{1,0:T(8,128)(2,1)}, u32[]{:S(2)}, u32[]{:S(2)}) collective-permute-start(bf16[256,768]{1,0:T(8,128)(2,1)} %copy-done.4), channel_id=1, source_target_pairs={{0,32},{32,0},{1,33},{33,1},{2,34},{34,2},{3,35},{35,3},{4,36},{36... | collective-permute-start | bytes 1179656 | tf_op jit(solution)/shard_map/ppermute | solution.py:232
  75.9 3.9 %collective-permute-start.13 = (bf16[256,768]{1,0:T(8,128)(2,1)}, bf16[256,768]{1,0:T(8,128)(2,1)}, u32[]{:S(2)}, u32[]{:S(2)}) collective-permute-start(bf16[256,768]{1,0:T(8,128)(2,1)} %copy-done.6), channel_id=1, source_target_pairs={{0,32},{32,0},{1,33},{33,1},{2,34},{34,2},{3,35},{35,3},{4,36},{36... | collective-permute-start | bytes 1179656 | tf_op jit(solution)/shard_map/ppermute | solution.py:232
  76.0 3.8 %collective-permute-start.14 = (bf16[256,768]{1,0:T(8,128)(2,1)}, bf16[256,768]{1,0:T(8,128)(2,1)}, u32[]{:S(2)}, u32[]{:S(2)}) collective-permute-start(bf16[256,768]{1,0:T(8,128)(2,1)} %copy-done.8), channel_id=1, source_target_pairs={{0,32},{32,0},{1,33},{33,1},{2,34},{34,2},{3,35},{35,3},{4,36},{36... | collective-permute-start | bytes 1179656 | tf_op jit(solution)/shard_map/ppermute | solution.py:232
  76.5 3.4 %collective-permute-start.15 = (bf16[256,768]{1,0:T(8,128)(2,1)}, bf16[256,768]{1,0:T(8,128)(2,1)}, u32[]{:S(2)}, u32[]{:S(2)}) collective-permute-start(bf16[256,768]{1,0:T(8,128)(2,1)} %collective-permute-done.11.refs_3_), channel_id=1, source_target_pairs={{0,32},{32,0},{1,33},{33,1},{2,34},{34,2},{3,35},{35,3},{4,36},{36... | collective-permute-start | bytes 1179656 | tf_op jit(solution)/shard_map/ppermute | solution.py:232
  76.6 1.7 %collective-permute-start.16 = (f32[32,768]{1,0:T(8,128)S(1)}, f32[32,768]{1,0:T(8,128)}, u32[]{:S(2)}, u32[]{:S(2)}) collective-permute-start(f32[32,768]{1,0:T(8,128)S(1)} %get-tuple-element.51), channel_id=1, source_target_pairs={{0,32},{32,0},{1,33},{33,1},{2,34},{34,2},{3,35},{35,3},{4,36},{36... | collective-permute-start | bytes 294920 | tf_op jit(solution)/shard_map/ppermute | solution.py:232
  79.9 1.0 copy-start.5
  80.9 1.0 copy-start.7
  81.9 1.0 copy-start.9
  88.5 1.2 %copy-start.10 = (bf16[768,1024]{1,0:T(8,128)(2,1)}, bf16[768,1024]{1,0:T(8,128)(2,1)S(1)}, u32[]{:S(2)}) copy-start(bf16[768,1024]{1,0:T(8,128)(2,1)S(1)} %get-tuple-element.53.turned_ref) | copy-start | bytes 4718596
  99.2 6.9 %collective-permute-start.17 = (s16[32,208,128]{2,1,0:T(8,128)(2,1)S(1)}, s16[32,208,128]{2,1,0:T(8,128)(2,1)S(1)}, u32[]{:S(2)}, u32[]{:S(2)}) collective-permute-start(s16[32,208,128]{2,1,0:T(8,128)(2,1)S(1)} %all-to-all-done.1.coded_ref), channel_id=1, source_target_pairs={{0,32},{32,0},{1,33},{33,1},{2,34},{34,2},{3,35},{35,3},{4,36},{36... | collective-permute-start | bytes 5111816 | tf_op jit(solution)/shard_map/ppermute | solution.py:232
  101.1 1.4 %copy-start.11 = (bf16[768,1024]{1,0:T(8,128)(2,1)S(1)}, bf16[768,1024]{1,0:T(8,128)(2,1)}, u32[]{:S(2)}) copy-start(bf16[768,1024]{1,0:T(8,128)(2,1)} %copy-done.10) | copy-start | bytes 4718596

commit v4 on v3

--- a/solution.py
+++ b/solution.py
@@ -119,7 +119,7 @@
     return [quantize(blocks[b], code) for b in range(COLS)], to_lanes(code)
 
 
-def group_kernel(in_ref, c0, c1, c2, c3, out_ref, centers_ref):
+def group_kernel(in_ref, out_ref):
     together = 8
 
     def step(t, carry):
@@ -134,16 +134,14 @@
     for b in range(COLS):
         out_ref[0, block(b), :] = coded[b]
     out_ref[0, BODY:CODED, :] = footer(counts, codes)
-    for i, ref in enumerate((c0, c1, c2, c3)):
-        n = ref.shape[0]
-        centers_ref[i * n : (i + 1) * n, :] = ref[...]
-
-
-def refine_kernel(own, one, two, three, refined_ref, coded_ref):
-    even = add_coded(two, 0, *add_coded(own, 0, *nothing()))
-    odd = add_coded(three, 0, *add_coded(one, 0, *nothing()))
-    counts = to_column(even[1] + odd[1])
-    refined = [(even[0][b] + odd[0][b]) / counts for b in range(COLS)]
+
+
+def refine_kernel(groups, refined_ref, coded_ref):
+    blocks, counts = nothing()
+    for g in range(groups.shape[0]):
+        blocks, counts = add_coded(groups, g, blocks, counts)
+    counts = to_column(counts)
+    refined = [blocks[b] / counts for b in range(COLS)]
     for b in range(COLS):
         refined_ref[:, b * 128 : (b + 1) * 128] = refined[b]
     coded, codes = code_blocks(refined)
@@ -224,16 +222,32 @@
     )(*args)
 
 
-def ring(axis, size, k):
-    return [(i, (i + k) % size) for i in range(size)]
-
-
 def swap(value, axis):
     return lax.ppermute(value, axis, [(0, 1), (1, 0)])
 
 
-def around(part, axis):
-    return [part] + [lax.ppermute(part, axis, ring(axis, 4, k)) for k in (1, 2, 3)]
+PLANE = ("core", "y", "x", "zl")
+
+
+def plane(core, y, x, zl=0):
+    return ((core * 4 + y) * 4 + x) * 2 + zl
+
+
+def along_first():
+    both = [(i, z) for i in range(4) for z in range(2)]
+    return [[plane(0, a, i, z) for i, z in both] for a in range(4)] + [
+        [plane(1, i, a, z) for i, z in both] for a in range(4)
+    ]
+
+
+def along_second(k):
+    pairs = []
+    for a in range(4):
+        for i in range(4):
+            to = (i + k) % 4
+            pairs.append((plane(0, i, a) // 2, plane(0, to, a) // 2))
+            pairs.append((plane(1, a, i) // 2, plane(1, a, to) // 2))
+    return pairs
 
 
 def after(first, values):
@@ -250,7 +264,10 @@
     other_rows = swap(embeddings, "core")
 
     mine = lax.dynamic_slice(centers, (core * HALF, 0), (HALF, D))
-    current = around(jnp.concatenate([mine, swap(mine, "zl")]), "x")
+    current = lax.all_to_all(
+        jnp.broadcast_to(mine[None], (8, HALF, D)),
+        PLANE, 0, 0, axis_index_groups=along_first(),
+    ).reshape(8 * HALF, D)
 
     wide = embeddings.astype(f32)
     norms = jnp.sum(wide * wide, 1).reshape(1, n)
@@ -268,21 +285,25 @@
         base, labels, other_labels, sums, other_rows,
         flops=2 * 1024 * n * D, moved=6 << 20, smem=1,
     )
-    sums, *current = lax.optimization_barrier((sums, *current))
+    sums, current = lax.optimization_barrier((sums, current))
     sums = lax.all_to_all(sums, SHARD, 0, 0)
-    group, current = call(
+    group = call(
         group_kernel,
-        (shape((1, CODED, 128), i16), shape((8 * HALF, D), bf16)),
-        sums, *current,
+        shape((1, CODED, 128), i16),
+        sums,
         flops=1 << 22, moved=2 << 20,
     )
+    (current,) = after(group, (current,))
+    current = [current] + [
+        lax.ppermute(current, PLANE[:3], along_second(k)) for k in (1, 3, 2)
+    ]
     groups, current = lax.optimization_barrier(
-        (around(group, "zh"), around(current, "y"))
+        (lax.all_gather(group, "zh", axis=0, tiled=True), current)
     )
     refined, coded = call(
         refine_kernel,
         (shape((HALF, D), f32), shape((CHUNKS, CODED, 128), i16)),
-        *groups,
+        groups,
         flops=1 << 20, moved=2 << 20,
     )
     new_own = lax.all_to_all(coded, SHARD, 0, 0)

time: 111 us -> 112 us (level)
  blocking collectives: 29.4 us -> 48.2 us
  waiting for transfers between devices: 17 us -> 4.2 us
  starting transfers between devices: 32.1 us -> 26.5 us
    all_gather x0 -> x1, blocking collectives: none -> 15.8 us  [on_device(): lax.all_gather(group, 'zh', axis=0, tiled=True)]
    ppermute x9 -> x3, starting transfers between devices: 17.5 us -> 2.76 us  [on_device(): lax.ppermute(current, PLANE[:3], along_second(k))]
    ppermute x9 -> x8, starting transfers between devices: 7.33 us -> 15.2 us  [swap(): return lax.ppermute(value, axis, [(0, 1), (1, 0)])]
    ppermute x9 -> x3, waiting for transfers between devices: 6.52 us -> 0.01 us  [on_device(): lax.ppermute(current, PLANE[:3], along_second(k))]
    all_to_all x1, waiting for transfers between devices: 9.49 us -> 3.26 us  [on_device(): new_own = lax.all_to_all(coded, SHARD, 0, 0)]
    all_to_all x0 -> x1, starting transfers between devices: none -> 4.09 us  [on_device(): lax.all_to_all(jnp.broadcast_to(mine[None], (8, HALF, D)), PLANE, 0, 0, a...]
    all_to_all x1, blocking collectives: 29.4 us -> 32.4 us  [on_device(): sums = lax.all_to_all(sums, SHARD, 0, 0)]
    all_to_all x1, starting transfers between devices: 7.19 us -> 4.43 us  [on_device(): new_own = lax.all_to_all(coded, SHARD, 0, 0)]
  transfers between devices with their start and end apart: 19 -> 13, of which waited for: 6 -> 2; matrix products, arithmetic and copies ran while one was open for 2% -> 2% of each run, Pallas kernels for 13% -> 13%
where the time goes in v4:
time: 112 us; the launch traced here: 111 us
  blocking collectives  48.2 us (43%)
  starting transfers between devices  26.5 us (24%)
  Pallas kernels  20.8 us (19%)
  local copies, waits for them, and re-layouts  8.97 us (8%)
  waiting for transfers between devices  4.2 us (4%)
  other arithmetic  1.97 us (2%)
    all_to_all x1, blocking collectives, on_device(): sums = lax.all_to_all(sums, SHARD, 0, 0)  32.4 us
    pallas_call x7, Pallas kernels, call(): pl.pallas_call(kernel, out_shape=out_shape, in_specs=specs, out_specs=tup...  20.8 us
    all_gather x1, blocking collectives, on_device(): lax.all_gather(group, 'zh', axis=0, tiled=True)  15.8 us
    ppermute x8, starting transfers between devices, swap(): return lax.ppermute(value, axis, [(0, 1), (1, 0)])  15.2 us
    unnamed x22, local copies, waits for them, and re-layouts  8.19 us
    all_to_all x1, starting transfers between devices, on_device(): new_own = lax.all_to_all(coded, SHARD, 0, 0)  4.43 us
    all_to_all x1, starting transfers between devices, on_device(): lax.all_to_all(jnp.broadcast_to(mine[None], (8, HALF, D)), PLANE, 0, 0, a...  4.09 us
    all_to_all x1, waiting for transfers between devices, on_device(): new_own = lax.all_to_all(coded, SHARD, 0, 0)  3.26 us
  transfers between devices with their start and end apart: 13, of which 2 were waited for; matrix products, arithmetic and copies ran while one was open for 2% of the time, Pallas kernels for 13%

profile of v4, /device:TPU:1, one launch (start us, length us, event | category | flops | bytes accessed | tf_op | source)
XLA Modules:
  0.0 111.5 jit_solution(15523348419386692210)
XLA Ops:
  0.6 3.3 %collective-permute-start.1 = (bf16[1024,768]{1,0:T(8,128)(2,1)}, bf16[1024,768]{1,0:T(8,128)(2,1)S(1)}, u32[]{:S(2)}, u32[]{:S(2)}) collective-permute-start(bf16[1024,768]{1,0:T(8,128)(2,1)} %rows_ref.1), channel_id=1, source_target_pairs={{0,32},{32,0},{1,33},{33,1},{2,34},{34,2},{3,35},{35,3},{4,36},{36... | collective-permute-start | bytes 4718600 | tf_op jit(solution)/shard_map/ppermute | solution.py:226
  4.0 0.8 broadcast_in_dim.4
  4.8 4.1 %all-to-all-start = ((bf16[8,32,768]{2,1,0:T(8,128)(2,1)}), bf16[8,32,768]{2,1,0:T(8,128)(2,1)}, u32[]{:S(2)}, u32[]{:S(2)}) async-start(bf16[8,32,768]{2,1,0:T(8,128)(2,1)} %broadcast_in_dim.4), calls=%async_computation | async-start | bytes 786432 | tf_op jit(solution)/shard_map/all_to_all | solution.py:267
  8.9 0.9 collective-permute-start
  9.7 1.4 %copy-done.1 = bf16[1024,768]{1,0:T(8,128)(2,1)S(1)} copy-done((bf16[1024,768]{1,0:T(8,128)(2,1)S(1)}, bf16[1024,768]{1,0:T(8,128)(2,1)}, u32[]{:S(2)}) %copy-start.1) | copy-done | bytes 1572888
  11.2 0.7 copy-done.3
  11.8 1.8 %shard_map.58.own_sums = f32[1024,768]{1,0:T(8,128)S(1)} custom-call(s32[1]{0:T(128)} %bitcast.1.base_ref, s32[1,1024]{1,0:T(1,128)S(1)} %bitcast.7, bf16[1024,768]{1,0:T(8,128)(2,1)S(1)} %copy-done.1), custom_call_target="tpu_custom_call" | custom-call | flops 1610612736 | bytes 5242880 | tf_op jit(solution)/shard_map/pallas_call | solution.py:213
  13.7 3.0 %shard_map.59 = s16[32,208,128]{2,1,0:T(8,128)(2,1)S(1)} custom-call(s32[1]{0:T(128)} %bitcast.1.base_ref, s32[1,1024]{1,0:T(1,128)S(1)} %bitcast.8, s32[1,1024]{1,0:T(1,128)S(1)} %collective-permute-done.labels, f32[1024,768]{1,0:T(8,128)S(1)} %shard_map.58.own_sums, bf16[1024,768]{1,0:T(8,128)(2,1)S(1)} %collective-permute-done.1.rows), custom_call_target="tpu_custom_call" | custom-call | flops 1610612736 | bytes 6291456 | tf_op jit(solution)/shard_map/pallas_call | solution.py:213
  16.8 32.4 %all_to_all.15.in_ref = s16[32,208,128]{2,1,0:T(8,128)(2,1)S(1)} all-to-all(s16[32,208,128]{2,1,0:T(8,128)(2,1)S(1)} %shard_map.59), channel_id=1, replica_groups=mesh['zh'=4,'core'=2,'y'=4,'x'=4,'zl'=2] {'y','x','zl'}, dimensions={0} | all-to-all | bytes 3407872 | tf_op jit(solution)/shard_map/all_to_all | solution.py:289
  49.1 0.8 shard_map.60
  49.9 0.6 collective-permute-start.2
  50.5 2.2 %collective-permute-start.3 = (bf16[256,768]{1,0:T(8,128)(2,1)}, bf16[256,768]{1,0:T(8,128)(2,1)S(1)}, u32[]{:S(2)}, u32[]{:S(2)}) collective-permute-start(bf16[256,768]{1,0:T(8,128)(2,1)} %bitcast.3.refs_0_), channel_id=1, source_target_pairs={{0,24},{32,38},{8,0},{34,32},{16,8},{36,34},{24,16},{38,36},{2,26}... | collective-permute-start | bytes 1179656 | tf_op jit(solution)/shard_map/ppermute | solution.py:298
  52.6 15.8 %all_gather.3.groups = s16[4,208,128]{2,1,0:T(8,128)(2,1)S(1)} all-gather(s16[1,208,128]{2,1,0:T(8,128)(2,1)S(1)} %shard_map.60), channel_id=1, replica_groups=mesh['zh'=4,'core'=2,'y'=4,'x'=4,'zl'=2] {'zh'}, dimensions={0}, use_global_device_ids=true | all-gather | bytes 266240 | tf_op jit(solution)/shard_map/all_gather | solution.py:301
  68.5 0.8 copy-done.5
  69.2 0.8 copy-done.7
  70.0 1.7 %shard_map.61 = (f32[32,768]{1,0:T(8,128)S(1)}, s16[32,208,128]{2,1,0:T(8,128)(2,1)}) custom-call(s16[4,208,128]{2,1,0:T(8,128)(2,1)S(1)} %all_gather.3.groups), custom_call_target="tpu_custom_call" | custom-call | flops 1048576 | bytes 2097152 | tf_op jit(solution)/shard_map/pallas_call | solution.py:213
  71.8 4.4 %all-to-all-start.2 = ((s16[32,208,128]{2,1,0:T(8,128)(2,1)}), s16[32,208,128]{2,1,0:T(8,128)(2,1)S(1)}, u32[]{:S(2)}, u32[]{:S(2)}) async-start(s16[32,208,128]{2,1,0:T(8,128)(2,1)} %get-tuple-element.26), calls=%async_computation.2 | async-start | bytes 3407872 | tf_op jit(solution)/shard_map/all_to_all | solution.py:309
  76.2 4.9 %collective-permute-start.5 = (bf16[256,768]{1,0:T(8,128)(2,1)}, bf16[256,768]{1,0:T(8,128)(2,1)}, u32[]{:S(2)}, u32[]{:S(2)}) collective-permute-start(bf16[256,768]{1,0:T(8,128)(2,1)} %bitcast.3.refs_0_), channel_id=1, source_target_pairs={{0,32},{32,0},{1,33},{33,1},{2,34},{34,2},{3,35},{35,3},{4,36},{36... | collective-permute-start | bytes 1179656 | tf_op jit(solution)/shard_map/ppermute | solution.py:226
  81.2 0.4 collective-permute-start.7
  81.7 0.4 collective-permute-start.9
  82.5 0.9 collective-permute-done.9
  83.4 0.9 broadcast_select_fusion.1
  84.3 0.7 pad_maximum_fusion
  85.1 1.0 copy-done.6
  86.1 1.0 copy-done.8
  87.1 5.8 %shard_map.62 = (f32[1,1024]{1,0:T(1,128)}, bf16[768,1024]{1,0:T(8,128)(2,1)S(1)}) custom-call(f32[1,1024]{1,0:T(1,128)S(1)} %bitcast.9, bf16[1024,768]{1,0:T(8,128)(2,1)S(1)} %copy-done.2, bf16[256,768]{1,0:T(8,128)(2,1)} %bitcast.3.refs_0_, bf16[256,768]{1,0:T(8,128)(2,1)S(1)} %copy-done.6, bf16[256,768]{1,0:T(8,128)(2,1)S(1)} %copy-done.8, ...), custom_call_target="tpu_custom_call" | custom-call | flops 3221225472 | bytes 5242880 | tf_op jit(solution)/shard_map/pallas_call | solution.py:213
  92.8 1.2 %copy-done.9 = bf16[768,1024]{1,0:T(8,128)(2,1)} copy-done((bf16[768,1024]{1,0:T(8,128)(2,1)}, bf16[768,1024]{1,0:T(8,128)(2,1)S(1)}, u32[]{:S(2)}) %copy-start.9) | copy-done | bytes 1572888
  94.0 3.3 %all-to-all-done.2.coded_ref = s16[32,208,128]{2,1,0:T(8,128)(2,1)S(1)} async-done(((s16[32,208,128]{2,1,0:T(8,128)(2,1)}), s16[32,208,128]{2,1,0:T(8,128)(2,1)S(1)}, u32[]{:S(2)}, u32[]{:S(2)}) %all-to-all-start.2) | async-done | bytes 1703968 | tf_op jit(solution)/shard_map/all_to_all | solution.py:309
  97.2 5.1 %collective-permute-start.10 = (s16[32,208,128]{2,1,0:T(8,128)(2,1)S(1)}, s16[32,208,128]{2,1,0:T(8,128)(2,1)S(1)}, u32[]{:S(2)}, u32[]{:S(2)}) collective-permute-start(s16[32,208,128]{2,1,0:T(8,128)(2,1)S(1)} %all-to-all-done.2.coded_ref), channel_id=1, source_target_pairs={{0,32},{32,0},{1,33},{33,1},{2,34},{34,2},{3,35},{35,3},{4,36},{36... | collective-permute-start | bytes 5111816 | tf_op jit(solution)/shard_map/ppermute | solution.py:226
  102.3 1.4 %copy-done.10 = bf16[768,1024]{1,0:T(8,128)(2,1)S(1)} copy-done((bf16[768,1024]{1,0:T(8,128)(2,1)S(1)}, bf16[768,1024]{1,0:T(8,128)(2,1)}, u32[]{:S(2)}) %copy-start.10) | copy-done | bytes 1572888
  103.7 3.5 %shard_map.63.least_ref = f32[8,1024]{1,0:T(8,128)S(1)} custom-call(bf16[768,1024]{1,0:T(8,128)(2,1)S(1)} %copy-done.10, s16[32,208,128]{2,1,0:T(8,128)(2,1)S(1)} %all-to-all-done.2.coded_ref, f32[1,1024]{1,0:T(1,128)S(1)} %bitcast.10, f32[8,1024]{1,0:T(8,128)S(1)} %broadcast_in_dim.10.least_ref), custom_call_target="tpu_custom_call" | custom-call | flops 3221225472 | bytes 3145728 | tf_op jit(solution)/shard_map/pallas_call | solution.py:213
  107.3 4.1 %shard_map.64 = f32[1,1024]{1,0:T(1,128)} custom-call(bf16[768,1024]{1,0:T(8,128)(2,1)S(1)} %copy-done.10, s16[32,208,128]{2,1,0:T(8,128)(2,1)S(1)} %collective-permute-done.10.coded_ref, f32[1,1024]{1,0:T(1,128)S(1)} %bitcast.11, f32[8,1024]{1,0:T(8,128)S(1)} %shard_map.63.least_ref), custom_call_target="tpu_custom_call" | custom-call | flops 3221225472 | bytes 3145728 | tf_op jit(solution)/shard_map/pallas_call | solution.py:213
  (31 shorter events, 0.6 us)
Async XLA Ops:
  0.6 3.3 %copy-start = (bf16[64,768]{1,0:T(8,128)(2,1)S(1)}, bf16[64,768]{1,0:T(8,128)(2,1)}, u32[]{:S(2)}) copy-start(bf16[64,768]{1,0:T(8,128)(2,1)} %param.4) | copy-start | bytes 294916
  0.6 13.0 %collective-permute-start.1 = (bf16[1024,768]{1,0:T(8,128)(2,1)}, bf16[1024,768]{1,0:T(8,128)(2,1)S(1)}, u32[]{:S(2)}, u32[]{:S(2)}) collective-permute-start(bf16[1024,768]{1,0:T(8,128)(2,1)} %rows_ref.1), channel_id=1, source_target_pairs={{0,32},{32,0},{1,33},{33,1},{2,34},{34,2},{3,35},{35,3},{4,36},{36... | collective-permute-start | bytes 4718600 | tf_op jit(solution)/shard_map/ppermute | solution.py:226
  4.8 12.0 %all-to-all-start = ((bf16[8,32,768]{2,1,0:T(8,128)(2,1)}), bf16[8,32,768]{2,1,0:T(8,128)(2,1)}, u32[]{:S(2)}, u32[]{:S(2)}) async-start(bf16[8,32,768]{2,1,0:T(8,128)(2,1)} %broadcast_in_dim.4), calls=%async_computation | async-start | bytes 786432 | tf_op jit(solution)/shard_map/all_to_all | solution.py:267
  8.9 4.8 %collective-permute-start = (s32[1,1024]{1,0:T(1,128)}, s32[1,1024]{1,0:T(1,128)S(1)}, u32[]{:S(2)}, u32[]{:S(2)}) collective-permute-start(s32[1,1024]{1,0:T(1,128)} %bitcast.6), channel_id=1, source_target_pairs={{0,32},{32,0},{1,33},{33,1},{2,34},{34,2},{3,35},{35,3},{4,36},{36... | collective-permute-start | bytes 12296 | tf_op jit(solution)/shard_map/ppermute | solution.py:226
  9.7 1.4 %copy-start.1 = (bf16[1024,768]{1,0:T(8,128)(2,1)S(1)}, bf16[1024,768]{1,0:T(8,128)(2,1)}, u32[]{:S(2)}) copy-start(bf16[1024,768]{1,0:T(8,128)(2,1)} %rows_ref.1) | copy-start | bytes 4718596
  11.2 0.7 copy-start.3
  11.8 1.9 %copy-start.4 = (s32[1024,1]{0,1:T(1,128)S(1)}, s32[1024,1]{0,1:T(1,128)}, u32[]{:S(2)}) copy-start(s32[1024,1]{0,1:T(1,128)} %param.5) | copy-start | bytes 12292
  49.9 18.6 %collective-permute-start.2 = (bf16[256,768]{1,0:T(8,128)(2,1)}, bf16[256,768]{1,0:T(8,128)(2,1)S(1)}, u32[]{:S(2)}, u32[]{:S(2)}) collective-permute-start(bf16[256,768]{1,0:T(8,128)(2,1)} %bitcast.3.refs_0_), channel_id=1, source_target_pairs={{0,8},{32,34},{8,16},{34,36},{16,24},{36,38},{24,0},{38,32},{2,10}... | collective-permute-start | bytes 1179656 | tf_op jit(solution)/shard_map/ppermute | solution.py:298
  50.5 18.0 %collective-permute-start.3 = (bf16[256,768]{1,0:T(8,128)(2,1)}, bf16[256,768]{1,0:T(8,128)(2,1)S(1)}, u32[]{:S(2)}, u32[]{:S(2)}) collective-permute-start(bf16[256,768]{1,0:T(8,128)(2,1)} %bitcast.3.refs_0_), channel_id=1, source_target_pairs={{0,24},{32,38},{8,0},{34,32},{16,8},{36,34},{24,16},{38,36},{2,26}... | collective-permute-start | bytes 1179656 | tf_op jit(solution)/shard_map/ppermute | solution.py:298
  52.6 17.4 %collective-permute-start.4 = (bf16[256,768]{1,0:T(8,128)(2,1)}, bf16[256,768]{1,0:T(8,128)(2,1)}, u32[]{:S(2)}, u32[]{:S(2)}) collective-permute-start(bf16[256,768]{1,0:T(8,128)(2,1)} %bitcast.3.refs_0_), channel_id=1, source_target_pairs={{0,16},{32,36},{8,24},{34,38},{16,0},{36,32},{24,8},{38,34},{2,18}... | collective-permute-start | bytes 1179656 | tf_op jit(solution)/shard_map/ppermute | solution.py:298
  68.5 0.8 copy-start.5
  69.2 0.8 copy-start.7
  71.8 10.4 %copy-start.2 = (bf16[1024,768]{1,0:T(8,128)(2,1)S(1)}, bf16[1024,768]{1,0:T(8,128)(2,1)}, u32[]{:S(2)}) copy-start(bf16[1024,768]{1,0:T(8,128)(2,1)} %rows_ref.1) | copy-start | bytes 4718596
  71.8 25.5 %all-to-all-start.2 = ((s16[32,208,128]{2,1,0:T(8,128)(2,1)}), s16[32,208,128]{2,1,0:T(8,128)(2,1)S(1)}, u32[]{:S(2)}, u32[]{:S(2)}) async-start(s16[32,208,128]{2,1,0:T(8,128)(2,1)} %get-tuple-element.26), calls=%async_computation.2 | async-start | bytes 3407872 | tf_op jit(solution)/shard_map/all_to_all | solution.py:309
  76.2 8.8 %collective-permute-start.5 = (bf16[256,768]{1,0:T(8,128)(2,1)}, bf16[256,768]{1,0:T(8,128)(2,1)}, u32[]{:S(2)}, u32[]{:S(2)}) collective-permute-start(bf16[256,768]{1,0:T(8,128)(2,1)} %bitcast.3.refs_0_), channel_id=1, source_target_pairs={{0,32},{32,0},{1,33},{33,1},{2,34},{34,2},{3,35},{35,3},{4,36},{36... | collective-permute-start | bytes 1179656 | tf_op jit(solution)/shard_map/ppermute | solution.py:226
  81.1 3.9 %collective-permute-start.6 = (bf16[256,768]{1,0:T(8,128)(2,1)}, bf16[256,768]{1,0:T(8,128)(2,1)}, u32[]{:S(2)}, u32[]{:S(2)}) collective-permute-start(bf16[256,768]{1,0:T(8,128)(2,1)} %copy-done.5), channel_id=1, source_target_pairs={{0,32},{32,0},{1,33},{33,1},{2,34},{34,2},{3,35},{35,3},{4,36},{36... | collective-permute-start | bytes 1179656 | tf_op jit(solution)/shard_map/ppermute | solution.py:226
  81.2 3.8 %collective-permute-start.7 = (bf16[256,768]{1,0:T(8,128)(2,1)}, bf16[256,768]{1,0:T(8,128)(2,1)}, u32[]{:S(2)}, u32[]{:S(2)}) collective-permute-start(bf16[256,768]{1,0:T(8,128)(2,1)} %copy-done.7), channel_id=1, source_target_pairs={{0,32},{32,0},{1,33},{33,1},{2,34},{34,2},{3,35},{35,3},{4,36},{36... | collective-permute-start | bytes 1179656 | tf_op jit(solution)/shard_map/ppermute | solution.py:226
  81.6 3.4 %collective-permute-start.8 = (bf16[256,768]{1,0:T(8,128)(2,1)}, bf16[256,768]{1,0:T(8,128)(2,1)}, u32[]{:S(2)}, u32[]{:S(2)}) collective-permute-start(bf16[256,768]{1,0:T(8,128)(2,1)} %collective-permute-done.4.refs_3_), channel_id=1, source_target_pairs={{0,32},{32,0},{1,33},{33,1},{2,34},{34,2},{3,35},{35,3},{4,36},{36... | collective-permute-start | bytes 1179656 | tf_op jit(solution)/shard_map/ppermute | solution.py:226
  81.7 1.7 %collective-permute-start.9 = (f32[32,768]{1,0:T(8,128)S(1)}, f32[32,768]{1,0:T(8,128)}, u32[]{:S(2)}, u32[]{:S(2)}) collective-permute-start(f32[32,768]{1,0:T(8,128)S(1)} %get-tuple-element.37), channel_id=1, source_target_pairs={{0,32},{32,0},{1,33},{33,1},{2,34},{34,2},{3,35},{35,3},{4,36},{36... | collective-permute-start | bytes 294920 | tf_op jit(solution)/shard_map/ppermute | solution.py:226
  85.1 1.0 copy-start.6
  86.1 1.0 copy-start.8
  92.8 1.2 %copy-start.9 = (bf16[768,1024]{1,0:T(8,128)(2,1)}, bf16[768,1024]{1,0:T(8,128)(2,1)S(1)}, u32[]{:S(2)}) copy-start(bf16[768,1024]{1,0:T(8,128)(2,1)S(1)} %get-tuple-element.39.turned_ref) | copy-start | bytes 4718596
  97.2 10.1 %collective-permute-start.10 = (s16[32,208,128]{2,1,0:T(8,128)(2,1)S(1)}, s16[32,208,128]{2,1,0:T(8,128)(2,1)S(1)}, u32[]{:S(2)}, u32[]{:S(2)}) collective-permute-start(s16[32,208,128]{2,1,0:T(8,128)(2,1)S(1)} %all-to-all-done.2.coded_ref), channel_id=1, source_target_pairs={{0,32},{32,0},{1,33},{33,1},{2,34},{34,2},{3,35},{35,3},{4,36},{36... | collective-permute-start | bytes 5111816 | tf_op jit(solution)/shard_map/ppermute | solution.py:226
  102.3 1.4 %copy-start.10 = (bf16[768,1024]{1,0:T(8,128)(2,1)S(1)}, bf16[768,1024]{1,0:T(8,128)(2,1)}, u32[]{:S(2)}) copy-start(bf16[768,1024]{1,0:T(8,128)(2,1)} %copy-done.9) | copy-start | bytes 4718596

commit v5 on v2

--- a/solution.py
+++ b/solution.py
@@ -13,24 +13,25 @@
 HALF = 32
 CHUNKS = 32
 COLS = D // 128
-BODY = COLS * HALF
+PART = HALF // 2
+BODY = COLS * PART
 CODED = BODY + 16
 LIMIT = 32700.0
 VMEM = 16 * 1024 * 1024
 
 
 def diagonal(rows):
-    r = lax.broadcasted_iota(jnp.int32, (rows, 128), 0) % HALF
+    r = lax.broadcasted_iota(jnp.int32, (rows, 128), 0) % PART
     c = lax.broadcasted_iota(jnp.int32, (rows, 128), 1)
     return r == c
 
 
 def to_lanes(column):
-    return jnp.sum(jnp.where(diagonal(HALF), column, 0.0), 0, keepdims=True)
+    return jnp.sum(jnp.where(diagonal(PART), column, 0.0), 0, keepdims=True)
 
 
 def to_column(row):
-    return jnp.sum(jnp.where(diagonal(HALF), row, 0.0), 1, keepdims=True)
+    return jnp.sum(jnp.where(diagonal(PART), row, 0.0), 1, keepdims=True)
 
 
 def code_of(values):
@@ -54,46 +55,51 @@
 
 
 TILE = 256
-
-
-def is_named(t, base, labels):
+EACH = TILE // PART
+TILES = CHUNKS * PART // TILE
+
+
+def is_named(part, t, base, labels):
     j = t * TILE + lax.broadcasted_iota(jnp.int32, (TILE, 1), 0)
-    k = j + (j // HALF) * HALF + base
+    k = (j // PART) * (2 * HALF) + (part * PART + base) + j % PART
     return jnp.where(k == labels, 1.0, 0.0)
 
 
 def own_sums_kernel(base_ref, labels, rows, out_ref):
-    for t in range(CHUNKS * HALF // TILE):
-        hot = is_named(t, base_ref[0], labels[...]).astype(jnp.bfloat16)
-        out_ref[t * TILE : (t + 1) * TILE, :] = jnp.dot(
-            hot, rows[...], preferred_element_type=jnp.float32
-        )
-
-
-def chip_sums_kernel(base_ref, own_labels, labels, own_sums, rows, out_ref):
-    for t in range(CHUNKS * HALF // TILE):
-        hot = is_named(t, base_ref[0], labels[...])
-        sums = own_sums[t * TILE : (t + 1) * TILE, :] + jnp.dot(
-            hot.astype(jnp.bfloat16), rows[...], preferred_element_type=jnp.float32
-        )
-        hot = hot + is_named(t, base_ref[0], own_labels[...])
-        counts = jnp.sum(hot, 1, keepdims=True)
-        code = code_of(sums)
-        coded = quantize(sums, code)
-        for c in range(TILE // HALF):
-            at = t * (TILE // HALF) + c
-            part = slice(c * HALF, (c + 1) * HALF)
-            for b in range(COLS):
-                out_ref[at, b * HALF : (b + 1) * HALF, :] = coded[
-                    part, b * 128 : (b + 1) * 128
-                ]
-            out_ref[at, BODY:CODED, :] = footer(
-                to_lanes(counts[part]), to_lanes(code[part])
+    for part in range(2):
+        for t in range(TILES):
+            hot = is_named(part, t, base_ref[0], labels[...]).astype(jnp.bfloat16)
+            at = (part * TILES + t) * TILE
+            out_ref[at : at + TILE, :] = jnp.dot(
+                hot, rows[...], preferred_element_type=jnp.float32
             )
 
 
+def chip_sums_kernel(base_ref, own_labels, labels, own_sums, rows, *out_refs):
+    for part in range(2):
+        for t in range(TILES):
+            hot = is_named(part, t, base_ref[0], labels[...])
+            at = (part * TILES + t) * TILE
+            sums = own_sums[at : at + TILE, :] + jnp.dot(
+                hot.astype(jnp.bfloat16), rows[...], preferred_element_type=jnp.float32
+            )
+            hot = hot + is_named(part, t, base_ref[0], own_labels[...])
+            counts = jnp.sum(hot, 1, keepdims=True)
+            code = code_of(sums)
+            coded = quantize(sums, code)
+            for c in range(EACH):
+                at = slice(c * PART, (c + 1) * PART)
+                for b in range(COLS):
+                    out_refs[part][t * EACH + c, block(b), :] = coded[
+                        at, b * 128 : (b + 1) * 128
+                    ]
+                out_refs[part][t * EACH + c, BODY:CODED, :] = footer(
+                    to_lanes(counts[at]), to_lanes(code[at])
+                )
+
+
 def block(b):
-    return slice(b * HALF, (b + 1) * HALF)
+    return slice(b * PART, (b + 1) * PART)
 
 
 def add_coded(ref, at, blocks, counts):
@@ -107,7 +113,7 @@
 
 
 def nothing():
-    zeros = [jnp.zeros((HALF, 128), jnp.float32) for _ in range(COLS)]
+    zeros = [jnp.zeros((PART, 128), jnp.float32) for _ in range(COLS)]
     return zeros, jnp.zeros((1, 128), jnp.float32)
 
 
@@ -119,7 +125,7 @@
     return [quantize(blocks[b], code) for b in range(COLS)], to_lanes(code)
 
 
-def group_kernel(in_ref, c0, c1, c2, c3, out_ref, centers_ref):
+def group_kernel(in_ref, out_ref):
     together = 8
 
     def step(t, carry):
@@ -134,6 +140,10 @@
     for b in range(COLS):
         out_ref[0, block(b), :] = coded[b]
     out_ref[0, BODY:CODED, :] = footer(counts, codes)
+
+
+def first_group_kernel(in_ref, c0, c1, c2, c3, out_ref, centers_ref):
+    group_kernel(in_ref, out_ref)
     for i, ref in enumerate((c0, c1, c2, c3)):
         n = ref.shape[0]
         centers_ref[i * n : (i + 1) * n, :] = ref[...]
@@ -176,21 +186,20 @@
     out_ref[...] = norms_ref[...] + jnp.min(least, 0, keepdims=True)
 
 
-def new_kernel(turned_ref, coded_ref, norms_ref, least_ref, out_ref):
-    per = TILE // HALF
+def new_kernel(turned_ref, norms_ref, least_ref, *refs):
+    *pieces, out_ref = refs
     turned = turned_ref[...]
     least = least_ref[...]
-    for t in range(CHUNKS // per):
+    for ref, t in [(ref, t) for ref in pieces for t in range(TILES)]:
         high, low, scale, norm = [], [], [], []
-        for c in range(per):
-            at = t * per + c
+        for c in range(t * EACH, (t + 1) * EACH):
             wide = jnp.concatenate(
-                [coded_ref[at, block(b), :].astype(jnp.float32) for b in range(COLS)], 1
+                [ref[c, block(b), :].astype(jnp.float32) for b in range(COLS)], 1
             )
             top = wide.astype(jnp.bfloat16)
             high.append(top)
             low.append((wide - top.astype(jnp.float32)).astype(jnp.bfloat16))
-            foot = coded_ref[at, BODY:CODED, :].astype(jnp.float32)
+            foot = ref[c, BODY:CODED, :].astype(jnp.float32)
             s = scale_of(to_column(foot[1:2, :]))
             scale.append(s)
             norm.append(jnp.sum(wide * wide, 1, keepdims=True) * (s * s))
@@ -224,16 +233,36 @@
     )(*args)
 
 
-def ring(axis, size, k):
-    return [(i, (i + k) % size) for i in range(size)]
-
-
 def swap(value, axis):
     return lax.ppermute(value, axis, [(0, 1), (1, 0)])
 
 
-def around(part, axis):
-    return [part] + [lax.ppermute(part, axis, ring(axis, 4, k)) for k in (1, 2, 3)]
+def around_z(part):
+    return [part] + [
+        lax.ppermute(part, "zh", [(i, (i + k) % 4) for i in range(4)])
+        for k in (1, 2, 3)
+    ]
+
+
+def onward(k, turn):
+    pairs = []
+    for core in range(2):
+        for y in range(4):
+            for x in range(4):
+                if core == turn:
+                    to = (y, (x + k) % 4)
+                else:
+                    to = ((y + k) % 4, x)
+                pairs.append((core * 16 + y * 4 + x, core * 16 + to[0] * 4 + to[1]))
+    return pairs
+
+
+def send(part, k, turn):
+    return lax.ppermute(part, ("core", "y", "x"), onward(k, turn))
+
+
+def around(part, turn):
+    return [part] + [send(part, k, turn) for k in (1, 3, 2)]
 
 
 def after(first, values):
@@ -245,57 +274,70 @@
     core = lax.axis_index("core")
     f32, bf16, i16 = jnp.float32, jnp.bfloat16, jnp.int16
     shape = jax.ShapeDtypeStruct
+    coded = shape((CHUNKS, CODED, 128), i16)
     labels = assignment.reshape(1, n)
     other_labels = swap(labels, "core")
     other_rows = swap(embeddings, "core")
 
     mine = lax.dynamic_slice(centers, (core * HALF, 0), (HALF, D))
-    current = around(jnp.concatenate([mine, swap(mine, "zl")]), "x")
+    current = around(jnp.concatenate([mine, swap(mine, "zl")]), 0)
 
     wide = embeddings.astype(f32)
     norms = jnp.sum(wide * wide, 1).reshape(1, n)
 
     base = (core * HALF).astype(jnp.int32).reshape(1)
-    sums = call(
+    own_sums = call(
         own_sums_kernel,
-        shape((CHUNKS * HALF, D), f32),
+        shape((2 * CHUNKS * PART, D), f32),
         base, labels, embeddings,
         flops=2 * 1024 * n * D, moved=5 << 20, smem=1,
     )
     sums = call(
         chip_sums_kernel,
-        shape((CHUNKS, CODED, 128), i16),
-        base, labels, other_labels, sums, other_rows,
+        (coded,) * 2,
+        base, labels, other_labels, own_sums, other_rows,
         flops=2 * 1024 * n * D, moved=6 << 20, smem=1,
     )
-    sums = lax.all_to_all(sums, SHARD, 0, 0)
-    group, current = call(
+    first_sums, *current = lax.optimization_barrier((sums[0], *current))
+    one = shape((1, CODED, 128), i16)
+    first_group, current = call(
+        first_group_kernel,
+        (one, shape((8 * HALF, D), bf16)),
+        lax.all_to_all(first_sums, SHARD, 0, 0), *current,
+        flops=1 << 21, moved=2 << 20,
+    )
+    second_group = call(
         group_kernel,
-        (shape((1, CODED, 128), i16), shape((8 * HALF, D), bf16)),
-        sums, *current,
-        flops=1 << 22, moved=2 << 20,
-    )
-    current = around(current, "y")
-    groups, current[1], current[3] = lax.optimization_barrier(
-        (around(group, "zh"), current[1], current[3])
-    )
-    refined, coded = call(
-        refine_kernel,
-        (shape((HALF, D), f32), shape((CHUNKS, CODED, 128), i16)),
-        *groups,
-        flops=1 << 20, moved=2 << 20,
-    )
-    new_own = lax.all_to_all(coded, SHARD, 0, 0)
-
-    current = after(coded, current)
-    current = current + tuple(swap(part, "core") for part in current)
+        one,
+        lax.all_to_all(sums[1], SHARD, 0, 0),
+        flops=1 << 21, moved=1 << 20,
+    )
+    groups = [around_z(first_group), around_z(second_group)]
+    groups[0], current = lax.optimization_barrier((groups[0], around(current, 1)))
+    def refine(parts):
+        return call(
+            refine_kernel,
+            (shape((PART, D), f32), coded),
+            *parts,
+            flops=1 << 20, moved=1 << 20,
+        )
+
+    first_refined, code = refine(groups[0])
+    first_new = lax.all_to_all(code, SHARD, 0, 0)
+
+    current = list(after(first_refined, current))
+    current = current + [swap(part, "core") for part in current]
     old_min, turned = call(
         old_kernel,
         (shape((1, n), f32), shape((D, n), bf16)),
         norms, embeddings, *current,
         flops=2 * 2048 * n * D, moved=5 << 20,
     )
-
+    groups[1], turned = lax.optimization_barrier((groups[1], turned))
+    second_refined, code = refine(groups[1])
+    second_new = lax.all_to_all(code, SHARD, 0, 0)
+
+    refined = jnp.concatenate([first_refined, second_refined])
     refined_other = swap(refined, "core")
     first = core == 0
     refined_centers = jnp.concatenate(
@@ -305,16 +347,22 @@
         ]
     )
 
-    (new_own,) = after(turned, (new_own,))
-    new_other = swap(new_own, "core")
-    least = jnp.full((8, n), jnp.inf, f32)
-    for coded, result in ((new_own, 8), (new_other, 1)):
-        least = call(
+    def nearest_new(result, least, *pieces):
+        return call(
             new_kernel,
             shape((result, n), f32),
-            turned, coded, norms, least,
-            flops=2 * 2048 * n * D, moved=3 << 20,
+            turned, norms, least, *pieces,
+            flops=4 * 512 * n * D * len(pieces), moved=len(pieces) << 20,
         )
+
+    least = jnp.full((8, n), jnp.inf, f32)
+    least = nearest_new(8, least, first_new, swap(first_new, "core"))
+    least, second_new, refined_centers = lax.optimization_barrier(
+        (least, second_new, refined_centers)
+    )
+    second_other = swap(second_new, "core")
+    least = nearest_new(8, least, second_new)
+    least = nearest_new(1, least, second_other)
     return old_min.reshape(n), refined_centers, least.reshape(n)
 
 

time: 130 us -> 125 us (0.962)
  waiting for transfers between devices: 56.9 us -> 9.64 us
  blocking collectives: 0 us -> 19.6 us
  starting transfers between devices: 40.5 us -> 59.3 us
  local copies, waits for them, and re-layouts: 7.46 us -> 12.1 us
    ppermute x9 -> x12, waiting for transfers between devices: 31.5 us -> 2.47 us  [the longest x6 1.65 us: around_z(): lax.ppermute(part, 'zh', [(i, (i + k) % 4) for i in range(4)])]
    ppermute x9 -> x10, waiting for transfers between devices: 25.5 us -> 1.92 us  [swap(): return lax.ppermute(value, axis, [(0, 1), (1, 0)])]
    all_to_all x0 -> x1, blocking collectives: none -> 19.6 us  [on_device(): lax.all_to_all(first_sums, SHARD, 0, 0)]
    ppermute x9 -> x12, starting transfers between devices: 19.8 us -> 27.1 us  [the longest x6 18.5 us: around_z(): lax.ppermute(part, 'zh', [(i, (i + k) % 4) for i in range(4)])]
    all_to_all x2 -> x3, starting transfers between devices: 12.6 us -> 18.5 us  [the longest x1 8.01 us: on_device(): second_new = lax.all_to_all(code, SHARD, 0, 0)]
    ppermute x9 -> x10, starting transfers between devices: 8.04 us -> 13.7 us  [swap(): return lax.ppermute(value, axis, [(0, 1), (1, 0)])]
    all_to_all x2 -> x3, waiting for transfers between devices: 0.01 us -> 5.25 us  [the longest x1 5.25 us: on_device(): second_new = lax.all_to_all(code, SHARD, 0, 0)]
    unnamed x22 -> x51, local copies, waits for them, and re-layouts: 7.44 us -> 12.1 us
  transfers between devices with their start and end apart: 20 -> 25, of which waited for: 11 -> 4; matrix products, arithmetic and copies ran while one was open for 1% -> 1% of each run, Pallas kernels for 8% -> 16%
where the time goes in v5:
time: 125 us; the launch traced here: 124 us
  starting transfers between devices  59.3 us (47%)
  Pallas kernels  21.9 us (18%)
  blocking collectives  19.6 us (16%)
  local copies, waits for them, and re-layouts  12.1 us (10%)
  waiting for transfers between devices  9.64 us (8%)
    pallas_call x10, Pallas kernels, call(): pl.pallas_call(kernel, out_shape=out_shape, in_specs=specs, out_specs=tup...  21.9 us
    all_to_all x1, blocking collectives, on_device(): lax.all_to_all(first_sums, SHARD, 0, 0)  19.6 us
    ppermute x6, starting transfers between devices, around_z(): lax.ppermute(part, 'zh', [(i, (i + k) % 4) for i in range(4)])  18.5 us
    ppermute x10, starting transfers between devices, swap(): return lax.ppermute(value, axis, [(0, 1), (1, 0)])  13.7 us
    unnamed x51, local copies, waits for them, and re-layouts  12.1 us
    ppermute x6, starting transfers between devices, send(): return lax.ppermute(part, ('core', 'y', 'x'), onward(k, turn))  8.62 us
    all_to_all x1, starting transfers between devices, on_device(): second_new = lax.all_to_all(code, SHARD, 0, 0)  8.01 us
    all_to_all x1, starting transfers between devices, on_device(): first_new = lax.all_to_all(code, SHARD, 0, 0)  5.75 us
  transfers between devices with their start and end apart: 25, of which 4 were waited for; matrix products, arithmetic and copies ran while one was open for 1% of the time, Pallas kernels for 16%

profile of v5, /device:TPU:1, one launch (start us, length us, event | category | flops | bytes accessed | tf_op | source)
XLA Modules:
  0.0 124.5 jit_solution(5419453237413893511)
XLA Ops:
  0.6 3.3 %collective-permute-start.1 = (bf16[1024,768]{1,0:T(8,128)(2,1)}, bf16[1024,768]{1,0:T(8,128)(2,1)S(1)}, u32[]{:S(2)}, u32[]{:S(2)}) collective-permute-start(bf16[1024,768]{1,0:T(8,128)(2,1)} %rows_ref.1), channel_id=1, source_target_pairs={{0,32},{32,0},{1,33},{33,1},{2,34},{34,2},{3,35},{35,3},{4,36},{36... | collective-permute-start | bytes 4718600 | tf_op jit(solution)/shard_map/ppermute | solution.py:237
  4.2 1.4 %copy-done.1 = bf16[1024,768]{1,0:T(8,128)(2,1)S(1)} copy-done((bf16[1024,768]{1,0:T(8,128)(2,1)S(1)}, bf16[1024,768]{1,0:T(8,128)(2,1)}, u32[]{:S(2)}) %copy-start.1) | copy-done | bytes 1572888
  6.3 1.8 %shard_map.58.own_sums = f32[1024,768]{1,0:T(8,128)S(1)} custom-call(s32[1]{0:T(128)} %bitcast.1.base_ref, s32[1,1024]{1,0:T(1,128)S(1)} %bitcast.10, bf16[1024,768]{1,0:T(8,128)(2,1)S(1)} %copy-done.1), custom_call_target="tpu_custom_call" | custom-call | flops 1610612736 | bytes 5242880 | tf_op jit(solution)/shard_map/pallas_call | solution.py:224
  9.4 1.5 %collective-permute-start.4 = (bf16[64,768]{1,0:T(8,128)(2,1)S(1)}, bf16[64,768]{1,0:T(8,128)(2,1)S(1)}, u32[]{:S(2)}, u32[]{:S(2)}) collective-permute-start(bf16[64,768]{1,0:T(8,128)(2,1)S(1)} %pad_maximum_fusion.1.c0), channel_id=1, source_target_pairs={{0,6},{2,0},{4,2},{6,4},{8,14},{10,8},{12,10},{14,12},{16,22},{18,... | collective-permute-start | bytes 294920 | tf_op jit(solution)/shard_map/ppermute | solution.py:261
  10.9 1.6 %collective-permute-start.5 = (bf16[64,768]{1,0:T(8,128)(2,1)S(1)}, bf16[64,768]{1,0:T(8,128)(2,1)S(1)}, u32[]{:S(2)}, u32[]{:S(2)}) collective-permute-start(bf16[64,768]{1,0:T(8,128)(2,1)S(1)} %pad_maximum_fusion.1.c0), channel_id=1, source_target_pairs={{0,4},{2,6},{4,0},{6,2},{8,12},{10,14},{12,8},{14,10},{16,20},{18,... | collective-permute-start | bytes 294920 | tf_op jit(solution)/shard_map/ppermute | solution.py:261
  12.4 4.0 %shard_map.59 = (s16[32,112,128]{2,1,0:T(8,128)(2,1)S(1)}, s16[32,112,128]{2,1,0:T(8,128)(2,1)}) custom-call(s32[1]{0:T(128)} %bitcast.1.base_ref, s32[1,1024]{1,0:T(1,128)S(1)} %bitcast.11, s32[1,1024]{1,0:T(1,128)S(1)} %collective-permute-done.labels, f32[1024,768]{1,0:T(8,128)S(1)} %shard_map.58.own_sums, bf16[1024,768]{1,0:T(8,128)(2,1)S(1)} %collective-permute-done.1.rows), custom_call_target="tpu_custom_call" | custom-call | flops 1610612736 | bytes 6291456 | tf_op jit(solution)/shard_map/pallas_call | solution.py:224
  16.5 19.6 %all_to_all.20.in_ref = s16[32,112,128]{2,1,0:T(8,128)(2,1)S(1)} all-to-all(s16[32,112,128]{2,1,0:T(8,128)(2,1)S(1)} %get-tuple-element.39), channel_id=1, replica_groups=mesh['zh'=4,'core'=2,'y'=4,'x'=4,'zl'=2] {'y','x','zl'}, dimensions={0} | all-to-all | bytes 1835008 | tf_op jit(solution)/shard_map/all_to_all | solution.py:306
  36.1 4.7 %all-to-all-start.1 = ((s16[32,112,128]{2,1,0:T(8,128)(2,1)}), s16[32,112,128]{2,1,0:T(8,128)(2,1)S(1)}, u32[]{:S(2)}, u32[]{:S(2)}) async-start(s16[32,112,128]{2,1,0:T(8,128)(2,1)} %get-tuple-element.60), calls=%async_computation.1 | async-start | bytes 1835008 | tf_op jit(solution)/shard_map/all_to_all | solution.py:312
  45.1 1.3 %collective-permute-start.9 = (bf16[256,768]{1,0:T(8,128)(2,1)S(1)}, bf16[256,768]{1,0:T(8,128)(2,1)S(1)}, u32[]{:S(2)}, u32[]{:S(2)}) collective-permute-start(bf16[256,768]{1,0:T(8,128)(2,1)S(1)} %get-tuple-element.55.refs_0_), channel_id=1, source_target_pairs={{0,8},{2,10},{4,12},{6,14},{8,16},{10,18},{12,20},{14,22},{16,24},... | collective-permute-start | bytes 1179656 | tf_op jit(solution)/shard_map/ppermute | solution.py:261
  46.4 1.4 %collective-permute-start.10 = (bf16[256,768]{1,0:T(8,128)(2,1)S(1)}, bf16[256,768]{1,0:T(8,128)(2,1)S(1)}, u32[]{:S(2)}, u32[]{:S(2)}) collective-permute-start(bf16[256,768]{1,0:T(8,128)(2,1)S(1)} %get-tuple-element.55.refs_0_), channel_id=1, source_target_pairs={{0,24},{2,26},{4,28},{6,30},{8,0},{10,2},{12,4},{14,6},{16,8},{18,... | collective-permute-start | bytes 1179656 | tf_op jit(solution)/shard_map/ppermute | solution.py:261
  47.8 1.5 %collective-permute-start.11 = (bf16[256,768]{1,0:T(8,128)(2,1)S(1)}, bf16[256,768]{1,0:T(8,128)(2,1)}, u32[]{:S(2)}, u32[]{:S(2)}) collective-permute-start(bf16[256,768]{1,0:T(8,128)(2,1)S(1)} %get-tuple-element.55.refs_0_), channel_id=1, source_target_pairs={{0,16},{2,18},{4,20},{6,22},{8,24},{10,26},{12,28},{14,30},{16,0},... | collective-permute-start | bytes 1179656 | tf_op jit(solution)/shard_map/ppermute | solution.py:261
  49.3 3.0 %collective-permute-start.6 = (s16[1,112,128]{2,1,0:T(8,128)(2,1)S(1)}, s16[1,112,128]{2,1,0:T(8,128)(2,1)S(1)}, u32[]{:S(2)}, u32[]{:S(2)}) collective-permute-start(s16[1,112,128]{2,1,0:T(8,128)(2,1)S(1)} %get-tuple-element.46.own), channel_id=1, source_target_pairs={{0,64},{64,128},{128,192},{192,0},{1,65},{65,129},{129,193},{193,1... | collective-permute-start | bytes 86024 | tf_op jit(solution)/shard_map/ppermute | solution.py:242
  52.3 4.7 %collective-permute-start.7 = (s16[1,112,128]{2,1,0:T(8,128)(2,1)S(1)}, s16[1,112,128]{2,1,0:T(8,128)(2,1)S(1)}, u32[]{:S(2)}, u32[]{:S(2)}) collective-permute-start(s16[1,112,128]{2,1,0:T(8,128)(2,1)S(1)} %get-tuple-element.46.own), channel_id=1, source_target_pairs={{0,128},{64,192},{128,0},{192,64},{1,129},{65,193},{129,1},{193,65... | collective-permute-start | bytes 86024 | tf_op jit(solution)/shard_map/ppermute | solution.py:242
  57.0 2.4 %collective-permute-start.8 = (s16[1,112,128]{2,1,0:T(8,128)(2,1)S(1)}, s16[1,112,128]{2,1,0:T(8,128)(2,1)S(1)}, u32[]{:S(2)}, u32[]{:S(2)}) collective-permute-start(s16[1,112,128]{2,1,0:T(8,128)(2,1)S(1)} %get-tuple-element.46.own), channel_id=1, source_target_pairs={{0,192},{64,0},{128,64},{192,128},{1,193},{65,1},{129,65},{193,129... | collective-permute-start | bytes 86024 | tf_op jit(solution)/shard_map/ppermute | solution.py:242
  59.4 1.6 %collective-permute-done.8.three = s16[1,112,128]{2,1,0:T(8,128)(2,1)S(1)} collective-permute-done((s16[1,112,128]{2,1,0:T(8,128)(2,1)S(1)}, s16[1,112,128]{2,1,0:T(8,128)(2,1)S(1)}, u32[]{:S(2)}, u32[]{:S(2)}) %collective-permute-start.8) | collective-permute-done | bytes 28704 | tf_op jit(solution)/shard_map/ppermute | solution.py:242
  64.6 5.8 %all-to-all-start.2 = ((s16[32,112,128]{2,1,0:T(8,128)(2,1)}), s16[32,112,128]{2,1,0:T(8,128)(2,1)S(1)}, u32[]{:S(2)}, u32[]{:S(2)}) async-start(s16[32,112,128]{2,1,0:T(8,128)(2,1)} %copy-done.3), calls=%async_computation.2 | async-start | bytes 1835008 | tf_op jit(solution)/shard_map/all_to_all | solution.py:326
  70.4 5.0 %collective-permute-start.12 = (bf16[256,768]{1,0:T(8,128)(2,1)}, bf16[256,768]{1,0:T(8,128)(2,1)S(1)}, u32[]{:S(2)}, u32[]{:S(2)}) collective-permute-start(bf16[256,768]{1,0:T(8,128)(2,1)} %copy-done.14), channel_id=1, source_target_pairs={{0,32},{32,0},{1,33},{33,1},{2,34},{34,2},{3,35},{35,3},{4,36},{36... | collective-permute-start | bytes 1179656 | tf_op jit(solution)/shard_map/ppermute | solution.py:237
  77.1 2.2 %collective-permute-start.16 = (s16[1,112,128]{2,1,0:T(8,128)(2,1)S(1)}, s16[1,112,128]{2,1,0:T(8,128)(2,1)S(1)}, u32[]{:S(2)}, u32[]{:S(2)}) collective-permute-start(s16[1,112,128]{2,1,0:T(8,128)(2,1)S(1)} %shard_map.63.own), channel_id=1, source_target_pairs={{0,64},{64,128},{128,192},{192,0},{1,65},{65,129},{129,193},{193,1... | collective-permute-start | bytes 86024 | tf_op jit(solution)/shard_map/ppermute | solution.py:242
  79.3 3.6 %collective-permute-start.17 = (s16[1,112,128]{2,1,0:T(8,128)(2,1)S(1)}, s16[1,112,128]{2,1,0:T(8,128)(2,1)S(1)}, u32[]{:S(2)}, u32[]{:S(2)}) collective-permute-start(s16[1,112,128]{2,1,0:T(8,128)(2,1)S(1)} %shard_map.63.own), channel_id=1, source_target_pairs={{0,128},{64,192},{128,0},{192,64},{1,129},{65,193},{129,1},{193,65... | collective-permute-start | bytes 86024 | tf_op jit(solution)/shard_map/ppermute | solution.py:242
  82.9 2.6 %collective-permute-start.18 = (s16[1,112,128]{2,1,0:T(8,128)(2,1)S(1)}, s16[1,112,128]{2,1,0:T(8,128)(2,1)S(1)}, u32[]{:S(2)}, u32[]{:S(2)}) collective-permute-start(s16[1,112,128]{2,1,0:T(8,128)(2,1)S(1)} %shard_map.63.own), channel_id=1, source_target_pairs={{0,192},{64,0},{128,64},{192,128},{1,193},{65,1},{129,65},{193,129... | collective-permute-start | bytes 86024 | tf_op jit(solution)/shard_map/ppermute | solution.py:242
  85.5 5.2 %shard_map.62 = (f32[1,1024]{1,0:T(1,128)}, bf16[768,1024]{1,0:T(8,128)(2,1)S(1)}) custom-call(f32[1,1024]{1,0:T(1,128)S(1)} %bitcast.5, bf16[1024,768]{1,0:T(8,128)(2,1)S(1)} %copy-done.2, bf16[256,768]{1,0:T(8,128)(2,1)S(1)} %copy-done.15, bf16[256,768]{1,0:T(8,128)(2,1)S(1)} %copy-done.17, bf16[256,768]{1,0:T(8,128)(2,1)S(1)} %copy-done.19, ...), custom_call_target="tpu_custom_call" | custom-call | flops 3221225472 | bytes 5242880 | tf_op jit(solution)/shard_map/pallas_call | solution.py:224
  91.9 1.4 %shard_map.65 = (f32[16,768]{1,0:T(8,128)S(1)}, s16[32,112,128]{2,1,0:T(8,128)(2,1)}) custom-call(s16[1,112,128]{2,1,0:T(8,128)(2,1)S(1)} %shard_map.63.own, s16[1,112,128]{2,1,0:T(8,128)(2,1)S(1)} %collective-permute-done.16.one, s16[1,112,128]{2,1,0:T(8,128)(2,1)S(1)} %collective-permute-done.17.two, s16[1,112,128]{2,1,0:T(8,128)(2,1)S(1)} %collective-permute-done.18.three), custom_call_target="tpu_custom_call" | custom-call | flops 1048576 | bytes 1048576 | tf_op jit(solution)/shard_map/pallas_call | solution.py:224
  93.3 8.0 %all-to-all-start.3 = ((s16[32,112,128]{2,1,0:T(8,128)(2,1)}), s16[32,112,128]{2,1,0:T(8,128)(2,1)S(1)}, u32[]{:S(2)}, u32[]{:S(2)}) async-start(s16[32,112,128]{2,1,0:T(8,128)(2,1)} %get-tuple-element.68), calls=%async_computation.3 | async-start | bytes 1835008 | tf_op jit(solution)/shard_map/all_to_all | solution.py:338
  101.3 1.6 %collective-permute-start.19 = (s16[32,112,128]{2,1,0:T(8,128)(2,1)S(1)}, s16[32,112,128]{2,1,0:T(8,128)(2,1)S(1)}, u32[]{:S(2)}, u32[]{:S(2)}) collective-permute-start(s16[32,112,128]{2,1,0:T(8,128)(2,1)S(1)} %all-to-all-done.2.refs_0_), channel_id=1, source_target_pairs={{0,32},{32,0},{1,33},{33,1},{2,34},{34,2},{3,35},{35,3},{4,36},{36... | collective-permute-start | bytes 2752520 | tf_op jit(solution)/shard_map/ppermute | solution.py:237
  103.2 1.9 %collective-permute-done.20 = f32[32,768]{1,0:T(8,128)S(1)} collective-permute-done((f32[32,768]{1,0:T(8,128)S(1)}, f32[32,768]{1,0:T(8,128)S(1)}, u32[]{:S(2)}, u32[]{:S(2)}) %collective-permute-start.20) | collective-permute-done | bytes 98336 | tf_op jit(solution)/shard_map/ppermute | solution.py:237
  105.9 1.4 %copy-done.23 = bf16[768,1024]{1,0:T(8,128)(2,1)S(1)} copy-done((bf16[768,1024]{1,0:T(8,128)(2,1)S(1)}, bf16[768,1024]{1,0:T(8,128)(2,1)}, u32[]{:S(2)}) %copy-start.23) | copy-done | bytes 1572888
  107.3 3.6 %shard_map.64.least_ref = f32[8,1024]{1,0:T(8,128)S(1)} custom-call(bf16[768,1024]{1,0:T(8,128)(2,1)S(1)} %copy-done.23, f32[1,1024]{1,0:T(1,128)S(1)} %bitcast.6, f32[8,1024]{1,0:T(8,128)S(1)} %broadcast_in_dim.3.least_ref, s16[32,112,128]{2,1,0:T(8,128)(2,1)S(1)} %all-to-all-done.2.refs_0_, s16[32,112,128]{2,1,0:T(8,128)(2,1)S(1)} %collective-permute-done.19.refs_1_), custom_call_target="tpu_custom_call" | custom-call | flops 3221225472 | bytes 2097152 | tf_op jit(solution)/shard_map/pallas_call | solution.py:224
  110.8 5.2 %all-to-all-done.3.refs_0_ = s16[32,112,128]{2,1,0:T(8,128)(2,1)S(1)} async-done(((s16[32,112,128]{2,1,0:T(8,128)(2,1)}), s16[32,112,128]{2,1,0:T(8,128)(2,1)S(1)}, u32[]{:S(2)}, u32[]{:S(2)}) %all-to-all-start.3) | async-done | bytes 917536 | tf_op jit(solution)/shard_map/all_to_all | solution.py:338
  116.1 2.6 %collective-permute-start.21 = (s16[32,112,128]{2,1,0:T(8,128)(2,1)S(1)}, s16[32,112,128]{2,1,0:T(8,128)(2,1)S(1)}, u32[]{:S(2)}, u32[]{:S(2)}) collective-permute-start(s16[32,112,128]{2,1,0:T(8,128)(2,1)S(1)} %all-to-all-done.3.refs_0_), channel_id=1, source_target_pairs={{0,32},{32,0},{1,33},{33,1},{2,34},{34,2},{3,35},{35,3},{4,36},{36... | collective-permute-start | bytes 2752520 | tf_op jit(solution)/shard_map/ppermute | solution.py:237
  118.7 1.4 %copy-done.24 = bf16[768,1024]{1,0:T(8,128)(2,1)S(1)} copy-done((bf16[768,1024]{1,0:T(8,128)(2,1)S(1)}, bf16[768,1024]{1,0:T(8,128)(2,1)}, u32[]{:S(2)}) %copy-start.24) | copy-done | bytes 1572888
  120.1 1.9 %shard_map.66.least_ref = f32[8,1024]{1,0:T(8,128)S(1)} custom-call(bf16[768,1024]{1,0:T(8,128)(2,1)S(1)} %copy-done.24, f32[1,1024]{1,0:T(1,128)S(1)} %bitcast.7, f32[8,1024]{1,0:T(8,128)S(1)} %shard_map.64.least_ref, s16[32,112,128]{2,1,0:T(8,128)(2,1)S(1)} %all-to-all-done.3.refs_0_), custom_call_target="tpu_custom_call" | custom-call | flops 1610612736 | bytes 1048576 | tf_op jit(solution)/shard_map/pallas_call | solution.py:224
  122.0 2.5 %shard_map.67 = f32[1,1024]{1,0:T(1,128)} custom-call(bf16[768,1024]{1,0:T(8,128)(2,1)S(1)} %copy-done.24, f32[1,1024]{1,0:T(1,128)S(1)} %bitcast.8, f32[8,1024]{1,0:T(8,128)S(1)} %shard_map.66.least_ref, s16[32,112,128]{2,1,0:T(8,128)(2,1)S(1)} %collective-permute-done.21.refs_0_), custom_call_target="tpu_custom_call" | custom-call | flops 1610612736 | bytes 1048576 | tf_op jit(solution)/shard_map/pallas_call | solution.py:224
  (87 shorter events, 13.8 us)
Async XLA Ops:
  0.6 11.8 %collective-permute-start.1 = (bf16[1024,768]{1,0:T(8,128)(2,1)}, bf16[1024,768]{1,0:T(8,128)(2,1)S(1)}, u32[]{:S(2)}, u32[]{:S(2)}) collective-permute-start(bf16[1024,768]{1,0:T(8,128)(2,1)} %rows_ref.1), channel_id=1, source_target_pairs={{0,32},{32,0},{1,33},{33,1},{2,34},{34,2},{3,35},{35,3},{4,36},{36... | collective-permute-start | bytes 4718600 | tf_op jit(solution)/shard_map/ppermute | solution.py:237
  4.0 8.5 %collective-permute-start = (s32[1,1024]{1,0:T(1,128)}, s32[1,1024]{1,0:T(1,128)S(1)}, u32[]{:S(2)}, u32[]{:S(2)}) collective-permute-start(s32[1,1024]{1,0:T(1,128)} %bitcast.9), channel_id=1, source_target_pairs={{0,32},{32,0},{1,33},{33,1},{2,34},{34,2},{3,35},{35,3},{4,36},{36... | collective-permute-start | bytes 12296 | tf_op jit(solution)/shard_map/ppermute | solution.py:237
  4.1 4.0 %collective-permute-start.2 = (bf16[32,768]{1,0:T(8,128)(2,1)S(1)}, bf16[32,768]{1,0:T(8,128)(2,1)S(1)}, u32[]{:S(2)}, u32[]{:S(2)}) collective-permute-start(bf16[32,768]{1,0:T(8,128)(2,1)S(1)} %constant_dynamic-slice_fusion), channel_id=1, source_target_pairs={{0,1},{1,0},{2,3},{3,2},{4,5},{5,4},{6,7},{7,6},{8,9},{9,8},{10,11... | collective-permute-start | bytes 147464 | tf_op jit(solution)/shard_map/ppermute | solution.py:237
  8.1 8.4 %collective-permute-start.3 = (bf16[64,768]{1,0:T(8,128)(2,1)S(1)}, bf16[64,768]{1,0:T(8,128)(2,1)S(1)}, u32[]{:S(2)}, u32[]{:S(2)}) collective-permute-start(bf16[64,768]{1,0:T(8,128)(2,1)S(1)} %pad_maximum_fusion.1.c0), channel_id=1, source_target_pairs={{0,2},{2,4},{4,6},{6,0},{8,10},{10,12},{12,14},{14,8},{16,18},{18,... | collective-permute-start | bytes 294920 | tf_op jit(solution)/shard_map/ppermute | solution.py:261
  9.4 7.1 %collective-permute-start.4 = (bf16[64,768]{1,0:T(8,128)(2,1)S(1)}, bf16[64,768]{1,0:T(8,128)(2,1)S(1)}, u32[]{:S(2)}, u32[]{:S(2)}) collective-permute-start(bf16[64,768]{1,0:T(8,128)(2,1)S(1)} %pad_maximum_fusion.1.c0), channel_id=1, source_target_pairs={{0,6},{2,0},{4,2},{6,4},{8,14},{10,8},{12,10},{14,12},{16,22},{18,... | collective-permute-start | bytes 294920 | tf_op jit(solution)/shard_map/ppermute | solution.py:261
  10.9 5.6 %collective-permute-start.5 = (bf16[64,768]{1,0:T(8,128)(2,1)S(1)}, bf16[64,768]{1,0:T(8,128)(2,1)S(1)}, u32[]{:S(2)}, u32[]{:S(2)}) collective-permute-start(bf16[64,768]{1,0:T(8,128)(2,1)S(1)} %pad_maximum_fusion.1.c0), channel_id=1, source_target_pairs={{0,4},{2,6},{4,0},{6,2},{8,12},{10,14},{12,8},{14,10},{16,20},{18,... | collective-permute-start | bytes 294920 | tf_op jit(solution)/shard_map/ppermute | solution.py:261
  16.5 19.6 %copy-start.6 = (bf16[64,768]{1,0:T(8,128)(2,1)}, bf16[64,768]{1,0:T(8,128)(2,1)S(1)}, u32[]{:S(2)}) copy-start(bf16[64,768]{1,0:T(8,128)(2,1)S(1)} %collective-permute-done.3.c1) | copy-start | bytes 294916
  16.5 19.6 %copy-start.8 = (bf16[64,768]{1,0:T(8,128)(2,1)}, bf16[64,768]{1,0:T(8,128)(2,1)S(1)}, u32[]{:S(2)}) copy-start(bf16[64,768]{1,0:T(8,128)(2,1)S(1)} %collective-permute-done.4.c2) | copy-start | bytes 294916
  16.5 19.6 %copy-start.10 = (bf16[64,768]{1,0:T(8,128)(2,1)}, bf16[64,768]{1,0:T(8,128)(2,1)S(1)}, u32[]{:S(2)}) copy-start(bf16[64,768]{1,0:T(8,128)(2,1)S(1)} %collective-permute-done.5.c3) | copy-start | bytes 294916
  36.1 28.5 %all-to-all-start.1 = ((s16[32,112,128]{2,1,0:T(8,128)(2,1)}), s16[32,112,128]{2,1,0:T(8,128)(2,1)S(1)}, u32[]{:S(2)}, u32[]{:S(2)}) async-start(s16[32,112,128]{2,1,0:T(8,128)(2,1)} %get-tuple-element.60), calls=%async_computation.1 | async-start | bytes 1835008 | tf_op jit(solution)/shard_map/all_to_all | solution.py:312
  44.4 31.6 %copy-start.2 = (bf16[1024,768]{1,0:T(8,128)(2,1)S(1)}, bf16[1024,768]{1,0:T(8,128)(2,1)}, u32[]{:S(2)}) copy-start(bf16[1024,768]{1,0:T(8,128)(2,1)} %rows_ref.1) | copy-start | bytes 4718596
  45.0 16.0 %copy-start.14 = (bf16[256,768]{1,0:T(8,128)(2,1)}, bf16[256,768]{1,0:T(8,128)(2,1)S(1)}, u32[]{:S(2)}) copy-start(bf16[256,768]{1,0:T(8,128)(2,1)S(1)} %get-tuple-element.55.refs_0_) | copy-start | bytes 1179652
  45.1 16.0 %collective-permute-start.9 = (bf16[256,768]{1,0:T(8,128)(2,1)S(1)}, bf16[256,768]{1,0:T(8,128)(2,1)S(1)}, u32[]{:S(2)}, u32[]{:S(2)}) collective-permute-start(bf16[256,768]{1,0:T(8,128)(2,1)S(1)} %get-tuple-element.55.refs_0_), channel_id=1, source_target_pairs={{0,8},{2,10},{4,12},{6,14},{8,16},{10,18},{12,20},{14,22},{16,24},... | collective-permute-start | bytes 1179656 | tf_op jit(solution)/shard_map/ppermute | solution.py:261
  46.4 14.7 %collective-permute-start.10 = (bf16[256,768]{1,0:T(8,128)(2,1)S(1)}, bf16[256,768]{1,0:T(8,128)(2,1)S(1)}, u32[]{:S(2)}, u32[]{:S(2)}) collective-permute-start(bf16[256,768]{1,0:T(8,128)(2,1)S(1)} %get-tuple-element.55.refs_0_), channel_id=1, source_target_pairs={{0,24},{2,26},{4,28},{6,30},{8,0},{10,2},{12,4},{14,6},{16,8},{18,... | collective-permute-start | bytes 1179656 | tf_op jit(solution)/shard_map/ppermute | solution.py:261
  47.8 15.5 %collective-permute-start.11 = (bf16[256,768]{1,0:T(8,128)(2,1)S(1)}, bf16[256,768]{1,0:T(8,128)(2,1)}, u32[]{:S(2)}, u32[]{:S(2)}) collective-permute-start(bf16[256,768]{1,0:T(8,128)(2,1)S(1)} %get-tuple-element.55.refs_0_), channel_id=1, source_target_pairs={{0,16},{2,18},{4,20},{6,22},{8,24},{10,26},{12,28},{14,30},{16,0},... | collective-permute-start | bytes 1179656 | tf_op jit(solution)/shard_map/ppermute | solution.py:261
  49.3 7.7 %collective-permute-start.6 = (s16[1,112,128]{2,1,0:T(8,128)(2,1)S(1)}, s16[1,112,128]{2,1,0:T(8,128)(2,1)S(1)}, u32[]{:S(2)}, u32[]{:S(2)}) collective-permute-start(s16[1,112,128]{2,1,0:T(8,128)(2,1)S(1)} %get-tuple-element.46.own), channel_id=1, source_target_pairs={{0,64},{64,128},{128,192},{192,0},{1,65},{65,129},{129,193},{193,1... | collective-permute-start | bytes 86024 | tf_op jit(solution)/shard_map/ppermute | solution.py:242
  52.3 7.0 %collective-permute-start.7 = (s16[1,112,128]{2,1,0:T(8,128)(2,1)S(1)}, s16[1,112,128]{2,1,0:T(8,128)(2,1)S(1)}, u32[]{:S(2)}, u32[]{:S(2)}) collective-permute-start(s16[1,112,128]{2,1,0:T(8,128)(2,1)S(1)} %get-tuple-element.46.own), channel_id=1, source_target_pairs={{0,128},{64,192},{128,0},{192,64},{1,129},{65,193},{129,1},{193,65... | collective-permute-start | bytes 86024 | tf_op jit(solution)/shard_map/ppermute | solution.py:242
  57.0 4.0 %collective-permute-start.8 = (s16[1,112,128]{2,1,0:T(8,128)(2,1)S(1)}, s16[1,112,128]{2,1,0:T(8,128)(2,1)S(1)}, u32[]{:S(2)}, u32[]{:S(2)}) collective-permute-start(s16[1,112,128]{2,1,0:T(8,128)(2,1)S(1)} %get-tuple-element.46.own), channel_id=1, source_target_pairs={{0,192},{64,0},{128,64},{192,128},{1,193},{65,1},{129,65},{193,129... | collective-permute-start | bytes 86024 | tf_op jit(solution)/shard_map/ppermute | solution.py:242
  64.6 28.6 %all-to-all-start.2 = ((s16[32,112,128]{2,1,0:T(8,128)(2,1)}), s16[32,112,128]{2,1,0:T(8,128)(2,1)S(1)}, u32[]{:S(2)}, u32[]{:S(2)}) async-start(s16[32,112,128]{2,1,0:T(8,128)(2,1)} %copy-done.3), calls=%async_computation.2 | async-start | bytes 1835008 | tf_op jit(solution)/shard_map/all_to_all | solution.py:326
  70.4 15.1 %copy-start.15 = (bf16[256,768]{1,0:T(8,128)(2,1)S(1)}, bf16[256,768]{1,0:T(8,128)(2,1)}, u32[]{:S(2)}) copy-start(bf16[256,768]{1,0:T(8,128)(2,1)} %copy-done.14) | copy-start | bytes 1179652
  70.4 15.1 %copy-start.17 = (bf16[256,768]{1,0:T(8,128)(2,1)S(1)}, bf16[256,768]{1,0:T(8,128)(2,1)}, u32[]{:S(2)}) copy-start(bf16[256,768]{1,0:T(8,128)(2,1)} %copy-done.16) | copy-start | bytes 1179652
  70.4 8.9 %collective-permute-start.12 = (bf16[256,768]{1,0:T(8,128)(2,1)}, bf16[256,768]{1,0:T(8,128)(2,1)S(1)}, u32[]{:S(2)}, u32[]{:S(2)}) collective-permute-start(bf16[256,768]{1,0:T(8,128)(2,1)} %copy-done.14), channel_id=1, source_target_pairs={{0,32},{32,0},{1,33},{33,1},{2,34},{34,2},{3,35},{35,3},{4,36},{36... | collective-permute-start | bytes 1179656 | tf_op jit(solution)/shard_map/ppermute | solution.py:237
  75.5 7.4 %collective-permute-start.13 = (bf16[256,768]{1,0:T(8,128)(2,1)}, bf16[256,768]{1,0:T(8,128)(2,1)S(1)}, u32[]{:S(2)}, u32[]{:S(2)}) collective-permute-start(bf16[256,768]{1,0:T(8,128)(2,1)} %copy-done.16), channel_id=1, source_target_pairs={{0,32},{32,0},{1,33},{33,1},{2,34},{34,2},{3,35},{35,3},{4,36},{36... | collective-permute-start | bytes 1179656 | tf_op jit(solution)/shard_map/ppermute | solution.py:237
  75.6 10.0 %collective-permute-start.14 = (bf16[256,768]{1,0:T(8,128)(2,1)}, bf16[256,768]{1,0:T(8,128)(2,1)S(1)}, u32[]{:S(2)}, u32[]{:S(2)}) collective-permute-start(bf16[256,768]{1,0:T(8,128)(2,1)} %copy-done.18), channel_id=1, source_target_pairs={{0,32},{32,0},{1,33},{33,1},{2,34},{34,2},{3,35},{35,3},{4,36},{36... | collective-permute-start | bytes 1179656 | tf_op jit(solution)/shard_map/ppermute | solution.py:237
  76.0 9.5 %collective-permute-start.15 = (bf16[256,768]{1,0:T(8,128)(2,1)}, bf16[256,768]{1,0:T(8,128)(2,1)S(1)}, u32[]{:S(2)}, u32[]{:S(2)}) collective-permute-start(bf16[256,768]{1,0:T(8,128)(2,1)} %collective-permute-done.11.refs_3_), channel_id=1, source_target_pairs={{0,32},{32,0},{1,33},{33,1},{2,34},{34,2},{3,35},{35,3},{4,36},{36... | collective-permute-start | bytes 1179656 | tf_op jit(solution)/shard_map/ppermute | solution.py:237
  77.1 14.8 %collective-permute-start.16 = (s16[1,112,128]{2,1,0:T(8,128)(2,1)S(1)}, s16[1,112,128]{2,1,0:T(8,128)(2,1)S(1)}, u32[]{:S(2)}, u32[]{:S(2)}) collective-permute-start(s16[1,112,128]{2,1,0:T(8,128)(2,1)S(1)} %shard_map.63.own), channel_id=1, source_target_pairs={{0,64},{64,128},{128,192},{192,0},{1,65},{65,129},{129,193},{193,1... | collective-permute-start | bytes 86024 | tf_op jit(solution)/shard_map/ppermute | solution.py:242
  79.3 12.6 %collective-permute-start.17 = (s16[1,112,128]{2,1,0:T(8,128)(2,1)S(1)}, s16[1,112,128]{2,1,0:T(8,128)(2,1)S(1)}, u32[]{:S(2)}, u32[]{:S(2)}) collective-permute-start(s16[1,112,128]{2,1,0:T(8,128)(2,1)S(1)} %shard_map.63.own), channel_id=1, source_target_pairs={{0,128},{64,192},{128,0},{192,64},{1,129},{65,193},{129,1},{193,65... | collective-permute-start | bytes 86024 | tf_op jit(solution)/shard_map/ppermute | solution.py:242
  82.9 9.0 %collective-permute-start.18 = (s16[1,112,128]{2,1,0:T(8,128)(2,1)S(1)}, s16[1,112,128]{2,1,0:T(8,128)(2,1)S(1)}, u32[]{:S(2)}, u32[]{:S(2)}) collective-permute-start(s16[1,112,128]{2,1,0:T(8,128)(2,1)S(1)} %shard_map.63.own), channel_id=1, source_target_pairs={{0,192},{64,0},{128,64},{192,128},{1,193},{65,1},{129,65},{193,129... | collective-permute-start | bytes 86024 | tf_op jit(solution)/shard_map/ppermute | solution.py:242
  93.3 22.8 %all-to-all-start.3 = ((s16[32,112,128]{2,1,0:T(8,128)(2,1)}), s16[32,112,128]{2,1,0:T(8,128)(2,1)S(1)}, u32[]{:S(2)}, u32[]{:S(2)}) async-start(s16[32,112,128]{2,1,0:T(8,128)(2,1)} %get-tuple-element.68), calls=%async_computation.3 | async-start | bytes 1835008 | tf_op jit(solution)/shard_map/all_to_all | solution.py:338
  101.3 4.6 %collective-permute-start.19 = (s16[32,112,128]{2,1,0:T(8,128)(2,1)S(1)}, s16[32,112,128]{2,1,0:T(8,128)(2,1)S(1)}, u32[]{:S(2)}, u32[]{:S(2)}) collective-permute-start(s16[32,112,128]{2,1,0:T(8,128)(2,1)S(1)} %all-to-all-done.2.refs_0_), channel_id=1, source_target_pairs={{0,32},{32,0},{1,33},{33,1},{2,34},{34,2},{3,35},{35,3},{4,36},{36... | collective-permute-start | bytes 2752520 | tf_op jit(solution)/shard_map/ppermute | solution.py:237
  102.9 2.2 %collective-permute-start.20 = (f32[32,768]{1,0:T(8,128)S(1)}, f32[32,768]{1,0:T(8,128)S(1)}, u32[]{:S(2)}, u32[]{:S(2)}) collective-permute-start(f32[32,768]{1,0:T(8,128)S(1)} %constant_dynamic-update-slice_fusion), channel_id=1, source_target_pairs={{0,32},{32,0},{1,33},{33,1},{2,34},{34,2},{3,35},{35,3},{4,36},{36... | collective-permute-start | bytes 294920 | tf_op jit(solution)/shard_map/ppermute | solution.py:237
  116.1 5.9 %collective-permute-start.21 = (s16[32,112,128]{2,1,0:T(8,128)(2,1)S(1)}, s16[32,112,128]{2,1,0:T(8,128)(2,1)S(1)}, u32[]{:S(2)}, u32[]{:S(2)}) collective-permute-start(s16[32,112,128]{2,1,0:T(8,128)(2,1)S(1)} %all-to-all-done.3.refs_0_), channel_id=1, source_target_pairs={{0,32},{32,0},{1,33},{33,1},{2,34},{34,2},{3,35},{35,3},{4,36},{36... | collective-permute-start | bytes 2752520 | tf_op jit(solution)/shard_map/ppermute | solution.py:237
  (18 other events, 73.5 us)
